TPU v7x, 128 devices: a whole 4x4x4 slice. The times are simulated.
128 devices in a mesh: inner: 32 (over y, z, core), rep: 4 (over x).
Axes of the slice: x: 4, y: 4, z: 4, core: 2. Of those that a mesh axis runs over, the one named last changes fastest.
Arguments:
- layer_input: bfloat16 [131072, 1024], P(('inner', 'rep')), may hold values from -6 to 6
- pre_act: bfloat16 [131072, 4096], P(('inner', 'rep')), may hold values from -5 to 5
- cotangent: bfloat16 [131072, 1024], P(('inner', 'rep')), may hold values from -1.25 to 1.25
- down_weight: bfloat16 [4096, 1024], replicated, may hold values from -0.09375 to 0.09375
- lengths: int32 [1024], P(('inner', 'rep')), may hold values from 32 to 128, as said below
Outputs:
- up_grad: float32 [1024, 4096], P('inner')
- down_grad: float32 [4096, 1024], P('inner')
Inputs may be any that keep to these rules, and one draw needn't show every extreme that they name: `lengths`: some sequence is full and some has exactly 32 valid tokens in every draw; rows past a sequence's length are padding.
All inputs are finite; a program needn't handle non-finite values.
Results may differ from a plain program's by a relative error of at most 0.0013.
Values sent between devices are 32-bit elements; how exact they have to be, the bound alone decides.
No kernel may reach another device: no remote copies, remote signals or barrier semaphores. Data moves between devices by JAX's collectives and lax.ppermute only.
A program may use at most 192 MiB of HBM per device.

v0:
```python
import jax
import jax.numpy as jnp
from jax import lax
from jax.sharding import PartitionSpec as P

SEQ = 128


SQRT_HALF = 0.7071067811865476
INV_ROOT_TWO_PI = 0.3989422804014327
EPSILON = 1e-06


def from_partner(block, axis, bit):
    count = lax.axis_size(axis)
    route = []
    for low in range(count):
        high = low | 1 << bit
        if high != low and high < count:
            route += [(low, high), (high, low)]
    return lax.ppermute(block, axis, route)


def on_device(layer_input, pre_act, cotangent, down_weight, lengths):
    row_count = layer_input.shape[0]
    seq_count = lengths.shape[0]
    replicas = lax.axis_size("rep")
    levels = replicas.bit_length() - 1
    replica = lax.axis_index("rep")
    position = lax.iota(jnp.int32, row_count)
    owner = position // SEQ
    belongs = owner[:, None] == lax.iota(jnp.int32, seq_count)[None, :]
    allowed = jnp.sum(jnp.where(belongs, lengths[None, :], 0), axis=1)
    is_valid = position % SEQ < allowed
    masked = jnp.where(is_valid[:, None], cotangent, jnp.zeros_like(cotangent))
    pre_wide = pre_act.astype(jnp.float32)
    cdf_value = 0.5 * (1.0 + jax.scipy.special.erf(pre_wide * SQRT_HALF))
    hidden = (pre_wide * cdf_value).astype(jnp.bfloat16)
    columns = hidden
    down_piece = lax.psum_scatter(
        lax.dot_general(
            columns, masked, (((0,), (0,)), ((), ())), preferred_element_type=jnp.float32
        ),
        "inner",
        scatter_dimension=0,
        tiled=True,
    )
    hidden_grad = lax.dot_general(
        masked, down_weight, (((1,), (1,)), ((), ())), preferred_element_type=jnp.float32
    )
    derivative = cdf_value + pre_wide * jnp.exp(-0.5 * pre_wide * pre_wide) * INV_ROOT_TWO_PI
    pre_grad = (hidden_grad * derivative).astype(jnp.bfloat16)
    columns = layer_input
    up_piece = lax.psum_scatter(
        lax.dot_general(
            columns, pre_grad, (((0,), (0,)), ((), ())), preferred_element_type=jnp.float32
        ),
        "inner",
        scatter_dimension=0,
        tiled=True,
    )
    for level in range(levels):
        level_bit = levels - 1 - level
        upper = replica // (1 << level_bit) % 2
        is_lower = upper == 0
        up_half = up_piece.shape[0] // 2
        down_half = down_piece.shape[0] // 2
        up_retained = lax.dynamic_slice_in_dim(up_piece, upper * up_half, up_half, 0)
        up_outgoing = lax.dynamic_slice_in_dim(up_piece, (1 - upper) * up_half, up_half, 0)
        down_retained = lax.dynamic_slice_in_dim(down_piece, upper * down_half, down_half, 0)
        down_outgoing = lax.dynamic_slice_in_dim(down_piece, (1 - upper) * down_half, down_half, 0)
        up_partner, down_partner = from_partner((up_outgoing, down_outgoing), "rep", level_bit)

        def partial_terms(retained, partner):
            cross = jnp.sum(retained * partner)
            own_square = jnp.sum(retained * retained)
            partner_square = jnp.sum(partner * partner)
            first_square = jnp.where(is_lower, own_square, partner_square)
            second_square = jnp.where(is_lower, partner_square, own_square)
            return [cross, first_square, second_square]

        partials = jnp.stack(
            partial_terms(up_retained, up_partner) + partial_terms(down_retained, down_partner)
        )
        groups = replicas >> level + 1
        my_group = replica % groups
        selector = (lax.iota(jnp.int32, groups) == my_group).astype(jnp.float32)
        slotted = selector[:, None] * partials[None, :]
        gathered_totals = lax.psum(slotted, ("inner", "rep"))
        totals = jnp.sum(selector[:, None] * gathered_totals, axis=0)

        def combined(retained, partner, offset):
            cross = totals[offset]
            first_coef = 1.0 - cross / (2.0 * (totals[offset + 1] + EPSILON))
            second_coef = 1.0 - cross / (2.0 * (totals[offset + 2] + EPSILON))
            own_coef = jnp.where(is_lower, first_coef, second_coef)
            partner_coef = jnp.where(is_lower, second_coef, first_coef)
            return own_coef * retained + partner_coef * partner

        up_piece = combined(up_retained, up_partner, 0)
        down_piece = combined(down_retained, down_partner, 3)
    up_grad, down_grad = (
        lax.all_gather(up_piece, "rep", axis=0, tiled=True),
        lax.all_gather(down_piece, "rep", axis=0, tiled=True),
    )
    return (up_grad, down_grad)


def solution(mesh):
    in_specs = (
        P(("inner", "rep"), None),
        P(("inner", "rep"), None),
        P(("inner", "rep"), None),
        P(),
        P(("inner", "rep")),
    )
    out_specs = (P("inner", None), P("inner", None))
    return jax.shard_map(
        on_device, mesh=mesh, in_specs=in_specs, out_specs=out_specs, check_vma=False
    )
```

profile of v0, /device:TPU:0, one launch (start us, length us, event | category | flops | bytes accessed | tf_op | source)
XLA Modules:
  0.0 493.5 jit_solution(1297209448297946646)
XLA Ops:
  7.2 0.9 select_reduce_fusion
  8.8 27.1 %fusion.10 = f32[1024,4096]{0,1:T(8,128)} fusion(bf16[1024,1024]{1,0:T(8,128)(2,1)S(1)} %copy-done, bf16[1024,4096]{1,0:T(8,128)(2,1)} %param.6, bf16[4096,1024]{1,0:T(8,128)(2,1)} %param.8, bf16[1024,1024]{1,0:T(8,128)(2,1)} %param.7, pred[1024]{0:T(1024)(128)(4,1)S(1)} %fusion.15), kind=kOutput, calls=%fused_computation.15 | convolution fusion | flops 17227055104 | bytes 37749760 | tf_op jit(solution)/shard_map/dot_general | solution.py:55
  35.9 17.5 %copy.26 = f32[1024,4096]{1,0:T(8,128)} copy(f32[1024,4096]{0,1:T(8,128)} %fusion.10) | data formatting | bytes 33554432
  53.7 16.3 %fusion.11 = f32[4096,1024]{1,0:T(8,128)} fusion(bf16[1024,4096]{1,0:T(8,128)(2,1)} %param.6, bf16[1024,1024]{1,0:T(8,128)(2,1)} %param.7, pred[1024]{0:T(1024)(128)(4,1)S(1)} %fusion.15), kind=kOutput, calls=%fused_computation.16 | convolution fusion | flops 8616148992 | bytes 27264000 | tf_op jit(solution)/shard_map/dot_general | solution.py:41
  70.0 101.3 %reduce-scatter.7.cloned.1.call-done = f32[32,4096]{1,0:T(8,128)} async-done(((f32[1024,4096]{1,0:T(8,128)}), f32[32,4096]{1,0:T(8,128)}) %reduce-scatter.7.cloned.1.call-update) | async-done | bytes 524304 | tf_op jit(solution)/shard_map/reduce_scatter | solution.py:54
  171.4 1.0 constant_dynamic-slice_fusion.3
  172.3 3.1 collective-permute-start
  175.4 114.5 %reduce-scatter.5.cloned.1.call-done = f32[128,1024]{1,0:T(8,128)} async-done(((f32[4096,1024]{1,0:T(8,128)}), f32[128,1024]{1,0:T(8,128)}) %reduce-scatter.5.cloned.1.call-update) | async-done | bytes 524304 | tf_op jit(solution)/shard_map/reduce_scatter | solution.py:40
  289.9 1.0 constant_dynamic-slice_fusion.2
  290.9 3.1 collective-permute-start.1
  294.0 1.6 multiply_reduce_fusion.4
  298.0 1.3 collective-permute-done.1
  299.3 1.7 multiply_reduce_fusion.1
  303.4 1.3 stack.48
  304.7 64.5 %psum.14 = f32[2,6]{1,0:T(2,128)S(1)} all-reduce(f32[2,6]{1,0:T(2,128)S(1)} %broadcast_multiply_fusion), channel_id=1, replica_groups=mesh['inner'=32,'rep'=4] {'inner','rep'}, use_global_device_ids=true, to_apply=%region_9.10 | all-reduce | flops 12 | bytes 96 | tf_op jit(solution)/shard_map/psum | solution.py:89
  375.2 1.0 multiply_add_fusion.1
  376.3 1.0 multiply_add_fusion
  377.3 2.1 collective-permute-start.3
  379.4 3.1 collective-permute-done.2
  388.7 1.3 stack.55
  390.0 62.4 %psum.15 = f32[1,6]{1,0:T(1,128)S(1)} all-reduce(f32[1,6]{1,0:T(1,128)S(1)} %stack.55), channel_id=1, replica_groups=mesh['inner'=32,'rep'=4] {'inner','rep'}, use_global_device_ids=true, to_apply=%region_17.18 | all-reduce | flops 6 | bytes 48 | tf_op jit(solution)/shard_map/psum | solution.py:89
  458.3 13.4 %all_gather.6 = f32[32,4096]{1,0:T(8,128)S(1)} all-gather(f32[8,4096]{1,0:T(8,128)S(1)} %multiply_add_fusion.3), channel_id=1, replica_groups=mesh['inner'=32,'rep'=4] {'rep'}, dimensions={0}, use_global_device_ids=true | all-gather | bytes 655360 | tf_op jit(solution)/shard_map/all_gather | solution.py:103
  471.8 13.3 %all_gather.7 = f32[128,1024]{1,0:T(8,128)S(1)} all-gather(f32[32,1024]{1,0:T(8,128)S(1)} %multiply_add_fusion.2), channel_id=1, replica_groups=mesh['inner'=32,'rep'=4] {'rep'}, dimensions={0}, use_global_device_ids=true | all-gather | bytes 655360 | tf_op jit(solution)/shard_map/all_gather | solution.py:104
  485.1 0.8 copy.31
  (25 shorter events, 4.8 us)
Async XLA Ops:
  7.2 1.6 copy-start
  7.2 164.2 %reduce-scatter.7.cloned.1.call-start = ((), (), s32[]{:S(2)}) async-start(), calls=%async_computation.3 | async-start | bytes 17301504 | tf_op jit(solution)/shard_map/reduce_scatter | solution.py:54
  53.4 236.5 %reduce-scatter.5.cloned.1.call-start = ((), (), s32[]{:S(2)}) async-start(), calls=%async_computation.2 | async-start | bytes 17301504 | tf_op jit(solution)/shard_map/reduce_scatter | solution.py:40
  53.6 433.0 %copy-start.1 = (bf16[1024,1024]{1,0:T(8,128)(2,1)S(1)}, bf16[1024,1024]{1,0:T(8,128)(2,1)}, u32[]{:S(2)}) copy-start(bf16[1024,1024]{1,0:T(8,128)(2,1)} %param.5) | copy-start | bytes 6291460
  172.3 121.6 %collective-permute-start = (f32[16,4096]{1,0:T(8,128)S(1)}, f32[16,4096]{1,0:T(8,128)S(1)}, u32[]{:S(2)}, u32[]{:S(2)}) collective-permute-start(f32[16,4096]{1,0:T(8,128)S(1)} %constant_dynamic-slice_fusion.3), channel_id=1, source_target_pairs={{0,2},{2,0},{1,3},{3,1},{4,6},{6,4},{5,7},{7,5},{8,10},{10,8},{9,1... | collective-permute-start | bytes 786440 | tf_op jit(solution)/shard_map/ppermute | solution.py:21
  290.9 8.4 %collective-permute-start.1 = (f32[64,1024]{1,0:T(8,128)S(1)}, f32[64,1024]{1,0:T(8,128)S(1)}, u32[]{:S(2)}, u32[]{:S(2)}) collective-permute-start(f32[64,1024]{1,0:T(8,128)S(1)} %constant_dynamic-slice_fusion.2), channel_id=1, source_target_pairs={{0,2},{2,0},{1,3},{3,1},{4,6},{6,4},{5,7},{7,5},{8,10},{10,8},{9,1... | collective-permute-start | bytes 786440 | tf_op jit(solution)/shard_map/ppermute | solution.py:21
  376.2 6.3 %collective-permute-start.2 = (f32[8,4096]{1,0:T(8,128)S(1)}, f32[8,4096]{1,0:T(8,128)S(1)}, u32[]{:S(2)}, u32[]{:S(2)}) collective-permute-start(f32[8,4096]{1,0:T(8,128)S(1)} %constant_dynamic-slice_fusion.1), channel_id=1, source_target_pairs={{0,1},{1,0},{2,3},{3,2},{4,5},{5,4},{6,7},{7,6},{8,9},{9,8},{10,11... | collective-permute-start | bytes 393224 | tf_op jit(solution)/shard_map/ppermute | solution.py:21
  377.3 8.2 %collective-permute-start.3 = (f32[32,1024]{1,0:T(8,128)S(1)}, f32[32,1024]{1,0:T(8,128)S(1)}, u32[]{:S(2)}, u32[]{:S(2)}) collective-permute-start(f32[32,1024]{1,0:T(8,128)S(1)} %constant_dynamic-slice_fusion), channel_id=1, source_target_pairs={{0,1},{1,0},{2,3},{3,2},{4,5},{5,4},{6,7},{7,6},{8,9},{9,8},{10,11... | collective-permute-start | bytes 393224 | tf_op jit(solution)/shard_map/ppermute | solution.py:21
Sparse Core Ops, SparseCore 0:
  53.5 117.7 reduce-scatter.6
  175.3 114.5 reduce-scatter.4
where the time goes:
time: 495 us; the launch traced here: 494 us
  waiting for transfers between devices  220 us (44%)
  blocking collectives  154 us (31%)
  matrix products  43.5 us (9%)
  between operations  34.3 us (7%)
  local copies, waits for them, and re-layouts  25.6 us (5%)
  starting transfers between devices  8.58 us (2%)
  other arithmetic  7.66 us (2%)
    psum x2, blocking collectives, on_device(): gathered_totals = lax.psum(slotted, ('inner', 'rep'))  127 us
    reduce_scatter x1, waiting for transfers between devices, on_device(): lax.psum_scatter(lax.dot_general(columns, masked, (((0,), (0,)), ((), ())...  114 us
    reduce_scatter x1, waiting for transfers between devices, on_device(): lax.psum_scatter(lax.dot_general(columns, pre_grad, (((0,), (0,)), ((), (...  101 us
    dot_general x1, matrix products, on_device(): lax.dot_general(columns, pre_grad, (((0,), (0,)), ((), ())), preferred_el...  27.1 us
    unnamed x7, local copies, waits for them, and re-layouts  19.7 us
    dot_general x1, matrix products, on_device(): lax.dot_general(columns, masked, (((0,), (0,)), ((), ())), preferred_elem...  16.3 us
    all_gather x1, blocking collectives, on_device(): lax.all_gather(up_piece, 'rep', axis=0, tiled=True)  13.4 us
    all_gather x1, blocking collectives, on_device(): lax.all_gather(down_piece, 'rep', axis=0, tiled=True)  13.3 us
  transfers between devices with their start and end apart: 6, of which 4 were waited for; matrix products, arithmetic and copies ran while one was open for 4% of the time, Pallas kernels for 0%

commit v1 on v0

v1 whole, which is shorter than its diff:
```python
import jax
import jax.numpy as jnp
from jax import lax
from jax.sharding import PartitionSpec as P

SEQ = 128
RING = 4
CORES = 2


SQRT_HALF = 0.7071067811865476
INV_ROOT_TWO_PI = 0.3989422804014327
EPSILON = 1e-06


def device_of(y, z, core):
    return (y % RING * RING + z % RING) * CORES + core


def ring_route(stage, step):
    route = []
    for y in range(RING):
        for z in range(RING):
            for core in range(CORES):
                along_y = core == stage
                target = device_of(y + step, z, core) if along_y else device_of(y, z + step, core)
                route.append((device_of(y, z, core), target))
    return route


def core_route():
    return [(index, index ^ 1) for index in range(RING * RING * CORES)]


def axis_route(axis, step):
    route = []
    for y in range(RING):
        for z in range(RING):
            for core in range(CORES):
                target = device_of(y + step, z, core) if axis == 0 else device_of(y, z + step, core)
                route.append((device_of(y, z, core), target))
    return route


def inner_permute(block, route):
    return lax.ppermute(block, "inner", route)


def ring_reduce(pieces, stage):
    ahead, behind = ring_route(stage, 1), ring_route(stage, -1)
    from_behind = inner_permute(jnp.stack([pieces[2][0], pieces[1][1]]), ahead)
    from_ahead = inner_permute(jnp.stack([pieces[2][1], pieces[3][0]]), behind)
    first = inner_permute(pieces[1][0] + from_behind[0], ahead)
    second = inner_permute(pieces[3][1] + from_ahead[0], behind)
    return (
        pieces[0][0] + from_ahead[1] + first,
        pieces[0][1] + from_behind[1] + second,
    )


def reduce_group(keep, send):
    total = keep + inner_permute(send, core_route())
    once = ring_reduce([[total[k, h] for h in range(2)] for k in range(RING)], 0)
    twice = ring_reduce([[once[h][l] for h in range(2)] for l in range(RING)], 1)
    return jnp.concatenate(twice, axis=0)


def destinations(core_to):
    inner = lax.axis_index("inner")
    y, z = inner // (RING * CORES), inner // CORES % RING
    k = lax.iota(jnp.int32, RING)[:, None]
    l = lax.iota(jnp.int32, RING)[None, :]
    to_y = jnp.where(core_to == 0, y + k, y + l) % RING
    to_z = jnp.where(core_to == 0, z + l, z + k) % RING
    return (to_y * RING + to_z) * CORES + core_to


def arrange(grad, core_to):
    rows = grad.shape[0] // (RING * RING * CORES * 2)
    order = destinations(core_to)[:, None, :] * 2 + lax.iota(jnp.int32, 2)[None, :, None]
    return grad.reshape(-1, rows, grad.shape[1])[order]


def across_replicas(block):
    count = lax.axis_size("rep")
    replica = lax.axis_index("rep")
    held = [block]
    for step in range(1, count):
        held.append(lax.ppermute(block, "rep", [(i, (i - step) % count) for i in range(count)]))
    return [lax.select_n((index - replica) % count, *held) for index in range(count)]


def products(vectors):
    a, d, b, e = vectors
    terms = []
    for first, second in ((a, b), (d, e)):
        both = first + second
        terms += [first * first, second * second, first * second, both * both, both * (first - second)]
    terms += [a * d, a * e, b * d, b * e]
    return jnp.stack([jnp.sum(term) for term in terms])


def sum_inner(values):
    values = values + inner_permute(values, core_route())
    for axis in (0, 1):
        others = [inner_permute(values, axis_route(axis, step)) for step in (1, 2, 3)]
        values = (values + others[1]) + (others[0] + others[2])
    return values


def pair_coefs(first_sq, second_sq, cross, both_sq, difference):
    first_wide, second_wide = first_sq + EPSILON, second_sq + EPSILON
    first_coef = 1.0 - cross / (2.0 * first_wide)
    second_coef = 1.0 - cross / (2.0 * second_wide)
    plain = (first_coef * first_coef * first_sq + 2.0 * first_coef * second_coef * cross
             + second_coef * second_coef * second_sq)
    mean = 0.5 * (first_coef + second_coef)
    skew = 0.25 * (cross / first_wide) * (difference / second_wide)
    apart = first_sq + second_sq - 2.0 * cross
    opposite = mean * mean * both_sq + 2.0 * mean * skew * difference + skew * skew * apart
    square = jnp.where(both_sq < 0.25 * (first_sq + second_sq), opposite, plain)
    return first_coef, second_coef, square


def coefficients(t):
    a, b, left = pair_coefs(t[0], t[1], t[2], t[3], t[4])
    d, e, right = pair_coefs(t[5], t[6], t[7], t[8], t[9])
    cross = a * (d * t[10] + e * t[11]) + b * (d * t[12] + e * t[13])
    left_coef = 1.0 - cross / (2.0 * (left + EPSILON))
    right_coef = 1.0 - cross / (2.0 * (right + EPSILON))
    return left_coef * a, right_coef * d, left_coef * b, right_coef * e


def mix(vectors, coefs):
    a, d, b, e = [vector * coef for vector, coef in zip(vectors, coefs)]
    return (a + b) + (d + e)


def on_device(layer_input, pre_act, cotangent, down_weight, lengths):
    row_count = layer_input.shape[0]
    seq_count = lengths.shape[0]
    core = lax.axis_index("inner") % CORES
    position = lax.iota(jnp.int32, row_count)
    owner = position // SEQ
    belongs = owner[:, None] == lax.iota(jnp.int32, seq_count)[None, :]
    allowed = jnp.sum(jnp.where(belongs, lengths[None, :], 0), axis=1)
    is_valid = position % SEQ < allowed
    masked = jnp.where(is_valid[:, None], cotangent, jnp.zeros_like(cotangent))
    pre_wide = pre_act.astype(jnp.float32)
    cdf_value = 0.5 * (1.0 + jax.scipy.special.erf(pre_wide * SQRT_HALF))
    hidden = (pre_wide * cdf_value).astype(jnp.bfloat16)
    down = lax.dot_general(
        hidden, masked, (((0,), (0,)), ((), ())), preferred_element_type=jnp.float32
    )
    hidden_grad = lax.dot_general(
        masked, down_weight, (((1,), (1,)), ((), ())), preferred_element_type=jnp.float32
    )
    derivative = cdf_value + pre_wide * jnp.exp(-0.5 * pre_wide * pre_wide) * INV_ROOT_TWO_PI
    pre_grad = (hidden_grad * derivative).astype(jnp.bfloat16)
    up = lax.dot_general(
        layer_input, pre_grad, (((0,), (0,)), ((), ())), preferred_element_type=jnp.float32
    )
    outs = []
    for grad in (down, up):
        piece = reduce_group(arrange(grad, core), arrange(grad, 1 - core))
        vectors = across_replicas(piece)
        totals = sum_inner(products(vectors))
        outs.append(mix(vectors, coefficients(totals)))
    return (outs[1], outs[0])


def solution(mesh):
    in_specs = (
        P(("inner", "rep"), None),
        P(("inner", "rep"), None),
        P(("inner", "rep"), None),
        P(),
        P(("inner", "rep")),
    )
    out_specs = (P("inner", None), P("inner", None))
    return jax.shard_map(
        on_device, mesh=mesh, in_specs=in_specs, out_specs=out_specs, check_vma=False
    )
```

time: 495 us -> 351 us (0.71)
  blocking collectives: 154 us -> 0 us
  waiting for transfers between devices: 220 us -> 94.9 us
  starting transfers between devices: 8.58 us -> 58.2 us
  local copies, waits for them, and re-layouts: 25.6 us -> 65 us
  other arithmetic: 7.66 us -> 41.3 us
  between operations: 34.3 us -> 43.7 us
    reduce_scatter x2 -> x0, waiting for transfers between devices: 216 us -> none  [the longest x1 114 us: on_device(): lax.psum_scatter(lax.dot_general(columns, masked, (((0,), (0,)), ((), ())...]
    psum x2 -> x0, blocking collectives: 127 us -> none  [on_device(): gathered_totals = lax.psum(slotted, ('inner', 'rep'))]
    ppermute x4 -> x38, waiting for transfers between devices: 4.37 us -> 94.9 us  [the longest x32 73.6 us: inner_permute(): return lax.ppermute(block, 'inner', route)]
    ppermute x4 -> x38, starting transfers between devices: 8.32 us -> 58.2 us  [the longest x32 48.3 us: inner_permute(): return lax.ppermute(block, 'inner', route)]
    gather x0 -> x4, local copies, waits for them, and re-layouts: none -> 40.2 us  [arrange(): return grad.reshape(-1, rows, grad.shape[1])[order]]
    add x4 -> x26, other arithmetic: 2.02 us -> 29.8 us  [the longest x2 23.1 us: reduce_group(): total = keep + inner_permute(send, core_route())]
    all_gather x2 -> x0, blocking collectives: 26.8 us -> none  [the longest x1 13.4 us: on_device(): lax.all_gather(up_piece, 'rep', axis=0, tiled=True)]
    another operation x2 -> x4, local copies, waits for them, and re-layouts: 2.59 us -> 23 us  [the longest x2 17.7 us: products(): return jnp.stack([jnp.sum(term) for term in terms])]
  transfers between devices with their start and end apart: 6 -> 38, of which waited for: 4 -> 14; matrix products, arithmetic and copies ran while one was open for 4% -> 34% of each run, Pallas kernels for 0% -> 0%
where the time goes in v1:
time: 351 us; the launch traced here: 345 us
  waiting for transfers between devices  94.9 us (27%)
  local copies, waits for them, and re-layouts  65 us (19%)
  starting transfers between devices  58.2 us (17%)
  between operations  43.7 us (12%)
  matrix products  42 us (12%)
  other arithmetic  41.3 us (12%)
    ppermute x32, waiting for transfers between devices, inner_permute(): return lax.ppermute(block, 'inner', route)  73.6 us
    ppermute x32, starting transfers between devices, inner_permute(): return lax.ppermute(block, 'inner', route)  48.3 us
    gather x4, local copies, waits for them, and re-layouts, arrange(): return grad.reshape(-1, rows, grad.shape[1])[order]  40.2 us
    dot_general x1, matrix products, on_device(): lax.dot_general(layer_input, pre_grad, (((0,), (0,)), ((), ())), preferre...  26.2 us
    add x2, other arithmetic, reduce_group(): total = keep + inner_permute(send, core_route())  23.1 us
    ppermute x6, waiting for transfers between devices, across_replicas(): lax.ppermute(block, 'rep', [(i, (i - step) % count) for i in range(count)])  21.3 us
    another operation x2, local copies, waits for them, and re-layouts, products(): return jnp.stack([jnp.sum(term) for term in terms])  17.7 us
    dot_general x1, matrix products, on_device(): lax.dot_general(hidden, masked, (((0,), (0,)), ((), ())), preferred_eleme...  15.8 us
  transfers between devices with their start and end apart: 38, of which 14 were waited for; matrix products, arithmetic and copies ran while one was open for 34% of the time, Pallas kernels for 0%

profile of v1, /device:TPU:0, one launch (start us, length us, event | category | flops | bytes accessed | tf_op | source)
XLA Modules:
  0.0 345.0 jit_solution(16401736110799279335)
XLA Ops:
  1.8 15.8 %fusion.10 = f32[4096,1024]{1,0:T(8,128)} fusion(bf16[1024,4096]{1,0:T(8,128)(2,1)} %param.6, bf16[1024,1024]{1,0:T(8,128)(2,1)} %param.7, pred[1024]{0:T(1024)(128)(4,1)S(1)} %fusion.38), kind=kOutput, calls=%fused_computation.19 | convolution fusion | flops 8616148992 | bytes 27264000 | tf_op jit(solution)/shard_map/dot_general | solution.py:152
  17.6 10.0 %gather_fusion.3 = f32[32,64,1024]{2,1,0:T(8,128)} fusion(f32[64,64,1024]{2,1,0:T(8,128)} %bitcast.188, s32[1024]{0:T(1024)S(1)} %pad_clamp_fusion), kind=kCustom, calls=%fused_computation.3 | custom fusion | bytes 16777344 | tf_op jit(solution)/shard_map/gather | solution.py:81
  27.8 26.2 %fusion.9 = f32[4096,1024]{0,1:T(8,128)} fusion(bf16[1024,1024]{1,0:T(8,128)(2,1)S(1)} %copy-done, bf16[1024,4096]{1,0:T(8,128)(2,1)} %param.6, bf16[4096,1024]{1,0:T(8,128)(2,1)} %param.8, bf16[1024,1024]{1,0:T(8,128)(2,1)} %param.7, pred[1024]{0:T(1024)(128)(4,1)S(1)} %fusion.38), kind=kOutput, calls=%fused_computation.18 | convolution fusion | flops 17227055104 | bytes 37749760 | tf_op jit(solution)/shard_map/dot_general | solution.py:160
  54.1 10.0 %gather_fusion.1 = f32[32,16,4096]{2,1,0:T(8,128)} fusion(f32[64,16,4096]{2,1,0:T(8,128)} %bitcast.190, s32[1024]{0:T(1024)S(1)} %pad_clamp_fusion), kind=kCustom, calls=%fused_computation.1 | custom fusion | bytes 16777344 | tf_op jit(solution)/shard_map/gather | solution.py:81
  64.9 10.0 %gather_fusion.2 = f32[32,64,1024]{2,1,0:T(8,128)} fusion(f32[64,64,1024]{2,1,0:T(8,128)} %bitcast.189, s32[1024]{0:T(1024)S(1)} %pad_clamp_fusion.1), kind=kCustom, calls=%fused_computation.2 | custom fusion | bytes 16777344 | tf_op jit(solution)/shard_map/gather | solution.py:81
  74.9 10.1 %gather_fusion = f32[32,16,4096]{2,1,0:T(8,128)} fusion(f32[64,16,4096]{2,1,0:T(8,128)} %bitcast.191, s32[1024]{0:T(1024)S(1)} %pad_clamp_fusion.1), kind=kCustom, calls=%fused_computation | custom fusion | bytes 16777344 | tf_op jit(solution)/shard_map/gather | solution.py:81
  85.0 11.9 %add.656 = f32[4,2,4,64,1024]{4,3,2,1,0:T(8,128)} add(f32[4,2,4,64,1024]{4,3,2,1,0:T(8,128)} %bitcast.183, f32[4,2,4,64,1024]{4,3,2,1,0:T(8,128)} %collective-permute-done.19) | non-fusion elementwise | flops 2097152 | bytes 25165824 | tf_op jit(solution)/shard_map/add | solution.py:62
  102.9 11.1 %add.603 = f32[4,2,4,16,4096]{4,3,2,1,0:T(8,128)} add(f32[4,2,4,16,4096]{4,3,2,1,0:T(8,128)} %bitcast.182, f32[4,2,4,16,4096]{4,3,2,1,0:T(8,128)} %collective-permute-done) | non-fusion elementwise | flops 2097152 | bytes 25165824 | tf_op jit(solution)/shard_map/add | solution.py:62
  119.5 6.9 %collective-permute-done.20 = f32[2,4,64,1024]{3,2,1,0:T(8,128)S(1)} collective-permute-done((f32[2,4,64,1024]{3,2,1,0:T(8,128)S(1)}, f32[2,4,64,1024]{3,2,1,0:T(8,128)S(1)}, u32[]{:S(2)}, u32[]{:S(2)}) %collective-permute-start.20) | collective-permute-done | bytes 2097184 | tf_op jit(solution)/shard_map/ppermute | solution.py:46
  126.6 3.8 %collective-permute-start.23 = (f32[4,64,1024]{2,1,0:T(8,128)S(1)}, f32[4,64,1024]{2,1,0:T(8,128)S(1)}, u32[]{:S(2)}, u32[]{:S(2)}) collective-permute-start(f32[4,64,1024]{2,1,0:T(8,128)S(1)} %fusion.14), channel_id=1, source_target_pairs={{0,96},{4,28},{8,104},{12,4},{16,112},{20,12},{24,120},{28,20},{32... | collective-permute-start | bytes 3145736 | tf_op jit(solution)/shard_map/ppermute | solution.py:46
  130.3 18.5 %collective-permute-done.1 = f32[2,4,16,4096]{3,2,1,0:T(8,128)S(1)} collective-permute-done((f32[2,4,16,4096]{3,2,1,0:T(8,128)S(1)}, f32[2,4,16,4096]{3,2,1,0:T(8,128)S(1)}, u32[]{:S(2)}, u32[]{:S(2)}) %collective-permute-start.1) | collective-permute-done | bytes 2097184 | tf_op jit(solution)/shard_map/ppermute | solution.py:46
  149.0 3.8 %collective-permute-start.4 = (f32[4,16,4096]{2,1,0:T(8,128)S(1)}, f32[4,16,4096]{2,1,0:T(8,128)S(1)}, u32[]{:S(2)}, u32[]{:S(2)}) collective-permute-start(f32[4,16,4096]{2,1,0:T(8,128)S(1)} %fusion.20), channel_id=1, source_target_pairs={{0,96},{4,28},{8,104},{12,4},{16,112},{20,12},{24,120},{28,20},{32... | collective-permute-start | bytes 3145736 | tf_op jit(solution)/shard_map/ppermute | solution.py:46
  152.8 7.4 %collective-permute-done.23 = f32[4,64,1024]{2,1,0:T(8,128)S(1)} collective-permute-done((f32[4,64,1024]{2,1,0:T(8,128)S(1)}, f32[4,64,1024]{2,1,0:T(8,128)S(1)}, u32[]{:S(2)}, u32[]{:S(2)}) %collective-permute-start.23) | collective-permute-done | bytes 1048608 | tf_op jit(solution)/shard_map/ppermute | solution.py:46
  161.8 5.9 %collective-permute-done.2 = f32[2,4,16,4096]{3,2,1,0:T(8,128)S(1)} collective-permute-done((f32[2,4,16,4096]{3,2,1,0:T(8,128)S(1)}, f32[2,4,16,4096]{3,2,1,0:T(8,128)S(1)}, u32[]{:S(2)}, u32[]{:S(2)}) %collective-permute-start.2) | collective-permute-done | bytes 2097184 | tf_op jit(solution)/shard_map/ppermute | solution.py:46
  172.9 6.0 %collective-permute-done.22 = f32[4,64,1024]{2,1,0:T(8,128)S(1)} collective-permute-done((f32[4,64,1024]{2,1,0:T(8,128)S(1)}, f32[4,64,1024]{2,1,0:T(8,128)S(1)}, u32[]{:S(2)}, u32[]{:S(2)}) %collective-permute-start.22) | collective-permute-done | bytes 1048608 | tf_op jit(solution)/shard_map/ppermute | solution.py:46
  181.2 14.5 %collective-permute-done.3 = f32[4,16,4096]{2,1,0:T(8,128)S(1)} collective-permute-done((f32[4,16,4096]{2,1,0:T(8,128)S(1)}, f32[4,16,4096]{2,1,0:T(8,128)S(1)}, u32[]{:S(2)}, u32[]{:S(2)}) %collective-permute-start.3) | collective-permute-done | bytes 1048608 | tf_op jit(solution)/shard_map/ppermute | solution.py:46
  200.8 6.7 %collective-permute-done.6 = f32[2,16,4096]{2,1,0:T(8,128)S(1)} collective-permute-done((f32[2,16,4096]{2,1,0:T(8,128)S(1)}, f32[2,16,4096]{2,1,0:T(8,128)S(1)}, u32[]{:S(2)}, u32[]{:S(2)}) %collective-permute-start.6) | collective-permute-done | bytes 524320 | tf_op jit(solution)/shard_map/ppermute | solution.py:46
  213.1 3.8 %collective-permute-done.5 = f32[2,16,4096]{2,1,0:T(8,128)S(1)} collective-permute-done((f32[2,16,4096]{2,1,0:T(8,128)S(1)}, f32[2,16,4096]{2,1,0:T(8,128)S(1)}, u32[]{:S(2)}, u32[]{:S(2)}) %collective-permute-start.5) | collective-permute-done | bytes 524320 | tf_op jit(solution)/shard_map/ppermute | solution.py:46
  229.3 8.7 %collective-permute-done.29 = f32[128,1024]{1,0:T(8,128)} collective-permute-done((f32[128,1024]{1,0:T(8,128)}, f32[128,1024]{1,0:T(8,128)}, u32[]{:S(2)}, u32[]{:S(2)}) %collective-permute-start.29) | collective-permute-done | bytes 524320 | tf_op jit(solution)/shard_map/ppermute | solution.py:89
  240.7 11.3 %collective-permute-done.30 = f32[128,1024]{1,0:T(8,128)} collective-permute-done((f32[128,1024]{1,0:T(8,128)}, f32[128,1024]{1,0:T(8,128)}, u32[]{:S(2)}, u32[]{:S(2)}) %collective-permute-start.30) | collective-permute-done | bytes 524320 | tf_op jit(solution)/shard_map/ppermute | solution.py:89
  252.0 4.2 %multiply_reduce_fusion = (f32[]{:T(128)}, f32[]{:T(128)}, f32[]{:T(128)}, f32[]{:T(128)}, f32[]{:T(128)}, /*index=5*/f32[]{:T(128)}, f32[]{:T(128)}, f32[]{:T(1...) fusion(f32[128,1024]{1,0:T(8,128)} %collective-permute-done.29,, ...), kind=kLoop, calls=%fused_computation.70 | loop fusion | flops 5898226 | bytes 4194372 | tf_op jit(solution)/shard_map/reduce_sum | solution.py:100
  256.2 8.9 %stack.151 = f32[14]{0:T(128)S(1)} concatenate(f32[1]{0:T(128)} %bitcast.68, f32[1]{0:T(128)} %bitcast.69, f32[1]{0:T(128)} %bitcast.70, f32[1]{0:T(128)} %bitcast.71, f32[1]{0:T(128)} %bitcast.72, f32[1]{0:T(128)} %bitcast.73, f32[1]{0:T(128)} %bitcast.74, f32[1]{0:T(128)} %bitcast.75, f32[1]{0:T(128)} %bitcast.76, f32[1]{0:T(128)} %bitcast.77, f32[1]{0:T(128)} %bitcast.78, ...), dimensions={0} | concatenate | bytes 112 | tf_op jit(solution)/shard_map/stack | solution.py:100
  266.4 3.9 %multiply_reduce_fusion.14 = (f32[]{:T(128)}, f32[]{:T(128)}, f32[]{:T(128)}, f32[]{:T(128)}, f32[]{:T(128)}, /*index=5*/f32[]{:T(128)}, f32[]{:T(128)}, f32[]{:...) fusion(f32[32,4096]{1,0:T(8,128)} %collective-permute-done.10, ...), kind=kLoop, calls=%fused_computation.89 | loop fusion | flops 5898226 | bytes 4194372 | tf_op jit(solution)/shard_map/reduce_sum | solution.py:100
  270.3 8.8 %stack.132 = f32[14]{0:T(128)S(1)} concatenate(f32[1]{0:T(128)} %bitcast.21, f32[1]{0:T(128)} %bitcast.22, f32[1]{0:T(128)} %bitcast.23, f32[1]{0:T(128)} %bitcast.24, f32[1]{0:T(128)} %bitcast.25, f32[1]{0:T(128)} %bitcast.26, f32[1]{0:T(128)} %bitcast.27, f32[1]{0:T(128)} %bitcast.28, f32[1]{0:T(128)} %bitcast.29, f32[1]{0:T(128)} %bitcast.30, f32[1]{0:T(128)} %bitcast.31, ...), dimensions={0} | concatenate | bytes 112 | tf_op jit(solution)/shard_map/stack | solution.py:100
  (129 shorter events, 73.2 us)
Async XLA Ops:
  27.7 57.3 %collective-permute-start.19 = (f32[4,2,4,64,1024]{4,3,2,1,0:T(8,128)}, f32[4,2,4,64,1024]{4,3,2,1,0:T(8,128)}, u32[]{:S(2)}, u32[]{:S(2)}) collective-permute-start(f32[4,2,4,64,1024]{4,3,2,1,0:T(8,128)} %bitcast.193), channel_id=1, source_target_pairs={{0,4},{4,0},{8,12},{12,8},{16,20},{20,16},{24,28},{28,24},{32,36},... | collective-permute-start | bytes 25165832 | tf_op jit(solution)/shard_map/ppermute | solution.py:46
  64.1 38.7 %collective-permute-start = (f32[4,2,4,16,4096]{4,3,2,1,0:T(8,128)}, f32[4,2,4,16,4096]{4,3,2,1,0:T(8,128)}, u32[]{:S(2)}, u32[]{:S(2)}) collective-permute-start(f32[4,2,4,16,4096]{4,3,2,1,0:T(8,128)} %bitcast.192), channel_id=1, source_target_pairs={{0,4},{4,0},{8,12},{12,8},{16,20},{20,16},{24,28},{28,24},{32,36},... | collective-permute-start | bytes 25165832 | tf_op jit(solution)/shard_map/ppermute | solution.py:46
  99.7 26.7 %collective-permute-start.20 = (f32[2,4,64,1024]{3,2,1,0:T(8,128)S(1)}, f32[2,4,64,1024]{3,2,1,0:T(8,128)S(1)}, u32[]{:S(2)}, u32[]{:S(2)}) collective-permute-start(f32[2,4,64,1024]{3,2,1,0:T(8,128)S(1)} %pad_maximum_fusion.2), channel_id=1, source_target_pairs={{0,96},{4,28},{8,104},{12,4},{16,112},{20,12},{24,120},{28,20},{32... | collective-permute-start | bytes 6291464 | tf_op jit(solution)/shard_map/ppermute | solution.py:46
  116.9 32.0 %collective-permute-start.1 = (f32[2,4,16,4096]{3,2,1,0:T(8,128)S(1)}, f32[2,4,16,4096]{3,2,1,0:T(8,128)S(1)}, u32[]{:S(2)}, u32[]{:S(2)}) collective-permute-start(f32[2,4,16,4096]{3,2,1,0:T(8,128)S(1)} %pad_maximum_fusion), channel_id=1, source_target_pairs={{0,96},{4,28},{8,104},{12,4},{16,112},{20,12},{24,120},{28,20},{32... | collective-permute-start | bytes 6291464 | tf_op jit(solution)/shard_map/ppermute | solution.py:46
  117.9 34.9 %collective-permute-start.21 = (f32[2,4,64,1024]{3,2,1,0:T(8,128)S(1)}, f32[2,4,64,1024]{3,2,1,0:T(8,128)S(1)}, u32[]{:S(2)}, u32[]{:S(2)}) collective-permute-start(f32[2,4,64,1024]{3,2,1,0:T(8,128)S(1)} %pad_maximum_fusion.3), channel_id=1, source_target_pairs={{0,32},{4,12},{8,40},{12,20},{16,48},{20,28},{24,56},{28,4},{32,64... | collective-permute-start | bytes 6291464 | tf_op jit(solution)/shard_map/ppermute | solution.py:46
  119.4 48.2 %collective-permute-start.2 = (f32[2,4,16,4096]{3,2,1,0:T(8,128)S(1)}, f32[2,4,16,4096]{3,2,1,0:T(8,128)S(1)}, u32[]{:S(2)}, u32[]{:S(2)}) collective-permute-start(f32[2,4,16,4096]{3,2,1,0:T(8,128)S(1)} %pad_maximum_fusion.1), channel_id=1, source_target_pairs={{0,32},{4,12},{8,40},{12,20},{16,48},{20,28},{24,56},{28,4},{32,64... | collective-permute-start | bytes 6291464 | tf_op jit(solution)/shard_map/ppermute | solution.py:46
  126.6 33.5 %collective-permute-start.23 = (f32[4,64,1024]{2,1,0:T(8,128)S(1)}, f32[4,64,1024]{2,1,0:T(8,128)S(1)}, u32[]{:S(2)}, u32[]{:S(2)}) collective-permute-start(f32[4,64,1024]{2,1,0:T(8,128)S(1)} %fusion.14), channel_id=1, source_target_pairs={{0,96},{4,28},{8,104},{12,4},{16,112},{20,12},{24,120},{28,20},{32... | collective-permute-start | bytes 3145736 | tf_op jit(solution)/shard_map/ppermute | solution.py:46
  149.0 22.4 %collective-permute-start.4 = (f32[4,16,4096]{2,1,0:T(8,128)S(1)}, f32[4,16,4096]{2,1,0:T(8,128)S(1)}, u32[]{:S(2)}, u32[]{:S(2)}) collective-permute-start(f32[4,16,4096]{2,1,0:T(8,128)S(1)} %fusion.20), channel_id=1, source_target_pairs={{0,96},{4,28},{8,104},{12,4},{16,112},{20,12},{24,120},{28,20},{32... | collective-permute-start | bytes 3145736 | tf_op jit(solution)/shard_map/ppermute | solution.py:46
  160.7 18.2 %collective-permute-start.22 = (f32[4,64,1024]{2,1,0:T(8,128)S(1)}, f32[4,64,1024]{2,1,0:T(8,128)S(1)}, u32[]{:S(2)}, u32[]{:S(2)}) collective-permute-start(f32[4,64,1024]{2,1,0:T(8,128)S(1)} %get-tuple-element.51), channel_id=1, source_target_pairs={{0,32},{4,12},{8,40},{12,20},{16,48},{20,28},{24,56},{28,4},{32,64... | collective-permute-start | bytes 3145736 | tf_op jit(solution)/shard_map/ppermute | solution.py:46
  171.6 24.1 %collective-permute-start.3 = (f32[4,16,4096]{2,1,0:T(8,128)S(1)}, f32[4,16,4096]{2,1,0:T(8,128)S(1)}, u32[]{:S(2)}, u32[]{:S(2)}) collective-permute-start(f32[4,16,4096]{2,1,0:T(8,128)S(1)} %get-tuple-element.53), channel_id=1, source_target_pairs={{0,32},{4,12},{8,40},{12,20},{16,48},{20,28},{24,56},{28,4},{32,64... | collective-permute-start | bytes 3145736 | tf_op jit(solution)/shard_map/ppermute | solution.py:46
  179.2 18.7 %collective-permute-start.25 = (f32[2,64,1024]{2,1,0:T(8,128)S(1)}, f32[2,64,1024]{2,1,0:T(8,128)S(1)}, u32[]{:S(2)}, u32[]{:S(2)}) collective-permute-start(f32[2,64,1024]{2,1,0:T(8,128)S(1)} %pad_maximum_fusion.8), channel_id=1, source_target_pairs={{0,8},{4,36},{8,16},{12,44},{16,24},{20,52},{24,0},{28,60},{32,40}... | collective-permute-start | bytes 1572872 | tf_op jit(solution)/shard_map/ppermute | solution.py:46
  196.0 11.6 %collective-permute-start.6 = (f32[2,16,4096]{2,1,0:T(8,128)S(1)}, f32[2,16,4096]{2,1,0:T(8,128)S(1)}, u32[]{:S(2)}, u32[]{:S(2)}) collective-permute-start(f32[2,16,4096]{2,1,0:T(8,128)S(1)} %pad_maximum_fusion.5), channel_id=1, source_target_pairs={{0,8},{4,36},{8,16},{12,44},{16,24},{20,52},{24,0},{28,60},{32,40}... | collective-permute-start | bytes 1572872 | tf_op jit(solution)/shard_map/ppermute | solution.py:46
  198.1 11.7 %collective-permute-start.24 = (f32[2,64,1024]{2,1,0:T(8,128)S(1)}, f32[2,64,1024]{2,1,0:T(8,128)S(1)}, u32[]{:S(2)}, u32[]{:S(2)}) collective-permute-start(f32[2,64,1024]{2,1,0:T(8,128)S(1)} %pad_maximum_fusion.7), channel_id=1, source_target_pairs={{0,24},{4,100},{8,0},{12,108},{16,8},{20,116},{24,16},{28,124},{32... | collective-permute-start | bytes 1572872 | tf_op jit(solution)/shard_map/ppermute | solution.py:46
  216.9 10.6 %collective-permute-start.8 = (f32[16,4096]{1,0:T(8,128)S(1)}, f32[16,4096]{1,0:T(8,128)S(1)}, u32[]{:S(2)}, u32[]{:S(2)}) collective-permute-start(f32[16,4096]{1,0:T(8,128)S(1)} %fusion.32), channel_id=1, source_target_pairs={{0,24},{4,100},{8,0},{12,108},{16,8},{20,116},{24,16},{28,124},{32... | collective-permute-start | bytes 786440 | tf_op jit(solution)/shard_map/ppermute | solution.py:46
  221.3 16.7 %collective-permute-start.29 = (f32[128,1024]{1,0:T(8,128)}, f32[128,1024]{1,0:T(8,128)}, u32[]{:S(2)}, u32[]{:S(2)}) collective-permute-start(f32[128,1024]{1,0:T(8,128)} %pad_maximum_fusion.9), channel_id=1, source_target_pairs={{0,2},{1,3},{2,0},{3,1},{4,6},{5,7},{6,4},{7,5},{8,10},{9,11},{10,... | collective-permute-start | bytes 1572872 | tf_op jit(solution)/shard_map/ppermute | solution.py:89
  224.3 27.7 %collective-permute-start.30 = (f32[128,1024]{1,0:T(8,128)}, f32[128,1024]{1,0:T(8,128)}, u32[]{:S(2)}, u32[]{:S(2)}) collective-permute-start(f32[128,1024]{1,0:T(8,128)} %pad_maximum_fusion.9), channel_id=1, source_target_pairs={{0,1},{1,2},{2,3},{3,0},{4,5},{5,6},{6,7},{7,4},{8,9},{9,10},{10,1... | collective-permute-start | bytes 1572872 | tf_op jit(solution)/shard_map/ppermute | solution.py:89
  224.9 27.1 %collective-permute-start.28 = (f32[128,1024]{1,0:T(8,128)}, f32[128,1024]{1,0:T(8,128)}, u32[]{:S(2)}, u32[]{:S(2)}) collective-permute-start(f32[128,1024]{1,0:T(8,128)} %pad_maximum_fusion.9), channel_id=1, source_target_pairs={{0,3},{1,0},{2,1},{3,2},{4,7},{5,4},{6,5},{7,6},{8,11},{9,8},{10,9... | collective-permute-start | bytes 1572872 | tf_op jit(solution)/shard_map/ppermute | solution.py:89
  228.4 36.7 %collective-permute-start.10 = (f32[32,4096]{1,0:T(8,128)}, f32[32,4096]{1,0:T(8,128)}, u32[]{:S(2)}, u32[]{:S(2)}) collective-permute-start(f32[32,4096]{1,0:T(8,128)} %pad_maximum_fusion.6), channel_id=1, source_target_pairs={{0,2},{1,3},{2,0},{3,1},{4,6},{5,7},{6,4},{7,5},{8,10},{9,11},{10,... | collective-permute-start | bytes 1572872 | tf_op jit(solution)/shard_map/ppermute | solution.py:89
  228.4 37.9 %collective-permute-start.11 = (f32[32,4096]{1,0:T(8,128)}, f32[32,4096]{1,0:T(8,128)}, u32[]{:S(2)}, u32[]{:S(2)}) collective-permute-start(f32[32,4096]{1,0:T(8,128)} %pad_maximum_fusion.6), channel_id=1, source_target_pairs={{0,1},{1,2},{2,3},{3,0},{4,5},{5,6},{6,7},{7,4},{8,9},{9,10},{10,1... | collective-permute-start | bytes 1572872 | tf_op jit(solution)/shard_map/ppermute | solution.py:89
  237.9 28.5 %collective-permute-start.9 = (f32[32,4096]{1,0:T(8,128)}, f32[32,4096]{1,0:T(8,128)}, u32[]{:S(2)}, u32[]{:S(2)}) collective-permute-start(f32[32,4096]{1,0:T(8,128)} %pad_maximum_fusion.6), channel_id=1, source_target_pairs={{0,3},{1,0},{2,1},{3,2},{4,7},{5,4},{6,5},{7,6},{8,11},{9,8},{10,9... | collective-permute-start | bytes 1572872 | tf_op jit(solution)/shard_map/ppermute | solution.py:89
  265.0 14.2 %collective-permute-start.31 = (f32[14]{0:T(128)S(1)}, f32[14]{0:T(128)S(1)}, u32[]{:S(2)}, u32[]{:S(2)}) collective-permute-start(f32[14]{0:T(128)S(1)} %stack.151), channel_id=1, source_target_pairs={{0,4},{4,0},{8,12},{12,8},{16,20},{20,16},{24,28},{28,24},{32,36},... | collective-permute-start | bytes 176 | tf_op jit(solution)/shard_map/ppermute | solution.py:46
  291.4 26.5 %collective-permute-start.18 = (f32[14]{0:T(128)S(1)}, f32[14]{0:T(128)S(1)}, u32[]{:S(2)}, u32[]{:S(2)}) collective-permute-start(f32[14]{0:T(128)S(1)} %add_add_fusion.5), channel_id=1, source_target_pairs={{0,24},{4,28},{8,0},{12,4},{16,8},{20,12},{24,16},{28,20},{32,56},... | collective-permute-start | bytes 176 | tf_op jit(solution)/shard_map/ppermute | solution.py:46
  293.4 24.6 %collective-permute-start.17 = (f32[14]{0:T(128)S(1)}, f32[14]{0:T(128)S(1)}, u32[]{:S(2)}, u32[]{:S(2)}) collective-permute-start(f32[14]{0:T(128)S(1)} %add_add_fusion.5), channel_id=1, source_target_pairs={{0,8},{4,12},{8,16},{12,20},{16,24},{20,28},{24,0},{28,4},{32,40},... | collective-permute-start | bytes 176 | tf_op jit(solution)/shard_map/ppermute | solution.py:46
  293.5 24.5 %collective-permute-start.16 = (f32[14]{0:T(128)S(1)}, f32[14]{0:T(128)S(1)}, u32[]{:S(2)}, u32[]{:S(2)}) collective-permute-start(f32[14]{0:T(128)S(1)} %add_add_fusion.5), channel_id=1, source_target_pairs={{0,16},{4,20},{8,24},{12,28},{16,0},{20,4},{24,8},{28,12},{32,48},... | collective-permute-start | bytes 176 | tf_op jit(solution)/shard_map/ppermute | solution.py:46
  (20 other events, 340.9 us)

commit v2 on v1

v2 whole, which is shorter than its diff:
```python
import math

import jax
import jax.numpy as jnp
from jax import lax
from jax.experimental import pallas as pl
from jax.experimental.pallas import tpu as pltpu
from jax.sharding import PartitionSpec as P

SEQ = 128
RING = 4
CORES = 2
CHIPS = RING * RING
HALVES = 2
LANES = 128
FF_BLOCK = 256
UP_SPLITS = 2
MIB = 1024 * 1024

EPSILON = 1e-06
INV_ROOT_TWO_PI = 0.3989422804014327
EXP2_SCALE = -0.5 / math.log(2.0)
TAIL_SCALE = 0.28
TAIL = (0.11652077734470367, 0.06749676167964935, 0.26891013979911804,
        -0.2369934469461441, 0.38987401127815247, -0.10580823570489883)
TERMS = 14
TERM_ROWS = 16


def device_of(y, z, core):
    return (y % RING * RING + z % RING) * CORES + core


def inner_route(move):
    route = []
    for y in range(RING):
        for z in range(RING):
            for core in range(CORES):
                route.append((device_of(y, z, core), device_of(*move(y, z, core))))
    return route


def ring_route(stage, step):
    return inner_route(
        lambda y, z, core: (y + step, z, core) if core == stage else (y, z + step, core)
    )


def core_route():
    return inner_route(lambda y, z, core: (y, z, 1 - core))


def inner_permute(block, route):
    return lax.ppermute(block, "inner", route)


def ring_reduce(piece, stage):
    ahead, behind = ring_route(stage, 1), ring_route(stage, -1)
    from_behind = inner_permute(jnp.stack([piece(2, 0), piece(1, 1)]), ahead)
    from_ahead = inner_permute(jnp.stack([piece(2, 1), piece(3, 0)]), behind)
    first = inner_permute(piece(1, 0) + from_behind[0], ahead)
    second = inner_permute(piece(3, 1) + from_ahead[0], behind)
    return (
        lambda at: piece(0, 0)[at] + from_ahead[1][at] + first[at],
        lambda at: piece(0, 1)[at] + from_behind[1][at] + second[at],
    )


def reduce_group(keep, send):
    other = inner_permute(send, core_route())
    once = ring_reduce(lambda k, h: keep[k, h] + other[k, h], 0)
    twice = ring_reduce(lambda l, h: once[h](l), 1)
    return jnp.concatenate([half(slice(None)) for half in twice], axis=0)


def destination_table():
    inner = lax.axis_index("inner")
    y, z, core = inner // (RING * CORES), inner // CORES % RING, inner % CORES
    k = lax.iota(jnp.int32, RING)[:, None]
    l = lax.iota(jnp.int32, RING)[None, :]

    def order(core_to):
        to_y = jnp.where(core_to == 0, y + k, y + l) % RING
        to_z = jnp.where(core_to == 0, z + l, z + k) % RING
        return (to_y * RING + to_z) * CORES + core_to

    return jnp.stack([order(core), order(1 - core)])


def write_masked(lengths_ref, cotangent_ref, masked_ref):
    columns = cotangent_ref.shape[1]
    for seq in range(cotangent_ref.shape[0] // SEQ):
        rows = slice(seq * SEQ, (seq + 1) * SEQ)
        valid = lax.broadcasted_iota(jnp.int32, (SEQ, columns), 0) < lengths_ref[seq]
        values = cotangent_ref[rows, :].astype(jnp.float32)
        masked_ref[rows, :] = jnp.where(valid, values, 0.0).astype(masked_ref.dtype)


def up_kernel(rows_ref, lengths_ref, x_ref, cotangent_ref, pre_ref, weight_ref,
              keep_ref, send_ref, hidden_ref, turned_ref, ordered_ref, masked_ref, grad_ref):
    tokens, width = x_ref.shape
    strip = width // (CHIPS * CORES * HALVES)

    @pl.when(pl.program_id(0) == 0)
    def _():
        write_masked(lengths_ref, cotangent_ref, masked_ref)
        turned_ref[...] = x_ref[...].T
        for index in range(width // strip):
            start = pl.multiple_of(rows_ref[index], strip)
            ordered_ref[index * strip:(index + 1) * strip, :] = turned_ref[pl.ds(start, strip), :]

    part = tokens // 4
    for index in range(4):
        rows = slice(index * part, (index + 1) * part)
        hidden_grad = lax.dot_general(
            masked_ref[rows, :], weight_ref[...], (((1,), (1,)), ((), ())),
            preferred_element_type=jnp.float32,
        )
        value = pre_ref[rows, :].astype(jnp.float32)
        density = jnp.exp2(value * value * EXP2_SCALE)
        t = 1.0 / (1.0 + TAIL_SCALE * jnp.abs(value))
        poly = TAIL[-1]
        for term in TAIL[-2::-1]:
            poly = poly * t + term
        tail = poly * t * density
        cdf = jnp.where(value < 0.0, tail, 1.0 - tail)
        hidden_ref[rows, :] = (value * cdf).astype(hidden_ref.dtype)
        derivative = cdf + value * density * INV_ROOT_TWO_PI
        grad_ref[rows, :] = (hidden_grad * derivative).astype(grad_ref.dtype)
    half = width // CORES
    keep_ref[...] = jnp.dot(ordered_ref[:half, :], grad_ref[...], preferred_element_type=jnp.float32)
    send_ref[...] = jnp.dot(ordered_ref[half:, :], grad_ref[...], preferred_element_type=jnp.float32)


def up_call(table, lengths, x, cotangent, pre_act, weight, part):
    tokens, width = x.shape
    hidden_units = pre_act.shape[1] // UP_SPLITS
    steps = hidden_units // FF_BLOCK
    strip = width // (CHIPS * CORES * HALVES)
    half = lax.iota(jnp.int32, HALVES)[None, None, :, None]
    rows = (table[:, :, None, :] * HALVES + half).reshape(-1) * strip
    whole = pl.BlockSpec(memory_space=pltpu.VMEM)
    out_block = pl.BlockSpec((width // CORES, FF_BLOCK), lambda j, *_: (0, j))
    keep, send, hidden = pl.pallas_call(
        up_kernel,
        grid_spec=pltpu.PrefetchScalarGridSpec(
            num_scalar_prefetch=2,
            grid=(steps,),
            in_specs=[
                whole,
                whole,
                pl.BlockSpec((tokens, FF_BLOCK), lambda j, *_: (0, part * steps + j)),
                pl.BlockSpec((FF_BLOCK, width), lambda j, *_: (part * steps + j, 0)),
            ],
            out_specs=[
                out_block,
                out_block,
                pl.BlockSpec((tokens, FF_BLOCK), lambda j, *_: (0, j)),
            ],
            scratch_shapes=[
                pltpu.VMEM((width, tokens), jnp.bfloat16),
                pltpu.VMEM((width, tokens), jnp.bfloat16),
                pltpu.VMEM((tokens, width), jnp.bfloat16),
                pltpu.VMEM((tokens, FF_BLOCK), jnp.bfloat16),
            ],
        ),
        out_shape=[
            jax.ShapeDtypeStruct((width // CORES, hidden_units), jnp.float32),
            jax.ShapeDtypeStruct((width // CORES, hidden_units), jnp.float32),
            jax.ShapeDtypeStruct((tokens, hidden_units), jnp.bfloat16),
        ],
        compiler_params=pltpu.CompilerParams(vmem_limit_bytes=40 * MIB),
        cost_estimate=pl.CostEstimate(
            flops=4 * tokens * width * hidden_units,
            bytes_accessed=(4 * tokens * width + 4 * tokens * hidden_units
                            + 6 * width * hidden_units),
            transcendentals=2 * tokens * hidden_units,
        ),
        name="up_partial",
    )(rows, lengths, x, cotangent, pre_act, weight)
    shape = (RING, HALVES, RING, strip, hidden_units)
    return keep.reshape(shape), send.reshape(shape), hidden


def down_kernel(blocks_ref, lengths_ref, cotangent_ref, *refs):
    hidden_refs, (keep_ref, send_ref, masked_ref) = refs[:-3], refs[-3:]

    @pl.when(pl.program_id(0) == 0)
    def _():
        write_masked(lengths_ref, cotangent_ref, masked_ref)

    parts = len(hidden_refs) // 2
    index = pl.program_id(0)
    columns = []
    for which in range(2):
        block = blocks_ref[which * CHIPS + index]
        mine = hidden_refs[which * parts][...]
        for part in range(1, parts):
            other = hidden_refs[which * parts + part][...]
            count = CHIPS * CORES // parts
            mine = jnp.where(block // count == part, other, mine)
        columns.append(mine)
    product = lax.dot_general(
        jnp.concatenate(columns, axis=1), masked_ref[...], (((0,), (0,)), ((), ())),
        preferred_element_type=jnp.float32,
    )
    rows = product.shape[0] // 2
    keep_ref[...] = product[:rows].reshape(keep_ref.shape)
    send_ref[...] = product[rows:].reshape(send_ref.shape)


def down_call(table, lengths, cotangent, hidden_parts):
    tokens, width = cotangent.shape
    parts = len(hidden_parts)
    count = CHIPS * CORES // parts
    rows = hidden_parts[0].shape[1] // count
    blocks = table.reshape(-1)

    def hidden_spec(which, part):
        def place(i, blocks_ref, lengths_ref):
            block = blocks_ref[which * CHIPS + i] - part * count
            return 0, jnp.clip(block, 0, count - 1)

        return pl.BlockSpec((tokens, rows), place)

    out_block = pl.BlockSpec(
        (1, HALVES, 1, rows // HALVES, width), lambda i, *_: (i // RING, 0, i % RING, 0, 0)
    )
    out_shape = jax.ShapeDtypeStruct(
        (RING, HALVES, RING, rows // HALVES, width), jnp.float32
    )
    return pl.pallas_call(
        down_kernel,
        grid_spec=pltpu.PrefetchScalarGridSpec(
            num_scalar_prefetch=2,
            grid=(CHIPS,),
            in_specs=[pl.BlockSpec(memory_space=pltpu.VMEM)]
            + [hidden_spec(which, part) for which in range(2) for part in range(parts)],
            out_specs=[out_block, out_block],
            scratch_shapes=[pltpu.VMEM((tokens, width), jnp.bfloat16)],
        ),
        out_shape=[out_shape, out_shape],
        compiler_params=pltpu.CompilerParams(vmem_limit_bytes=40 * MIB),
        cost_estimate=pl.CostEstimate(
            flops=2 * tokens * width * rows * CHIPS * CORES,
            bytes_accessed=2 * tokens * width + (2 * tokens + 4 * width) * rows * CHIPS * CORES,
            transcendentals=0,
        ),
        name="down_partial",
    )(blocks, lengths, cotangent, *hidden_parts * 2)


def across_replicas(block):
    count = lax.axis_size("rep")
    held = [block]
    for step in range(1, count):
        held.append(lax.ppermute(block, "rep", [(i, (i - step) % count) for i in range(count)]))
    return held


def in_order(values, replica):
    once = [jnp.where(replica % 2 == 1, values[i - 1], values[i]) for i in range(4)]
    return [jnp.where(replica // 2 == 1, once[i - 2], once[i]) for i in range(4)]


def products_kernel(replica_ref, *refs):
    groups, out_ref = refs[:-1], refs[-1]
    replica = replica_ref[0]
    totals = jnp.zeros((TERMS * 8, LANES), jnp.float32)
    for first in range(0, len(groups), 4):
        held = groups[first:first + 4]
        rows, columns = held[0].shape

        def add_rows(index, totals):
            at = pl.ds(pl.multiple_of(index * 8, 8), 8)
            sums = [totals[i * 8:(i + 1) * 8, :] for i in range(TERMS)]
            for column in range(0, columns, LANES):
                values = [ref[at, column:column + LANES] for ref in held]
                a, d, b, e = in_order(values, replica)
                terms = []
                for left, right in ((a, b), (d, e)):
                    both = left + right
                    terms += [left * left, right * right, left * right, both * both,
                              both * (left - right)]
                terms += [a * d, a * e, b * d, b * e]
                sums = [total + term for total, term in zip(sums, terms)]
            return jnp.concatenate(sums, axis=0)

        totals = lax.fori_loop(0, rows // 8, add_rows, totals)
    for i in range(TERMS):
        out_ref[i:i + 1, :] = jnp.sum(totals[i * 8:(i + 1) * 8, :], axis=0, keepdims=True)
    out_ref[TERMS:, :] = jnp.zeros((TERM_ROWS - TERMS, LANES), jnp.float32)


def products_call(replica, groups):
    flat = [block for held in groups for block in held]
    vmem = pl.BlockSpec(memory_space=pltpu.VMEM)
    return pl.pallas_call(
        products_kernel,
        in_specs=[pl.BlockSpec(memory_space=pltpu.SMEM)] + [vmem] * len(flat),
        out_specs=vmem,
        out_shape=jax.ShapeDtypeStruct((TERM_ROWS, LANES), jnp.float32),
        compiler_params=pltpu.CompilerParams(vmem_limit_bytes=24 * MIB),
        cost_estimate=pl.CostEstimate(
            flops=TERMS * 2 * sum(block.size for block in flat) // 4,
            bytes_accessed=4 * sum(block.size for block in flat),
            transcendentals=0,
        ),
        name="inner_products",
    )(replica, *flat)


def sum_inner(values):
    values = values + inner_permute(values, core_route())
    for axis in (0, 1):
        others = [
            inner_permute(values, inner_route(
                lambda y, z, core: (y + step, z, core) if axis == 0 else (y, z + step, core)))
            for step in (1, 2, 3)
        ]
        values = (values + others[1]) + (others[0] + others[2])
    return values


def pair_coefs(first_sq, second_sq, cross, both_sq, difference):
    first_wide, second_wide = first_sq + EPSILON, second_sq + EPSILON
    first_coef = 1.0 - cross / (2.0 * first_wide)
    second_coef = 1.0 - cross / (2.0 * second_wide)
    plain = (first_coef * first_coef * first_sq + 2.0 * first_coef * second_coef * cross
             + second_coef * second_coef * second_sq)
    mean = 0.5 * (first_coef + second_coef)
    skew = 0.25 * (cross / first_wide) * (difference / second_wide)
    apart = first_sq + second_sq - 2.0 * cross
    opposite = mean * mean * both_sq + 2.0 * mean * skew * difference + skew * skew * apart
    square = jnp.where(both_sq < 0.25 * (first_sq + second_sq), opposite, plain)
    return first_coef, second_coef, square


def coefficients(t):
    a, b, left = pair_coefs(*t[0:5])
    d, e, right = pair_coefs(*t[5:10])
    cross = a * (d * t[10] + e * t[11]) + b * (d * t[12] + e * t[13])
    left_coef = 1.0 - cross / (2.0 * (left + EPSILON))
    right_coef = 1.0 - cross / (2.0 * (right + EPSILON))
    return left_coef * a, right_coef * d, left_coef * b, right_coef * e


def mix_kernel(replica_ref, totals_ref, *refs):
    groups, out_ref = refs[:-1], refs[-1]
    replica = replica_ref[0]
    totals = jnp.sum(totals_ref[...], axis=1, keepdims=True)
    coefs = coefficients([totals[i:i + 1, :] for i in range(TERMS)])
    start = 0
    for first in range(0, len(groups), 4):
        held = groups[first:first + 4]
        columns = held[0].shape[1]
        a, d, b, e = [
            value * coef for value, coef in zip(in_order([ref[...] for ref in held], replica), coefs)
        ]
        out_ref[:, start:start + columns] = (a + b) + (d + e)
        start += columns


def mix_call(replica, totals, groups):
    flat = [block for held in groups for block in held]
    rows = flat[0].shape[0]
    columns = sum(held[0].shape[1] for held in groups)
    vmem = pl.BlockSpec(memory_space=pltpu.VMEM)
    return pl.pallas_call(
        mix_kernel,
        in_specs=[pl.BlockSpec(memory_space=pltpu.SMEM)] + [vmem] * (len(flat) + 1),
        out_specs=vmem,
        out_shape=jax.ShapeDtypeStruct((rows, columns), jnp.float32),
        compiler_params=pltpu.CompilerParams(vmem_limit_bytes=24 * MIB),
        cost_estimate=pl.CostEstimate(
            flops=7 * rows * columns, bytes_accessed=20 * rows * columns, transcendentals=0
        ),
        name="combine",
    )(replica, totals, *flat)


def on_device(layer_input, pre_act, cotangent, down_weight, lengths):
    table = destination_table()
    replica = lax.axis_index("rep").reshape(1)
    up_groups, hidden_parts = [], []
    for part in range(UP_SPLITS):
        keep, send, hidden = up_call(
            table, lengths, layer_input, cotangent, pre_act, down_weight, part
        )
        up_groups.append(across_replicas(reduce_group(keep, send)))
        hidden_parts.append(hidden)
    keep, send = down_call(table, lengths, cotangent, hidden_parts)
    down_groups = [across_replicas(reduce_group(keep, send))]
    totals = sum_inner(jnp.stack([
        products_call(replica, up_groups), products_call(replica, down_groups)
    ]))
    return (
        mix_call(replica, totals[0], up_groups),
        mix_call(replica, totals[1], down_groups),
    )


def solution(mesh):
    in_specs = (
        P(("inner", "rep"), None),
        P(("inner", "rep"), None),
        P(("inner", "rep"), None),
        P(),
        P(("inner", "rep")),
    )
    out_specs = (P("inner", None), P("inner", None))
    return jax.shard_map(
        on_device, mesh=mesh, in_specs=in_specs, out_specs=out_specs, check_vma=False
    )
```

time: 351 us -> 287 us (0.82); the launches traced: 345 us -> 287 us
  Pallas kernels: 0 us -> 67.2 us
  local copies, waits for them, and re-layouts: 65 us -> 18.2 us
  between operations: 43.7 us -> 1.24 us
  matrix products: 42 us -> 0 us
  waiting for transfers between devices: 94.9 us -> 116 us
  other arithmetic: 41.3 us -> 23.7 us
    pallas_call x0 -> x7, Pallas kernels: none -> 67.2 us  [the longest x2 42.2 us: up_call(): pl.pallas_call(up_kernel, grid_spec=pltpu.PrefetchScalarGridSpec(num_scal...]
    dot_general x2 -> x0, matrix products: 42 us -> none  [the longest x1 26.2 us: on_device(): lax.dot_general(layer_input, pre_grad, (((0,), (0,)), ((), ())), preferre...]
    gather x4 -> x0, local copies, waits for them, and re-layouts: 40.2 us -> none  [arrange(): return grad.reshape(-1, rows, grad.shape[1])[order]]
    another operation x4 -> x0, local copies, waits for them, and re-layouts: 23 us -> none  [the longest x2 17.7 us: products(): return jnp.stack([jnp.sum(term) for term in terms])]
    unnamed x12 -> x62, local copies, waits for them, and re-layouts: 0.03 us -> 18 us
    ppermute x32 -> x34, waiting for transfers between devices: 73.6 us -> 89.2 us  [inner_permute(): return lax.ppermute(block, 'inner', route)]
    reduce_sum x3 -> x0, other arithmetic: 8.92 us -> none  [the longest x2 8.05 us: products(): return jnp.stack([jnp.sum(term) for term in terms])]
    add x20 -> x23, other arithmetic: 29.8 us -> 21.1 us  [the longest x3 6.07 us: reduce_group(): once = ring_reduce(lambda k, h: keep[k, h] + other[k, h], 0)]
  transfers between devices with their start and end apart: 38 -> 43, of which waited for: 14 -> 21; matrix products, arithmetic and copies ran while one was open for 34% -> 8% of each run, Pallas kernels for 0% -> 1%
where the time goes in v2:
time: 287 us
  waiting for transfers between devices  116 us (40%)
  Pallas kernels  67.2 us (23%)
  starting transfers between devices  60.7 us (21%)
  other arithmetic  23.7 us (8%)
  local copies, waits for them, and re-layouts  18.2 us (6%)
    ppermute x34, waiting for transfers between devices, inner_permute(): return lax.ppermute(block, 'inner', route)  89.2 us
    ppermute x34, starting transfers between devices, inner_permute(): return lax.ppermute(block, 'inner', route)  46.4 us
    pallas_call x2, Pallas kernels, up_call(): pl.pallas_call(up_kernel, grid_spec=pltpu.PrefetchScalarGridSpec(num_scal...  42.2 us
    ppermute x9, waiting for transfers between devices, across_replicas(): lax.ppermute(block, 'rep', [(i, (i - step) % count) for i in range(count)])  26.4 us
    pallas_call x1, Pallas kernels, down_call(): pl.pallas_call(down_kernel, grid_spec=pltpu.PrefetchScalarGridSpec(num_sc...  18.3 us
    unnamed x62, local copies, waits for them, and re-layouts  18 us
    ppermute x9, starting transfers between devices, across_replicas(): lax.ppermute(block, 'rep', [(i, (i - step) % count) for i in range(count)])  14.4 us
    add x3, other arithmetic, reduce_group(): once = ring_reduce(lambda k, h: keep[k, h] + other[k, h], 0)  6.07 us
  transfers between devices with their start and end apart: 43, of which 21 were waited for; matrix products, arithmetic and copies ran while one was open for 8% of the time, Pallas kernels for 1%

profile of v2, /device:TPU:0, one launch (start us, length us, event | category | flops | bytes accessed | tf_op | source)
XLA Modules:
  0.0 286.7 jit_solution(1307967365624223052)
XLA Ops:
  4.7 21.1 %up_partial.3 = (f32[512,2048]{1,0:T(8,128)S(1)}, f32[512,2048]{1,0:T(8,128)S(1)}, bf16[1024,2048]{1,0:T(8,128)(2,1)}) custom-call(s32[64]{0:T(128)S(1)} %mul.69.rows_ref, s32[8]{0:T(128)S(1)} %copy-done.12, bf16[1024,1024]{1,0:T(8,128)(2,1)S(1)} %copy-done.9, bf16[1024,1024]{1,0:T(8,128)(2,1)S(1)} %copy-done.10, bf16[1024,4096]{1,0:T(8,128)(2,1)} %pre_ref.3, ...), custom_call_target="tpu_custom_call" | custom-call | flops 8589934592 | bytes 25165824 | tf_op jit(solution)/shard_map/up_partial/pallas_call | solution.py:144
  30.0 21.1 %up_partial.2 = (f32[512,2048]{1,0:T(8,128)S(1)}, f32[512,2048]{1,0:T(8,128)S(1)}, bf16[1024,2048]{1,0:T(8,128)(2,1)}) custom-call(s32[64]{0:T(128)S(1)} %mul.69.rows_ref, s32[8]{0:T(128)S(1)} %copy-done.12, bf16[1024,1024]{1,0:T(8,128)(2,1)S(1)} %copy-done.9, bf16[1024,1024]{1,0:T(8,128)(2,1)S(1)} %copy-done.10, bf16[1024,4096]{1,0:T(8,128)(2,1)} %pre_ref.3, ...), custom_call_target="tpu_custom_call" | custom-call | flops 8589934592 | bytes 25165824 | tf_op jit(solution)/shard_map/up_partial/pallas_call | solution.py:144
  59.5 18.3 %down_partial.1 = (f32[4,2,4,64,1024]{4,3,2,1,0:T(8,128)}, f32[4,2,4,64,1024]{4,3,2,1,0:T(8,128)}) custom-call(s32[32]{0:T(128)S(1)} %reshape.750.blocks_ref, s32[8]{0:T(128)S(1)} %copy-done.13, bf16[1024,1024]{1,0:T(8,128)(2,1)S(1)} %copy-done.11, bf16[1024,2048]{1,0:T(8,128)(2,1)S(1)} %copy-done.15, bf16[1024,2048]{1,0:T(8,128)(2,1)S(1)} %copy-done.14, ...), custom_call_target="tpu_custom_call" | custom-call | flops 8589934592 | bytes 27262976 | tf_op jit(solution)/shard_map/down_partial/pallas_call | solution.py:232
  78.3 24.8 %collective-permute-done.12 = f32[4,2,4,16,2048]{4,3,2,1,0:T(8,128)S(1)} collective-permute-done((f32[4,2,4,16,2048]{4,3,2,1,0:T(8,128)}, f32[4,2,4,16,2048]{4,3,2,1,0:T(8,128)S(1)}, u32[]{:S(2)}, u32[]{:S(2)}) %collective-permute-start.12) | collective-permute-done | bytes 4194336 | tf_op jit(solution)/shard_map/ppermute | solution.py:54
  104.7 3.3 %collective-permute-start.13 = (f32[2,4,16,2048]{3,2,1,0:T(8,128)S(1)}, f32[2,4,16,2048]{3,2,1,0:T(8,128)}, u32[]{:S(2)}, u32[]{:S(2)}) collective-permute-start(f32[2,4,16,2048]{3,2,1,0:T(8,128)S(1)} %pad_maximum_fusion.4), channel_id=1, source_target_pairs={{0,96},{4,28},{8,104},{12,4},{16,112},{20,12},{24,120},{28,20},{32... | collective-permute-start | bytes 3145736 | tf_op jit(solution)/shard_map/ppermute | solution.py:54
  109.9 3.3 %collective-permute-start.1 = (f32[2,4,16,2048]{3,2,1,0:T(8,128)S(1)}, f32[2,4,16,2048]{3,2,1,0:T(8,128)S(1)}, u32[]{:S(2)}, u32[]{:S(2)}) collective-permute-start(f32[2,4,16,2048]{3,2,1,0:T(8,128)S(1)} %pad_maximum_fusion.2), channel_id=1, source_target_pairs={{0,96},{4,28},{8,104},{12,4},{16,112},{20,12},{24,120},{28,20},{32... | collective-permute-start | bytes 3145736 | tf_op jit(solution)/shard_map/ppermute | solution.py:54
  113.5 6.8 %collective-permute-done.13 = f32[2,4,16,2048]{3,2,1,0:T(8,128)} collective-permute-done((f32[2,4,16,2048]{3,2,1,0:T(8,128)S(1)}, f32[2,4,16,2048]{3,2,1,0:T(8,128)}, u32[]{:S(2)}, u32[]{:S(2)}) %collective-permute-start.13) | collective-permute-done | bytes 1048608 | tf_op jit(solution)/shard_map/ppermute | solution.py:54
  120.3 3.9 %collective-permute-done.14 = f32[2,4,16,2048]{3,2,1,0:T(8,128)} collective-permute-done((f32[2,4,16,2048]{3,2,1,0:T(8,128)S(1)}, f32[2,4,16,2048]{3,2,1,0:T(8,128)}, u32[]{:S(2)}, u32[]{:S(2)}) %collective-permute-start.14) | collective-permute-done | bytes 1048608 | tf_op jit(solution)/shard_map/ppermute | solution.py:54
  128.5 3.1 %collective-permute-done.1 = f32[2,4,16,2048]{3,2,1,0:T(8,128)S(1)} collective-permute-done((f32[2,4,16,2048]{3,2,1,0:T(8,128)S(1)}, f32[2,4,16,2048]{3,2,1,0:T(8,128)S(1)}, u32[]{:S(2)}, u32[]{:S(2)}) %collective-permute-start.1) | collective-permute-done | bytes 1048608 | tf_op jit(solution)/shard_map/ppermute | solution.py:54
  131.6 3.8 %collective-permute-done.2 = f32[2,4,16,2048]{3,2,1,0:T(8,128)S(1)} collective-permute-done((f32[2,4,16,2048]{3,2,1,0:T(8,128)S(1)}, f32[2,4,16,2048]{3,2,1,0:T(8,128)S(1)}, u32[]{:S(2)}, u32[]{:S(2)}) %collective-permute-start.2) | collective-permute-done | bytes 1048608 | tf_op jit(solution)/shard_map/ppermute | solution.py:54
  140.0 3.0 %slice_add_fusion.1 = (f32[1,1,4,64,1024]{4,3,2,1,0:T(8,128)}, f32[1,4,64,1024]{3,2,1,0:T(8,128)S(1)}, f32[1,4,64,1024]{3,2,1,0:T(8,128)}, f32[1,4,64,1024]{3,2,...) fusion(f32[4,2,4,64,1024]{4,3,2,1,0:T(8,128)S(1)} %collective-permute-done.24, ...), kind=kLoop, calls=%fused_computation.6 | loop fusion | flops 1572864 | bytes 18874368 | tf_op jit(solution)/shard_map/add | solution.py:71
  148.6 4.2 %collective-permute-start.17 = (f32[2,16,2048]{2,1,0:T(8,128)S(1)}, f32[2,16,2048]{2,1,0:T(8,128)S(1)}, u32[]{:S(2)}, u32[]{:S(2)}) collective-permute-start(f32[2,16,2048]{2,1,0:T(8,128)S(1)} %pad_maximum_fusion.12), channel_id=1, source_target_pairs={{0,24},{4,100},{8,0},{12,108},{16,8},{20,116},{24,16},{28,124},{32... | collective-permute-start | bytes 786440 | tf_op jit(solution)/shard_map/ppermute | solution.py:54
  155.0 3.3 %collective-permute-start.5 = (f32[2,16,2048]{2,1,0:T(8,128)S(1)}, f32[2,16,2048]{2,1,0:T(8,128)S(1)}, u32[]{:S(2)}, u32[]{:S(2)}) collective-permute-start(f32[2,16,2048]{2,1,0:T(8,128)S(1)} %pad_maximum_fusion.9), channel_id=1, source_target_pairs={{0,24},{4,100},{8,0},{12,108},{16,8},{20,116},{24,16},{28,124},{32... | collective-permute-start | bytes 786440 | tf_op jit(solution)/shard_map/ppermute | solution.py:54
  158.3 18.2 %collective-permute-done.25 = f32[2,4,64,1024]{3,2,1,0:T(8,128)S(1)} collective-permute-done((f32[2,4,64,1024]{3,2,1,0:T(8,128)S(1)}, f32[2,4,64,1024]{3,2,1,0:T(8,128)S(1)}, u32[]{:S(2)}, u32[]{:S(2)}) %collective-permute-start.25) | collective-permute-done | bytes 2097184 | tf_op jit(solution)/shard_map/ppermute | solution.py:54
  179.0 3.7 %collective-permute-start.28 = (f32[4,64,1024]{2,1,0:T(8,128)S(1)}, f32[4,64,1024]{2,1,0:T(8,128)S(1)}, u32[]{:S(2)}, u32[]{:S(2)}) collective-permute-start(f32[4,64,1024]{2,1,0:T(8,128)S(1)} %get-tuple-element.24), channel_id=1, source_target_pairs={{0,96},{4,28},{8,104},{12,4},{16,112},{20,12},{24,120},{28,20},{32... | collective-permute-start | bytes 3145736 | tf_op jit(solution)/shard_map/ppermute | solution.py:54
  188.3 3.1 %collective-permute-done.19 = f32[16,2048]{1,0:T(8,128)S(1)} collective-permute-done((f32[16,2048]{1,0:T(8,128)S(1)}, f32[16,2048]{1,0:T(8,128)S(1)}, u32[]{:S(2)}, u32[]{:S(2)}) %collective-permute-start.19) | collective-permute-done | bytes 131104 | tf_op jit(solution)/shard_map/ppermute | solution.py:54
  193.4 3.0 %collective-permute-done.28 = f32[4,64,1024]{2,1,0:T(8,128)S(1)} collective-permute-done((f32[4,64,1024]{2,1,0:T(8,128)S(1)}, f32[4,64,1024]{2,1,0:T(8,128)S(1)}, u32[]{:S(2)}, u32[]{:S(2)}) %collective-permute-start.28) | collective-permute-done | bytes 1048608 | tf_op jit(solution)/shard_map/ppermute | solution.py:54
  196.5 5.2 %collective-permute-done.27 = f32[4,64,1024]{2,1,0:T(8,128)S(1)} collective-permute-done((f32[4,64,1024]{2,1,0:T(8,128)S(1)}, f32[4,64,1024]{2,1,0:T(8,128)S(1)}, u32[]{:S(2)}, u32[]{:S(2)}) %collective-permute-start.27) | collective-permute-done | bytes 1048608 | tf_op jit(solution)/shard_map/ppermute | solution.py:54
  206.9 5.4 %collective-permute-done.30 = f32[2,64,1024]{2,1,0:T(8,128)S(1)} collective-permute-done((f32[2,64,1024]{2,1,0:T(8,128)S(1)}, f32[2,64,1024]{2,1,0:T(8,128)S(1)}, u32[]{:S(2)}, u32[]{:S(2)}) %collective-permute-start.30) | collective-permute-done | bytes 524320 | tf_op jit(solution)/shard_map/ppermute | solution.py:54
  228.3 2.8 collective-permute-start.34
  237.8 23.9 %collective-permute-done.10.refs_2_ = f32[32,2048]{1,0:T(8,128)} collective-permute-done((f32[32,2048]{1,0:T(8,128)S(1)}, f32[32,2048]{1,0:T(8,128)}, u32[]{:S(2)}, u32[]{:S(2)}) %collective-permute-start.10) | collective-permute-done | bytes 262176 | tf_op jit(solution)/shard_map/ppermute | solution.py:257
  266.8 3.3 %collective-permute-start.39 = (f32[2,16,128]{2,1,0:T(8,128)S(1)}, f32[2,16,128]{2,1,0:T(8,128)S(1)}, u32[]{:S(2)}, u32[]{:S(2)}) collective-permute-start(f32[2,16,128]{2,1,0:T(8,128)S(1)} %fusion.90), channel_id=1, source_target_pairs={{0,96},{4,100},{8,104},{12,108},{16,112},{20,116},{24,120},{28,124... | collective-permute-start | bytes 49160 | tf_op jit(solution)/shard_map/ppermute | solution.py:54
  271.7 3.6 %collective-permute-done.37 = f32[2,16,128]{2,1,0:T(8,128)S(1)} collective-permute-done((f32[2,16,128]{2,1,0:T(8,128)S(1)}, f32[2,16,128]{2,1,0:T(8,128)S(1)}, u32[]{:S(2)}, u32[]{:S(2)}) %collective-permute-start.37) | collective-permute-done | bytes 16416 | tf_op jit(solution)/shard_map/ppermute | solution.py:54
  279.1 3.0 %collective-permute-done.41 = f32[2,16,128]{2,1,0:T(8,128)S(1)} collective-permute-done((f32[2,16,128]{2,1,0:T(8,128)S(1)}, f32[2,16,128]{2,1,0:T(8,128)S(1)}, u32[]{:S(2)}, u32[]{:S(2)}) %collective-permute-start.41) | collective-permute-done | bytes 16416 | tf_op jit(solution)/shard_map/ppermute | solution.py:54
  (179 shorter events, 90.3 us)
Async XLA Ops:
  77.8 62.2 %collective-permute-start.24 = (f32[4,2,4,64,1024]{4,3,2,1,0:T(8,128)}, f32[4,2,4,64,1024]{4,3,2,1,0:T(8,128)S(1)}, u32[]{:S(2)}, u32[]{:S(2)}) collective-permute-start(f32[4,2,4,64,1024]{4,3,2,1,0:T(8,128)} %get-tuple-element.17), channel_id=1, source_target_pairs={{0,4},{4,0},{8,12},{12,8},{16,20},{20,16},{24,28},{28,24},{32,36},... | collective-permute-start | bytes 25165832 | tf_op jit(solution)/shard_map/ppermute | solution.py:54
  77.8 25.4 %collective-permute-start.12 = (f32[4,2,4,16,2048]{4,3,2,1,0:T(8,128)}, f32[4,2,4,16,2048]{4,3,2,1,0:T(8,128)S(1)}, u32[]{:S(2)}, u32[]{:S(2)}) collective-permute-start(f32[4,2,4,16,2048]{4,3,2,1,0:T(8,128)} %bitcast.466), channel_id=1, source_target_pairs={{0,4},{4,0},{8,12},{12,8},{16,20},{20,16},{24,28},{28,24},{32,36},... | collective-permute-start | bytes 12582920 | tf_op jit(solution)/shard_map/ppermute | solution.py:54
  78.3 29.9 %collective-permute-start = (f32[4,2,4,16,2048]{4,3,2,1,0:T(8,128)S(1)}, f32[4,2,4,16,2048]{4,3,2,1,0:T(8,128)S(1)}, u32[]{:S(2)}, u32[]{:S(2)}) collective-permute-start(f32[4,2,4,16,2048]{4,3,2,1,0:T(8,128)S(1)} %bitcast.465), channel_id=1, source_target_pairs={{0,4},{4,0},{8,12},{12,8},{16,20},{20,16},{24,28},{28,24},{32,36},... | collective-permute-start | bytes 12582920 | tf_op jit(solution)/shard_map/ppermute | solution.py:54
  108.1 16.2 %collective-permute-start.14 = (f32[2,4,16,2048]{3,2,1,0:T(8,128)S(1)}, f32[2,4,16,2048]{3,2,1,0:T(8,128)}, u32[]{:S(2)}, u32[]{:S(2)}) collective-permute-start(f32[2,4,16,2048]{3,2,1,0:T(8,128)S(1)} %pad_maximum_fusion.5), channel_id=1, source_target_pairs={{0,32},{4,12},{8,40},{12,20},{16,48},{20,28},{24,56},{28,4},{32,64... | collective-permute-start | bytes 3145736 | tf_op jit(solution)/shard_map/ppermute | solution.py:54
  109.9 21.7 %collective-permute-start.1 = (f32[2,4,16,2048]{3,2,1,0:T(8,128)S(1)}, f32[2,4,16,2048]{3,2,1,0:T(8,128)S(1)}, u32[]{:S(2)}, u32[]{:S(2)}) collective-permute-start(f32[2,4,16,2048]{3,2,1,0:T(8,128)S(1)} %pad_maximum_fusion.2), channel_id=1, source_target_pairs={{0,96},{4,28},{8,104},{12,4},{16,112},{20,12},{24,120},{28,20},{32... | collective-permute-start | bytes 3145736 | tf_op jit(solution)/shard_map/ppermute | solution.py:54
  113.2 22.2 %collective-permute-start.2 = (f32[2,4,16,2048]{3,2,1,0:T(8,128)S(1)}, f32[2,4,16,2048]{3,2,1,0:T(8,128)S(1)}, u32[]{:S(2)}, u32[]{:S(2)}) collective-permute-start(f32[2,4,16,2048]{3,2,1,0:T(8,128)S(1)} %pad_maximum_fusion.3), channel_id=1, source_target_pairs={{0,32},{4,12},{8,40},{12,20},{16,48},{20,28},{24,56},{28,4},{32,64... | collective-permute-start | bytes 3145736 | tf_op jit(solution)/shard_map/ppermute | solution.py:54
  126.5 20.9 %collective-permute-start.15 = (f32[4,16,2048]{2,1,0:T(8,128)}, f32[4,16,2048]{2,1,0:T(8,128)}, u32[]{:S(2)}, u32[]{:S(2)}) collective-permute-start(f32[4,16,2048]{2,1,0:T(8,128)} %get-tuple-element.33), channel_id=1, source_target_pairs={{0,32},{4,12},{8,40},{12,20},{16,48},{20,28},{24,56},{28,4},{32,64... | collective-permute-start | bytes 1572872 | tf_op jit(solution)/shard_map/ppermute | solution.py:54
  136.7 16.1 %collective-permute-start.4 = (f32[4,16,2048]{2,1,0:T(8,128)}, f32[4,16,2048]{2,1,0:T(8,128)}, u32[]{:S(2)}, u32[]{:S(2)}) collective-permute-start(f32[4,16,2048]{2,1,0:T(8,128)} %get-tuple-element.40), channel_id=1, source_target_pairs={{0,96},{4,28},{8,104},{12,4},{16,112},{20,12},{24,120},{28,20},{32... | collective-permute-start | bytes 1572872 | tf_op jit(solution)/shard_map/ppermute | solution.py:54
  136.7 17.2 %collective-permute-start.3 = (f32[4,16,2048]{2,1,0:T(8,128)}, f32[4,16,2048]{2,1,0:T(8,128)}, u32[]{:S(2)}, u32[]{:S(2)}) collective-permute-start(f32[4,16,2048]{2,1,0:T(8,128)} %get-tuple-element.41), channel_id=1, source_target_pairs={{0,32},{4,12},{8,40},{12,20},{16,48},{20,28},{24,56},{28,4},{32,64... | collective-permute-start | bytes 1572872 | tf_op jit(solution)/shard_map/ppermute | solution.py:54
  144.8 31.7 %collective-permute-start.25 = (f32[2,4,64,1024]{3,2,1,0:T(8,128)S(1)}, f32[2,4,64,1024]{3,2,1,0:T(8,128)S(1)}, u32[]{:S(2)}, u32[]{:S(2)}) collective-permute-start(f32[2,4,64,1024]{3,2,1,0:T(8,128)S(1)} %pad_maximum_fusion), channel_id=1, source_target_pairs={{0,96},{4,28},{8,104},{12,4},{16,112},{20,12},{24,120},{28,20},{32... | collective-permute-start | bytes 6291464 | tf_op jit(solution)/shard_map/ppermute | solution.py:54
  147.3 31.0 %collective-permute-start.26 = (f32[2,4,64,1024]{3,2,1,0:T(8,128)S(1)}, f32[2,4,64,1024]{3,2,1,0:T(8,128)S(1)}, u32[]{:S(2)}, u32[]{:S(2)}) collective-permute-start(f32[2,4,64,1024]{3,2,1,0:T(8,128)S(1)} %pad_maximum_fusion.1), channel_id=1, source_target_pairs={{0,32},{4,12},{8,40},{12,20},{16,48},{20,28},{24,56},{28,4},{32,64... | collective-permute-start | bytes 6291464 | tf_op jit(solution)/shard_map/ppermute | solution.py:54
  148.6 38.0 %collective-permute-start.17 = (f32[2,16,2048]{2,1,0:T(8,128)S(1)}, f32[2,16,2048]{2,1,0:T(8,128)S(1)}, u32[]{:S(2)}, u32[]{:S(2)}) collective-permute-start(f32[2,16,2048]{2,1,0:T(8,128)S(1)} %pad_maximum_fusion.12), channel_id=1, source_target_pairs={{0,24},{4,100},{8,0},{12,108},{16,8},{20,116},{24,16},{28,124},{32... | collective-permute-start | bytes 786440 | tf_op jit(solution)/shard_map/ppermute | solution.py:54
  152.8 29.9 %collective-permute-start.18 = (f32[2,16,2048]{2,1,0:T(8,128)S(1)}, f32[2,16,2048]{2,1,0:T(8,128)S(1)}, u32[]{:S(2)}, u32[]{:S(2)}) collective-permute-start(f32[2,16,2048]{2,1,0:T(8,128)S(1)} %pad_maximum_fusion.13), channel_id=1, source_target_pairs={{0,8},{4,36},{8,16},{12,44},{16,24},{20,52},{24,0},{28,60},{32,40}... | collective-permute-start | bytes 786440 | tf_op jit(solution)/shard_map/ppermute | solution.py:54
  155.0 48.5 %collective-permute-start.5 = (f32[2,16,2048]{2,1,0:T(8,128)S(1)}, f32[2,16,2048]{2,1,0:T(8,128)S(1)}, u32[]{:S(2)}, u32[]{:S(2)}) collective-permute-start(f32[2,16,2048]{2,1,0:T(8,128)S(1)} %pad_maximum_fusion.9), channel_id=1, source_target_pairs={{0,24},{4,100},{8,0},{12,108},{16,8},{20,116},{24,16},{28,124},{32... | collective-permute-start | bytes 786440 | tf_op jit(solution)/shard_map/ppermute | solution.py:54
  179.0 17.4 %collective-permute-start.28 = (f32[4,64,1024]{2,1,0:T(8,128)S(1)}, f32[4,64,1024]{2,1,0:T(8,128)S(1)}, u32[]{:S(2)}, u32[]{:S(2)}) collective-permute-start(f32[4,64,1024]{2,1,0:T(8,128)S(1)} %get-tuple-element.24), channel_id=1, source_target_pairs={{0,96},{4,28},{8,104},{12,4},{16,112},{20,12},{24,120},{28,20},{32... | collective-permute-start | bytes 3145736 | tf_op jit(solution)/shard_map/ppermute | solution.py:54
  185.7 16.0 %collective-permute-start.27 = (f32[4,64,1024]{2,1,0:T(8,128)S(1)}, f32[4,64,1024]{2,1,0:T(8,128)S(1)}, u32[]{:S(2)}, u32[]{:S(2)}) collective-permute-start(f32[4,64,1024]{2,1,0:T(8,128)S(1)} %get-tuple-element.25), channel_id=1, source_target_pairs={{0,32},{4,12},{8,40},{12,20},{16,48},{20,28},{24,56},{28,4},{32,64... | collective-permute-start | bytes 3145736 | tf_op jit(solution)/shard_map/ppermute | solution.py:54
  186.6 16.9 %collective-permute-start.7 = (f32[16,2048]{1,0:T(8,128)S(1)}, f32[16,2048]{1,0:T(8,128)S(1)}, u32[]{:S(2)}, u32[]{:S(2)}) collective-permute-start(f32[16,2048]{1,0:T(8,128)S(1)} %fusion.67), channel_id=1, source_target_pairs={{0,8},{4,36},{8,16},{12,44},{16,24},{20,52},{24,0},{28,60},{32,40}... | collective-permute-start | bytes 393224 | tf_op jit(solution)/shard_map/ppermute | solution.py:54
  192.5 20.3 %collective-permute-start.20 = (f32[16,2048]{1,0:T(8,128)S(1)}, f32[16,2048]{1,0:T(8,128)S(1)}, u32[]{:S(2)}, u32[]{:S(2)}) collective-permute-start(f32[16,2048]{1,0:T(8,128)S(1)} %get-tuple-element.57), channel_id=1, source_target_pairs={{0,24},{4,100},{8,0},{12,108},{16,8},{20,116},{24,16},{28,124},{32... | collective-permute-start | bytes 393224 | tf_op jit(solution)/shard_map/ppermute | solution.py:54
  204.6 18.1 %collective-permute-start.8 = (f32[16,2048]{1,0:T(8,128)S(1)}, f32[16,2048]{1,0:T(8,128)S(1)}, u32[]{:S(2)}, u32[]{:S(2)}) collective-permute-start(f32[16,2048]{1,0:T(8,128)S(1)} %get-tuple-element.59), channel_id=1, source_target_pairs={{0,24},{4,100},{8,0},{12,108},{16,8},{20,116},{24,16},{28,124},{32... | collective-permute-start | bytes 393224 | tf_op jit(solution)/shard_map/ppermute | solution.py:54
  226.8 37.8 %collective-permute-start.35 = (f32[128,1024]{1,0:T(8,128)S(1)}, f32[128,1024]{1,0:T(8,128)S(1)}, u32[]{:S(2)}, u32[]{:S(2)}) collective-permute-start(f32[128,1024]{1,0:T(8,128)S(1)} %pad_maximum_fusion.8.refs_0_), channel_id=1, source_target_pairs={{0,1},{1,2},{2,3},{3,0},{4,5},{5,6},{6,7},{7,4},{8,9},{9,10},{10,1... | collective-permute-start | bytes 1572872 | tf_op jit(solution)/shard_map/ppermute | solution.py:257
  228.3 36.3 %collective-permute-start.34 = (f32[128,1024]{1,0:T(8,128)S(1)}, f32[128,1024]{1,0:T(8,128)S(1)}, u32[]{:S(2)}, u32[]{:S(2)}) collective-permute-start(f32[128,1024]{1,0:T(8,128)S(1)} %pad_maximum_fusion.8.refs_0_), channel_id=1, source_target_pairs={{0,2},{1,3},{2,0},{3,1},{4,6},{5,7},{6,4},{7,5},{8,10},{9,11},{10,... | collective-permute-start | bytes 1572872 | tf_op jit(solution)/shard_map/ppermute | solution.py:257
  231.1 33.5 %collective-permute-start.33 = (f32[128,1024]{1,0:T(8,128)S(1)}, f32[128,1024]{1,0:T(8,128)S(1)}, u32[]{:S(2)}, u32[]{:S(2)}) collective-permute-start(f32[128,1024]{1,0:T(8,128)S(1)} %pad_maximum_fusion.8.refs_0_), channel_id=1, source_target_pairs={{0,3},{1,0},{2,1},{3,2},{4,7},{5,4},{6,5},{7,6},{8,11},{9,8},{10,9... | collective-permute-start | bytes 1572872 | tf_op jit(solution)/shard_map/ppermute | solution.py:257
  232.5 29.3 %collective-permute-start.10 = (f32[32,2048]{1,0:T(8,128)S(1)}, f32[32,2048]{1,0:T(8,128)}, u32[]{:S(2)}, u32[]{:S(2)}) collective-permute-start(f32[32,2048]{1,0:T(8,128)S(1)} %pad_maximum_fusion.11.refs_0_), channel_id=1, source_target_pairs={{0,2},{1,3},{2,0},{3,1},{4,6},{5,7},{6,4},{7,5},{8,10},{9,11},{10,... | collective-permute-start | bytes 786440 | tf_op jit(solution)/shard_map/ppermute | solution.py:257
  236.1 25.8 %collective-permute-start.9 = (f32[32,2048]{1,0:T(8,128)S(1)}, f32[32,2048]{1,0:T(8,128)}, u32[]{:S(2)}, u32[]{:S(2)}) collective-permute-start(f32[32,2048]{1,0:T(8,128)S(1)} %pad_maximum_fusion.11.refs_0_), channel_id=1, source_target_pairs={{0,3},{1,0},{2,1},{3,2},{4,7},{5,4},{6,5},{7,6},{8,11},{9,8},{10,9... | collective-permute-start | bytes 786440 | tf_op jit(solution)/shard_map/ppermute | solution.py:257
  (50 other events, 556.1 us)

commit v3 on v1

v3 whole, which is shorter than its diff:
```python
import functools
import math

import jax
import jax.numpy as jnp
from jax import lax
from jax.experimental import pallas as pl
from jax.experimental.pallas import tpu as pltpu
from jax.sharding import PartitionSpec as P

SEQ = 128
RING = 4
CORES = 2
CHIPS = RING * RING
HALVES = 2
LANES = 128
FF_BLOCK = 512
MIB = 1024 * 1024

EPSILON = 1e-06
SQRT_HALF = 0.7071067811865476
INV_ROOT_TWO_PI = 0.3989422804014327
EXP2_SCALE = -0.5 / math.log(2.0)
TERMS = 14
TERM_ROWS = 16


def device_of(y, z, core):
    return (y % RING * RING + z % RING) * CORES + core


def inner_route(move):
    route = []
    for y in range(RING):
        for z in range(RING):
            for core in range(CORES):
                route.append((device_of(y, z, core), device_of(*move(y, z, core))))
    return route


def ring_route(stage, step):
    return inner_route(
        lambda y, z, core: (y + step, z, core) if core == stage else (y, z + step, core)
    )


def core_route():
    return inner_route(lambda y, z, core: (y, z, 1 - core))


def inner_permute(block, route):
    return lax.ppermute(block, "inner", route)


def ring_start(piece, stage):
    return (
        inner_permute(jnp.stack([piece(2, 0), piece(1, 1)]), ring_route(stage, 1)),
        inner_permute(jnp.stack([piece(2, 1), piece(3, 0)]), ring_route(stage, -1)),
    )


def ring_pass(piece, stage, received):
    from_behind, from_ahead = received
    return (
        inner_permute(piece(1, 0) + from_behind[0], ring_route(stage, 1)),
        inner_permute(piece(3, 1) + from_ahead[0], ring_route(stage, -1)),
    )


def ring_end(piece, received, passed):
    from_behind, from_ahead = received
    return (
        lambda at: piece(0, 0)[at] + from_ahead[1][at] + passed[0][at],
        lambda at: piece(0, 1)[at] + from_behind[1][at] + passed[1][at],
    )


def once_reduced(halves):
    return lambda l, h: halves[h](l)


def joined(halves):
    return jnp.concatenate([half(...) for half in halves], axis=-2)


def direct(halves):
    return [
        inner_permute(jnp.stack([half(step) for half in halves]), ring_route(1, step))
        for step in range(1, RING)
    ]


def direct_end(halves, received):
    one, two, three = received
    return jnp.concatenate(
        [(half(0) + two[h]) + (one[h] + three[h]) for h, half in enumerate(halves)], axis=-2
    )


def core_sum(keep, other):
    return lambda k, h: keep[k, h] + other[k, h]


def gate(arrived, earlier=()):
    return lax.optimization_barrier((arrived, earlier))[0]


def destination_table():
    inner = lax.axis_index("inner")
    y, z, core = inner // (RING * CORES), inner // CORES % RING, inner % CORES
    k = lax.iota(jnp.int32, RING)[:, None]
    l = lax.iota(jnp.int32, RING)[None, :]

    def order(core_to):
        to_y = jnp.where(core_to == 0, y + k, y + l) % RING
        to_z = jnp.where(core_to == 0, z + l, z + k) % RING
        return (to_y * RING + to_z) * CORES + core_to

    return jnp.stack([order(core), order(1 - core)])


def write_masked(lengths_ref, cotangent_ref, masked_ref):
    columns = cotangent_ref.shape[1]
    for seq in range(cotangent_ref.shape[0] // SEQ):
        rows = slice(seq * SEQ, (seq + 1) * SEQ)
        valid = lax.broadcasted_iota(jnp.int32, (SEQ, columns), 0) < lengths_ref[seq]
        values = cotangent_ref[rows, :].astype(jnp.float32)
        masked_ref[rows, :] = jnp.where(valid, values, 0.0).astype(masked_ref.dtype)


def prepare(rows_ref, lengths_ref, x_ref, cotangent_ref, ordered_ref, masked_ref, turned_ref):
    strip = x_ref.shape[1] // (CHIPS * CORES * HALVES)
    write_masked(lengths_ref, cotangent_ref, masked_ref)
    turned_ref[...] = x_ref[...].T
    for index in range(x_ref.shape[1] // strip):
        start = pl.multiple_of(rows_ref[index], strip)
        ordered_ref[index * strip:(index + 1) * strip, :] = turned_ref[pl.ds(start, strip), :]


def down_blocks(pre_refs, masked_ref, keep_ref, send_ref):
    rows = pre_refs[0].shape[1]
    for first in range(0, len(pre_refs), 2):
        columns = []
        for ref in pre_refs[first:first + 2]:
            value = ref[...].astype(jnp.float32)
            cdf = 0.5 + 0.5 * lax.erf(value * SQRT_HALF)
            columns.append((value * cdf).astype(jnp.bfloat16))
        product = lax.dot_general(
            jnp.concatenate(columns, axis=1), masked_ref[...], (((0,), (0,)), ((), ())),
            preferred_element_type=jnp.float32,
        )
        for index in range(2):
            which, place = divmod(first + index, len(pre_refs) // 2)
            out_ref = (keep_ref, send_ref)[which]
            part = product[index * rows:(index + 1) * rows]
            out_ref[0, :, place, :, :] = part.reshape(HALVES, rows // HALVES, part.shape[1])


def first_down_kernel(blocks_ref, rows_ref, lengths_ref, x_ref, cotangent_ref, *refs):
    pre_refs, (keep_ref, send_ref, ordered_ref, masked_ref, turned_ref) = refs[:-5], refs[-5:]

    @pl.when(pl.program_id(0) == 0)
    def _():
        prepare(rows_ref, lengths_ref, x_ref, cotangent_ref, ordered_ref, masked_ref, turned_ref)

    down_blocks(pre_refs, masked_ref, keep_ref, send_ref)


def down_kernel(blocks_ref, masked_ref, *refs):
    down_blocks(refs[:-2], masked_ref, *refs[-2:])


def down_call(table, pre_act, places, lengths=None, x=None, cotangent=None, masked=None):
    is_first = masked is None
    tokens, width = (cotangent if is_first else masked).shape
    rows = pre_act.shape[1] // (CHIPS * CORES)
    strip = width // (CHIPS * CORES * HALVES)

    def pre_spec(which, place):
        return pl.BlockSpec(
            (tokens, rows), lambda k, blocks_ref, *_: (0, blocks_ref[which * CHIPS + k * RING + place])
        )

    whole = pl.BlockSpec((tokens, width), lambda k, *_: (0, 0))
    turned = pl.BlockSpec((width, tokens), lambda k, *_: (0, 0))
    out_block = pl.BlockSpec(
        (1, HALVES, len(places), rows // HALVES, width), lambda k, *_: (k, 0, 0, 0, 0)
    )
    out_shape = [
        jax.ShapeDtypeStruct((RING, HALVES, len(places), rows // HALVES, width), jnp.float32)
    ] * 2
    prefetch, wholes, scratch, extra = [table.reshape(-1)], [masked], [], []
    if is_first:
        half = lax.iota(jnp.int32, HALVES)[None, None, :, None]
        strips = (table[:, :, None, :] * HALVES + half).reshape(-1) * strip
        prefetch, wholes = prefetch + [strips, lengths], [x, cotangent]
        scratch, extra = [pltpu.VMEM((width, tokens), jnp.bfloat16)], [turned, whole]
        out_shape = out_shape + [
            jax.ShapeDtypeStruct((width, tokens), jnp.bfloat16),
            jax.ShapeDtypeStruct((tokens, width), jnp.bfloat16),
        ]
    count = 2 * len(places)
    return pl.pallas_call(
        first_down_kernel if is_first else down_kernel,
        grid_spec=pltpu.PrefetchScalarGridSpec(
            num_scalar_prefetch=len(prefetch),
            grid=(RING,),
            in_specs=[whole] * len(wholes)
            + [pre_spec(which, place) for which in range(2) for place in places],
            out_specs=[out_block, out_block] + extra,
            scratch_shapes=scratch,
        ),
        out_shape=out_shape,
        compiler_params=pltpu.CompilerParams(vmem_limit_bytes=60 * MIB),
        cost_estimate=pl.CostEstimate(
            flops=2 * tokens * width * rows * RING * count,
            bytes_accessed=4 * tokens * width + (2 * tokens + 4 * width) * rows * RING * count,
            transcendentals=0,
        ),
        name="down_partial",
    )(*prefetch, *wholes, *[pre_act] * count)


def up_kernel(ordered_ref, masked_ref, pre_ref, weight_ref, *refs):
    keep_ref, send_ref = refs[-2:]
    tokens, width = masked_ref.shape
    grads = []
    part = tokens // 4
    for first in range(0, tokens, part):
        rows = slice(first, first + part)
        hidden_grad = lax.dot_general(
            masked_ref[rows, :], weight_ref[...], (((1,), (1,)), ((), ())),
            preferred_element_type=jnp.float32,
        )
        value = pre_ref[rows, :].astype(jnp.float32)
        cdf = 0.5 + 0.5 * lax.erf(value * SQRT_HALF)
        density = jnp.exp2(value * value * EXP2_SCALE)
        derivative = cdf + value * density * INV_ROOT_TWO_PI
        grads.append((hidden_grad * derivative).astype(jnp.bfloat16))
    grad = jnp.concatenate(grads, axis=0)
    half = width // CORES
    keep_ref[...] = jnp.dot(ordered_ref[:half, :], grad, preferred_element_type=jnp.float32)
    send_ref[...] = jnp.dot(ordered_ref[half:, :], grad, preferred_element_type=jnp.float32)


def up_call(ordered, masked, pre_act, weight, start, count):
    width, tokens = ordered.shape
    at = start // FF_BLOCK
    out_block = pl.BlockSpec((width // CORES, FF_BLOCK), lambda j: (0, j))
    out_shape = jax.ShapeDtypeStruct((width // CORES, count), jnp.float32)
    keep, send = pl.pallas_call(
        up_kernel,
        grid=(count // FF_BLOCK,),
        in_specs=[
            pl.BlockSpec((width, tokens), lambda j: (0, 0)),
            pl.BlockSpec((tokens, width), lambda j: (0, 0)),
            pl.BlockSpec((tokens, FF_BLOCK), lambda j: (0, at + j)),
            pl.BlockSpec((FF_BLOCK, width), lambda j: (at + j, 0)),
        ],
        out_specs=[out_block, out_block],
        out_shape=[out_shape, out_shape],
        compiler_params=pltpu.CompilerParams(vmem_limit_bytes=40 * MIB),
        cost_estimate=pl.CostEstimate(
            flops=4 * tokens * width * count,
            bytes_accessed=4 * tokens * width + 2 * tokens * count + 6 * width * count,
            transcendentals=2 * tokens * count,
        ),
        name="up_partial",
    )(ordered, masked, pre_act, weight)
    shape = (RING, HALVES, RING, width // (CHIPS * CORES * HALVES), count)
    return keep.reshape(shape), send.reshape(shape)


def replica_route(step):
    count = lax.axis_size("rep")
    return [(i, (i + step) % count) for i in range(count)]


def neighbours(block):
    return tuple(lax.ppermute(block, "rep", replica_route(step)) for step in (1, -1))


def opposite(received):
    from_behind, from_ahead = received
    half = from_behind.shape[0] // 2
    return (
        lax.ppermute(from_behind[:half], "rep", replica_route(1)),
        lax.ppermute(from_ahead[half:], "rep", replica_route(-1)),
    )


def held_blocks(block, received, far):
    return [block, received[1], jnp.concatenate(far, axis=0), received[0]]


def across_replicas(block):
    return [block] + [lax.ppermute(block, "rep", replica_route(-step)) for step in range(1, RING)]


def in_order(values, replica):
    once = [jnp.where(replica % 2 == 1, values[i - 1], values[i]) for i in range(4)]
    return [jnp.where(replica // 2 == 1, once[i - 2], once[i]) for i in range(4)]


def products_kernel(replica_ref, *refs):
    held, out_ref = refs[:-1], refs[-1]
    replica = replica_ref[0]
    rows, columns = held[0].shape[-2:]

    def add_rows(index, totals):
        at = pl.ds(pl.multiple_of(index * 8, 8), 8)
        sums = [totals[i * 8:(i + 1) * 8, :] for i in range(TERMS)]
        for column in range(0, columns, LANES):
            a, d, b, e = in_order(
                [ref[at, column:column + LANES] for ref in held], replica
            )
            terms = []
            for left, right in ((a, b), (d, e)):
                both = left + right
                terms += [left * left, right * right, left * right, both * both,
                          both * (left - right)]
            terms += [a * d, a * e, b * d, b * e]
            sums = [total + term for total, term in zip(sums, terms)]
        return jnp.concatenate(sums, axis=0)

    totals = lax.fori_loop(0, rows // 8, add_rows, jnp.zeros((TERMS * 8, LANES), jnp.float32))
    for i in range(TERMS):
        out_ref[i:i + 1, :] = jnp.sum(totals[i * 8:(i + 1) * 8, :], axis=0, keepdims=True)
    out_ref[TERMS:, :] = jnp.zeros((TERM_ROWS - TERMS, LANES), jnp.float32)


def products_call(replica, held):
    vmem = pl.BlockSpec(memory_space=pltpu.VMEM)
    return pl.pallas_call(
        products_kernel,
        in_specs=[pl.BlockSpec(memory_space=pltpu.SMEM)] + [vmem] * len(held),
        out_specs=vmem,
        out_shape=jax.ShapeDtypeStruct((TERM_ROWS, LANES), jnp.float32),
        compiler_params=pltpu.CompilerParams(vmem_limit_bytes=24 * MIB),
        cost_estimate=pl.CostEstimate(
            flops=TERMS * 2 * held[0].size, bytes_accessed=16 * held[0].size, transcendentals=0
        ),
        name="inner_products",
    )(replica, *held)


def sum_inner(values):
    values = values + inner_permute(values, core_route())
    for axis in (0, 1):
        others = [
            inner_permute(values, inner_route(
                lambda y, z, core: (y + step, z, core) if axis == 0 else (y, z + step, core)))
            for step in (1, 2, 3)
        ]
        values = (values + others[1]) + (others[0] + others[2])
    return values


def pair_coefs(first_sq, second_sq, cross, both_sq, difference):
    first_wide, second_wide = first_sq + EPSILON, second_sq + EPSILON
    first_coef = 1.0 - cross / (2.0 * first_wide)
    second_coef = 1.0 - cross / (2.0 * second_wide)
    plain = (first_coef * first_coef * first_sq + 2.0 * first_coef * second_coef * cross
             + second_coef * second_coef * second_sq)
    mean = 0.5 * (first_coef + second_coef)
    skew = 0.25 * (cross / first_wide) * (difference / second_wide)
    apart = first_sq + second_sq - 2.0 * cross
    opposite = mean * mean * both_sq + 2.0 * mean * skew * difference + skew * skew * apart
    square = jnp.where(both_sq < 0.25 * (first_sq + second_sq), opposite, plain)
    return first_coef, second_coef, square


def coefficients(t):
    a, b, left = pair_coefs(*t[0:5])
    d, e, right = pair_coefs(*t[5:10])
    cross = a * (d * t[10] + e * t[11]) + b * (d * t[12] + e * t[13])
    left_coef = 1.0 - cross / (2.0 * (left + EPSILON))
    right_coef = 1.0 - cross / (2.0 * (right + EPSILON))
    return left_coef * a, right_coef * d, left_coef * b, right_coef * e


def mix_kernel(counts, replica_ref, totals_ref, *refs):
    groups, outs = refs[:-len(counts)], refs[-len(counts):]
    replica = replica_ref[0]
    group = 0
    for count, out_ref in zip(counts, outs):
        totals = totals_ref[group]
        for index in range(1, count):
            totals = totals + totals_ref[group + index]
        totals = jnp.sum(totals, axis=1, keepdims=True)
        coefs = coefficients([totals[i:i + 1, :] for i in range(TERMS)])
        start = 0
        for index in range(group, group + count):
            held = groups[4 * index:4 * index + 4]
            rows, columns = out_ref.shape[0], held[0].shape[1]
            for first in range(0, held[0].shape[0], rows):
                values = in_order([ref[first:first + rows, :] for ref in held], replica)
                a, d, b, e = [value * coef for value, coef in zip(values, coefs)]
                out_ref[:, start:start + columns] = (a + b) + (d + e)
                start += columns
        group += count


def mix_call(replica, totals, rows, outs):
    vmem = pl.BlockSpec(memory_space=pltpu.VMEM)
    flat = [block for groups in outs for held in groups for block in held]
    shapes = [
        jax.ShapeDtypeStruct((count, sum(held[0].size for held in groups) // count), jnp.float32)
        for count, groups in zip(rows, outs)
    ]
    size = sum(shape.size for shape in shapes)
    return pl.pallas_call(
        functools.partial(mix_kernel, [len(groups) for groups in outs]),
        in_specs=[pl.BlockSpec(memory_space=pltpu.SMEM)] + [vmem] * (len(flat) + 1),
        out_specs=[vmem] * len(shapes),
        out_shape=shapes,
        compiler_params=pltpu.CompilerParams(vmem_limit_bytes=24 * MIB),
        cost_estimate=pl.CostEstimate(flops=7 * size, bytes_accessed=20 * size, transcendentals=0),
        name="combine",
    )(replica, totals, *flat)


ORDER = ['d0', 'd1', 'e0', 'e1', 'a0', 'd2', 'e2', 'a1', 'b0', 'a2', 'b1', 'a3', 'd3', 'd5', 'b2', 'a4', 'b3', 'a5', 'a6', 'b5']
GATES = {'b0': ('a1',), 'a0': ('d1', 'e1'), 'kb': ('e2',)}
RINGS = {'a': True, 'b': False, 'd': False}
SPLIT = 2
FAR = {'a': True, 'b': False, 'd': False}
JOINT = False


def on_device(layer_input, pre_act, cotangent, down_weight, lengths):
    table = destination_table()
    replica = lax.axis_index("rep").reshape(1)
    got = {}

    def wait(name, value):
        return gate(value, [got[other] for other in GATES.get(name, ())])

    places = [tuple(range(RING // 2)), tuple(range(RING // 2, RING))]
    kept, sent, sums, firsts, ends, blocks = {}, {}, {}, {}, {}, {}
    kept["d"], sent["d"], ordered, masked = down_call(
        table, pre_act, places[0], lengths, layer_input, cotangent
    )
    kept["e"], sent["e"] = down_call(table, pre_act, places[1], masked=masked)
    split = pre_act.shape[1] // 4 * SPLIT

    def core(name):
        if name == "a":
            kept[name], sent[name] = up_call(
                wait("ka", ordered), masked, pre_act, down_weight, 0, split
            )
        if name == "b":
            kept[name], sent[name] = up_call(
                wait("kb", ordered), masked, pre_act, down_weight, split, pre_act.shape[1] - split
            )
        return inner_permute(wait(name + "0", sent[name]), core_route())

    def first(name):
        extra = [sent["e"]] if name == "d" else []
        other = gate(got[name + "0"], [got[o] for o in GATES.get(name + "1", ())] + extra)
        sums[name] = core_sum(kept[name], other)
        return ring_start(sums[name], 0)

    def second(name):
        return ring_pass(sums[name], 0, wait(name + "2", got[name + "1"]))

    def third(name):
        parts = {"d": "de", "a": "ab" if JOINT else "a"}.get(name, name)
        passed = wait(name + "3", [got[part + "2"] for part in parts])
        found = [ring_end(sums[part], got[part + "1"], two) for part, two in zip(parts, passed)]
        if name == "d":
            count = RING // len(parts)
            ends[name] = [
                lambda l, h=h: found[l // count][h](l % count) for h in range(HALVES)
            ]
        elif len(parts) > 1:
            ends[name] = [
                lambda l, h=h: jnp.stack([part[h](l) for part in found]) for h in range(HALVES)
            ]
        else:
            ends[name] = found[0]
        if RINGS[name]:
            return ring_start(once_reduced(ends[name]), 1)
        return direct(ends[name])

    def fourth(name):
        return ring_pass(once_reduced(ends[name]), 1, wait(name + "4", got[name + "3"]))

    def near(name):
        if RINGS[name]:
            last = wait(name + "5", got[name + "4"])
            blocks[name] = joined(ring_end(once_reduced(ends[name]), got[name + "3"], last))
        else:
            blocks[name] = direct_end(ends[name], wait(name + "5", got[name + "3"]))
        if FAR[name]:
            return neighbours(blocks[name])
        return across_replicas(blocks[name])[1:]

    def far(name):
        return opposite(wait(name + "6", got[name + "5"]))

    steps = [core, first, second, third, fourth, near, far]
    for item in ORDER:
        got[item] = steps[int(item[1])](item[0])
    groups = [
        held_blocks(blocks[name], got[name + "5"], got[name + "6"]) if FAR[name]
        else [blocks[name], *got[name + "5"]]
        for name in ("a" if JOINT else "ab") + "d"
    ]
    groups = [[x.reshape(-1, x.shape[-1]) for x in held] for held in groups]
    totals = sum_inner(jnp.stack([products_call(replica, held) for held in groups]))
    rows = layer_input.shape[1] // (CHIPS * CORES), pre_act.shape[1] // (CHIPS * CORES)
    return tuple(mix_call(replica, totals, rows, [groups[:-1], groups[-1:]]))


def solution(mesh):
    in_specs = (
        P(("inner", "rep"), None),
        P(("inner", "rep"), None),
        P(("inner", "rep"), None),
        P(),
        P(("inner", "rep")),
    )
    out_specs = (P("inner", None), P("inner", None))
    return jax.shard_map(
        on_device, mesh=mesh, in_specs=in_specs, out_specs=out_specs, check_vma=False
    )
```

time: 351 us -> 209 us (0.60); the launches traced: 345 us -> 208 us
  local copies, waits for them, and re-layouts: 65 us -> 3.41 us
  Pallas kernels: 0 us -> 49.4 us
  between operations: 43.7 us -> 1.25 us
  matrix products: 42 us -> 0 us
  waiting for transfers between devices: 94.9 us -> 56.3 us
  other arithmetic: 41.3 us -> 31.1 us
  starting transfers between devices: 58.2 us -> 66.6 us
    pallas_call x0 -> x8, Pallas kernels: none -> 49.4 us  [the longest x2 24.1 us: up_call(): pl.pallas_call(up_kernel, grid=(count // FF_BLOCK,), in_specs=[pl.BlockSp...]
    dot_general x2 -> x0, matrix products: 42 us -> none  [the longest x1 26.2 us: on_device(): lax.dot_general(layer_input, pre_grad, (((0,), (0,)), ((), ())), preferre...]
    gather x4 -> x0, local copies, waits for them, and re-layouts: 40.2 us -> none  [arrange(): return grad.reshape(-1, rows, grad.shape[1])[order]]
    ppermute x32 -> x37, waiting for transfers between devices: 73.6 us -> 45.6 us  [inner_permute(): return lax.ppermute(block, 'inner', route)]
    another operation x4 -> x0, local copies, waits for them, and re-layouts: 23 us -> none  [the longest x2 17.7 us: products(): return jnp.stack([jnp.sum(term) for term in terms])]
    ppermute x6 -> x10, waiting for transfers between devices: 21.3 us -> 10.7 us  [the longest x6 10.7 us: across_replicas(): lax.ppermute(block, 'rep', replica_route(-step))]
    reduce_sum x3 -> x0, other arithmetic: 8.92 us -> none  [the longest x2 8.05 us: products(): return jnp.stack([jnp.sum(term) for term in terms])]
    ppermute x6 -> x10, starting transfers between devices: 9.91 us -> 16.8 us  [the longest x6 10.5 us: across_replicas(): lax.ppermute(block, 'rep', replica_route(-step))]
  transfers between devices with their start and end apart: 38 -> 47, of which waited for: 14 -> 22; matrix products, arithmetic and copies ran while one was open for 34% -> 15% of each run, Pallas kernels for 0% -> 17%
where the time goes in v3:
time: 209 us; the launch traced here: 208 us
  starting transfers between devices  66.6 us (32%)
  waiting for transfers between devices  56.3 us (27%)
  Pallas kernels  49.4 us (24%)
  other arithmetic  31.1 us (15%)
  local copies, waits for them, and re-layouts  3.41 us (2%)
    ppermute x37, starting transfers between devices, inner_permute(): return lax.ppermute(block, 'inner', route)  49.8 us
    ppermute x37, waiting for transfers between devices, inner_permute(): return lax.ppermute(block, 'inner', route)  45.6 us
    pallas_call x2, Pallas kernels, up_call(): pl.pallas_call(up_kernel, grid=(count // FF_BLOCK,), in_specs=[pl.BlockSp...  24.1 us
    pallas_call x2, Pallas kernels, down_call(): pl.pallas_call(first_down_kernel if is_first else down_kernel, grid_spec=...  21.5 us
    ppermute x6, waiting for transfers between devices, across_replicas(): lax.ppermute(block, 'rep', replica_route(-step))  10.7 us
    ppermute x6, starting transfers between devices, across_replicas(): lax.ppermute(block, 'rep', replica_route(-step))  10.5 us
    add x5, other arithmetic, ring_pass(): piece(3, 1) + from_ahead[0]  7.32 us
    add x4, other arithmetic, core_sum(): return lambda k, h: keep[k, h] + other[k, h]  6 us
  transfers between devices with their start and end apart: 47, of which 22 were waited for; matrix products, arithmetic and copies ran while one was open for 15% of the time, Pallas kernels for 17%

profile of v3, /device:TPU:0, one launch (start us, length us, event | category | flops | bytes accessed | tf_op | source)
XLA Modules:
  0.0 208.0 jit_solution(3126134280307210634)
XLA Ops:
  2.0 12.1 %down_partial.2 = (f32[4,2,2,64,1024]{4,3,2,1,0:T(8,128)}, f32[4,2,2,64,1024]{4,3,2,1,0:T(8,128)}, bf16[1024,1024]{1,0:T(8,128)(2,1)}, bf16[1024,1024]{1,0:T(8,128)(2,1)}) custom-call(s32[32]{0:T(128)} %reshape.822.blocks_ref, s32[64]{0:T(128)} %mul.75.rows_ref, s32[8]{0:T(128)} %lengths_ref.1, bf16[1024,1024]{1,0:T(8,128)(2,1)} %x_ref.1, ...), custom_call_target="tpu_custom_call" | custom-call | flops 4294967296 | bytes 16777216 | tf_op jit(solution)/shard_map/down_partial/pallas_call | solution.py:203
  14.1 9.5 %down_partial.3 = (f32[4,2,2,64,1024]{4,3,2,1,0:T(8,128)}, f32[4,2,2,64,1024]{4,3,2,1,0:T(8,128)}) custom-call(s32[32]{0:T(128)} %reshape.822.blocks_ref, bf16[1024,1024]{1,0:T(8,128)(2,1)} %get-tuple-element.45.masked_ref, bf16[1024,4096]{1,0:T(8,128)(2,1)} %pre_ref.3, bf16[1024,4096]{1,0:T(8,128)(2,1)} %pre_ref.3, bf16[1024,4096]{1,0:T(8,128)(2,1)} %pre_ref.3, ...), custom_call_target="tpu_custom_call" | custom-call | flops 4294967296 | bytes 16777216 | tf_op jit(solution)/shard_map/down_partial/pallas_call | solution.py:203
  24.0 3.7 %slice_add_fusion.25 = (f32[1,1,2,64,1024]{4,3,2,1,0:T(8,128)S(1)}, f32[1,1,2,64,1024]{4,3,2,1,0:T(8,128)S(1)}, f32[1,2,64,1024]{3,2,1,0:T(8,128)S(1)}, f32[1,2,...) fusion(f32[4,2,2,64,1024]{4,3,2,1,0:T(8,128)} %collective-permute-done, ...), kind=kLoop, calls=%fused_computation.63 | loop fusion | flops 786432 | bytes 9437184 | tf_op jit(solution)/shard_map/add | solution.py:101
  37.3 12.0 %up_partial.2 = (f32[512,2048]{1,0:T(8,128)S(1)}, f32[512,2048]{1,0:T(8,128)S(1)}) custom-call(bf16[1024,1024]{1,0:T(8,128)(2,1)S(1)} %copy-done.1, bf16[1024,1024]{1,0:T(8,128)(2,1)S(1)} %copy-done, bf16[1024,4096]{1,0:T(8,128)(2,1)} %pre_ref.3, bf16[4096,1024]{1,0:T(8,128)(2,1)} %weight_ref.3), custom_call_target="tpu_custom_call" | custom-call | flops 8589934592 | bytes 20971520 | tf_op jit(solution)/shard_map/up_partial/pallas_call | solution.py:251
  49.4 6.0 %collective-permute-done.4 = f32[2,2,64,1024]{3,2,1,0:T(8,128)} collective-permute-done((f32[2,2,64,1024]{3,2,1,0:T(8,128)S(1)}, f32[2,2,64,1024]{3,2,1,0:T(8,128)}, u32[]{:S(2)}, u32[]{:S(2)}) %collective-permute-start.4) | collective-permute-done | bytes 1048608 | tf_op jit(solution)/shard_map/ppermute | solution.py:52
  57.8 2.8 %collective-permute-start.20 = (f32[2,64,1024]{2,1,0:T(8,128)S(1)}, f32[2,64,1024]{2,1,0:T(8,128)S(1)}, u32[]{:S(2)}, u32[]{:S(2)}) collective-permute-start(f32[2,64,1024]{2,1,0:T(8,128)S(1)} %get-tuple-element.114), channel_id=1, source_target_pairs={{0,96},{4,28},{8,104},{12,4},{16,112},{20,12},{24,120},{28,20},{32... | collective-permute-start | bytes 1572872 | tf_op jit(solution)/shard_map/ppermute | solution.py:52
  60.7 2.4 %collective-permute-done.6 = f32[4,2,4,16,2048]{4,3,2,1,0:T(8,128)S(1)} collective-permute-done((f32[4,2,4,16,2048]{4,3,2,1,0:T(8,128)S(1)}, f32[4,2,4,16,2048]{4,3,2,1,0:T(8,128)S(1)}, u32[]{:S(2)}, u32[]{:S(2)}) %collective-permute-start.6) | collective-permute-done | bytes 4194336 | tf_op jit(solution)/shard_map/ppermute | solution.py:52
  64.9 2.8 %collective-permute-start.7 = (f32[2,4,16,2048]{3,2,1,0:T(8,128)}, f32[2,4,16,2048]{3,2,1,0:T(8,128)}, u32[]{:S(2)}, u32[]{:S(2)}) collective-permute-start(f32[2,4,16,2048]{3,2,1,0:T(8,128)} %pad_maximum_fusion.4), channel_id=1, source_target_pairs={{0,96},{4,28},{8,104},{12,4},{16,112},{20,12},{24,120},{28,20},{32... | collective-permute-start | bytes 3145736 | tf_op jit(solution)/shard_map/ppermute | solution.py:52
  68.8 3.0 %bitcast_add_fusion = (f32[2,64,1024]{2,1,0:T(8,128)}, f32[2,64,1024]{2,1,0:T(8,128)}) fusion(f32[2,2,64,1024]{3,2,1,0:T(8,128)} %collective-permute-done.2, f32[4,2,2,64,1024]{4,3,2,1,0:T(8,128)} %collective-permute-done, f32[4,2,2,64,1024]{4,3,2,1,0:T(8,128)} %get-tuple-element.48, f32[2,2,64,1024]{3,2,1,0:T(8,128)S(1)} %copy-done.7), kind=kLoop, calls=%fused_computation.60 | loop fusion | flops 524288 | bytes 4194304 | tf_op jit(solution)/shard_map/add | solution.py:66
  71.8 3.2 %collective-permute-start.33 = (f32[2,64,1024]{2,1,0:T(8,128)}, f32[2,64,1024]{2,1,0:T(8,128)S(1)}, u32[]{:S(2)}, u32[]{:S(2)}) collective-permute-start(f32[2,64,1024]{2,1,0:T(8,128)} %get-tuple-element.116), channel_id=1, source_target_pairs={{0,96},{4,28},{8,104},{12,4},{16,112},{20,12},{24,120},{28,20},{32... | collective-permute-start | bytes 1572872 | tf_op jit(solution)/shard_map/ppermute | solution.py:52
  75.8 12.1 %up_partial.3 = (f32[512,2048]{1,0:T(8,128)S(1)}, f32[512,2048]{1,0:T(8,128)S(1)}) custom-call(bf16[1024,1024]{1,0:T(8,128)(2,1)S(1)} %copy-done.1, bf16[1024,1024]{1,0:T(8,128)(2,1)S(1)} %copy-done, bf16[1024,4096]{1,0:T(8,128)(2,1)} %pre_ref.3, bf16[4096,1024]{1,0:T(8,128)(2,1)} %weight_ref.3), custom_call_target="tpu_custom_call" | custom-call | flops 8589934592 | bytes 20971520 | tf_op jit(solution)/shard_map/up_partial/pallas_call | solution.py:251
  101.0 3.7 %collective-permute-start.35 = (f32[2,64,1024]{2,1,0:T(8,128)S(1)}, f32[2,64,1024]{2,1,0:T(8,128)S(1)}, u32[]{:S(2)}, u32[]{:S(2)}) collective-permute-start(f32[2,64,1024]{2,1,0:T(8,128)S(1)} %pad_maximum_fusion.9), channel_id=1, source_target_pairs={{0,16},{4,68},{8,24},{12,76},{16,0},{20,84},{24,8},{28,92},{32,48}... | collective-permute-start | bytes 1572872 | tf_op jit(solution)/shard_map/ppermute | solution.py:52
  104.7 3.3 %collective-permute-done.10 = f32[4,16,2048]{2,1,0:T(8,128)S(1)} collective-permute-done((f32[4,16,2048]{2,1,0:T(8,128)S(1)}, f32[4,16,2048]{2,1,0:T(8,128)S(1)}, u32[]{:S(2)}, u32[]{:S(2)}) %collective-permute-start.10) | collective-permute-done | bytes 524320 | tf_op jit(solution)/shard_map/ppermute | solution.py:52
  111.4 5.2 %collective-permute-start.12 = (f32[2,16,2048]{2,1,0:T(8,128)S(1)}, f32[2,16,2048]{2,1,0:T(8,128)S(1)}, u32[]{:S(2)}, u32[]{:S(2)}) collective-permute-start(f32[2,16,2048]{2,1,0:T(8,128)S(1)} %pad_maximum_fusion.13), channel_id=1, source_target_pairs={{0,8},{4,36},{8,16},{12,44},{16,24},{20,52},{24,0},{28,60},{32,40}... | collective-permute-start | bytes 786440 | tf_op jit(solution)/shard_map/ppermute | solution.py:52
  133.2 2.7 %collective-permute-start.38 = (f32[128,1024]{1,0:T(8,128)S(1)}, f32[128,1024]{1,0:T(8,128)S(1)}, u32[]{:S(2)}, u32[]{:S(2)}) collective-permute-start(f32[128,1024]{1,0:T(8,128)S(1)} %pad_maximum_fusion.11.refs_0_.refs_8_), channel_id=1, source_target_pairs={{0,2},{1,3},{2,0},{3,1},{4,6},{5,7},{6,4},{7,5},{8,10},{9,11},{10,... | collective-permute-start | bytes 1572872 | tf_op jit(solution)/shard_map/ppermute | solution.py:297
  137.0 2.8 %collective-permute-start.37 = (f32[128,1024]{1,0:T(8,128)S(1)}, f32[128,1024]{1,0:T(8,128)S(1)}, u32[]{:S(2)}, u32[]{:S(2)}) collective-permute-start(f32[128,1024]{1,0:T(8,128)S(1)} %pad_maximum_fusion.11.refs_0_.refs_8_), channel_id=1, source_target_pairs={{0,3},{1,0},{2,1},{3,2},{4,7},{5,4},{6,5},{7,6},{8,11},{9,8},{10,9... | collective-permute-start | bytes 1572872 | tf_op jit(solution)/shard_map/ppermute | solution.py:297
  140.9 2.7 %collective-permute-done.23 = f32[2,4,16,2048]{3,2,1,0:T(8,128)S(1)} collective-permute-done((f32[2,4,16,2048]{3,2,1,0:T(8,128)S(1)}, f32[2,4,16,2048]{3,2,1,0:T(8,128)S(1)}, u32[]{:S(2)}, u32[]{:S(2)}) %collective-permute-start.23) | collective-permute-done | bytes 1048608 | tf_op jit(solution)/shard_map/ppermute | solution.py:52
  146.9 6.2 %collective-permute-done.25 = f32[4,16,2048]{2,1,0:T(8,128)S(1)} collective-permute-done((f32[4,16,2048]{2,1,0:T(8,128)S(1)}, f32[4,16,2048]{2,1,0:T(8,128)S(1)}, u32[]{:S(2)}, u32[]{:S(2)}) %collective-permute-start.25) | collective-permute-done | bytes 524320 | tf_op jit(solution)/shard_map/ppermute | solution.py:52
  155.2 2.8 %collective-permute-start.15 = (f32[32,2048]{1,0:T(8,128)S(1)}, f32[32,2048]{1,0:T(8,128)S(1)}, u32[]{:S(2)}, u32[]{:S(2)}) collective-permute-start(f32[32,2048]{1,0:T(8,128)S(1)} %pad_maximum_fusion.14.refs_0_), channel_id=1, source_target_pairs={{0,3},{1,0},{2,1},{3,2},{4,7},{5,4},{6,5},{7,6},{8,11},{9,8},{10,9... | collective-permute-start | bytes 786440 | tf_op jit(solution)/shard_map/ppermute | solution.py:280
  160.6 4.1 %collective-permute-start.27 = (f32[2,16,2048]{2,1,0:T(8,128)}, f32[2,16,2048]{2,1,0:T(8,128)}, u32[]{:S(2)}, u32[]{:S(2)}) collective-permute-start(f32[2,16,2048]{2,1,0:T(8,128)} %pad_maximum_fusion.16), channel_id=1, source_target_pairs={{0,16},{4,68},{8,24},{12,76},{16,0},{20,84},{24,8},{28,92},{32,48}... | collective-permute-start | bytes 786440 | tf_op jit(solution)/shard_map/ppermute | solution.py:52
  168.4 3.7 %collective-permute-done.27 = f32[2,16,2048]{2,1,0:T(8,128)} collective-permute-done((f32[2,16,2048]{2,1,0:T(8,128)}, f32[2,16,2048]{2,1,0:T(8,128)}, u32[]{:S(2)}, u32[]{:S(2)}) %collective-permute-start.27) | collective-permute-done | bytes 262176 | tf_op jit(solution)/shard_map/ppermute | solution.py:52
  177.6 10.1 %collective-permute-done.31.refs_3_.refs_7_ = f32[32,2048]{1,0:T(8,128)S(1)} collective-permute-done((f32[32,2048]{1,0:T(8,128)S(1)}, f32[32,2048]{1,0:T(8,128)S(1)}, u32[]{:S(2)}, u32[]{:S(2)}) %collective-permute-start.31) | collective-permute-done | bytes 262176 | tf_op jit(solution)/shard_map/ppermute | solution.py:297
  190.2 3.0 %collective-permute-start.43 = (f32[3,16,128]{2,1,0:T(8,128)S(1)}, f32[3,16,128]{2,1,0:T(8,128)S(1)}, u32[]{:S(2)}, u32[]{:S(2)}) collective-permute-start(f32[3,16,128]{2,1,0:T(8,128)S(1)} %fusion.98), channel_id=1, source_target_pairs={{0,96},{4,100},{8,104},{12,108},{16,112},{20,116},{24,120},{28,124... | collective-permute-start | bytes 73736 | tf_op jit(solution)/shard_map/ppermute | solution.py:52
  195.0 3.5 %collective-permute-done.41 = f32[3,16,128]{2,1,0:T(8,128)S(1)} collective-permute-done((f32[3,16,128]{2,1,0:T(8,128)S(1)}, f32[3,16,128]{2,1,0:T(8,128)S(1)}, u32[]{:S(2)}, u32[]{:S(2)}) %collective-permute-start.41) | collective-permute-done | bytes 24608 | tf_op jit(solution)/shard_map/ppermute | solution.py:52
  (165 shorter events, 83.6 us)
Async XLA Ops:
  27.9 21.4 %collective-permute-start.1 = (f32[2,2,64,1024]{3,2,1,0:T(8,128)S(1)}, f32[2,2,64,1024]{3,2,1,0:T(8,128)S(1)}, u32[]{:S(2)}, u32[]{:S(2)}) collective-permute-start(f32[2,2,64,1024]{3,2,1,0:T(8,128)S(1)} %pad_maximum_fusion), channel_id=1, source_target_pairs={{0,32},{4,12},{8,40},{12,20},{16,48},{20,28},{24,56},{28,4},{32,64... | collective-permute-start | bytes 3145736 | tf_op jit(solution)/shard_map/ppermute | solution.py:52
  29.7 19.6 %collective-permute-start.2 = (f32[2,2,64,1024]{3,2,1,0:T(8,128)S(1)}, f32[2,2,64,1024]{3,2,1,0:T(8,128)}, u32[]{:S(2)}, u32[]{:S(2)}) collective-permute-start(f32[2,2,64,1024]{3,2,1,0:T(8,128)S(1)} %pad_maximum_fusion.1), channel_id=1, source_target_pairs={{0,96},{4,28},{8,104},{12,4},{16,112},{20,12},{24,120},{28,20},{32... | collective-permute-start | bytes 3145736 | tf_op jit(solution)/shard_map/ppermute | solution.py:52
  33.8 21.5 %collective-permute-start.4 = (f32[2,2,64,1024]{3,2,1,0:T(8,128)S(1)}, f32[2,2,64,1024]{3,2,1,0:T(8,128)}, u32[]{:S(2)}, u32[]{:S(2)}) collective-permute-start(f32[2,2,64,1024]{3,2,1,0:T(8,128)S(1)} %pad_maximum_fusion.2), channel_id=1, source_target_pairs={{0,32},{4,12},{8,40},{12,20},{16,48},{20,28},{24,56},{28,4},{32,64... | collective-permute-start | bytes 3145736 | tf_op jit(solution)/shard_map/ppermute | solution.py:52
  35.3 20.7 %collective-permute-start.5 = (f32[2,2,64,1024]{3,2,1,0:T(8,128)S(1)}, f32[2,2,64,1024]{3,2,1,0:T(8,128)}, u32[]{:S(2)}, u32[]{:S(2)}) collective-permute-start(f32[2,2,64,1024]{3,2,1,0:T(8,128)S(1)} %pad_maximum_fusion.3), channel_id=1, source_target_pairs={{0,96},{4,28},{8,104},{12,4},{16,112},{20,12},{24,120},{28,20},{32... | collective-permute-start | bytes 3145736 | tf_op jit(solution)/shard_map/ppermute | solution.py:52
  57.8 17.2 %collective-permute-start.20 = (f32[2,64,1024]{2,1,0:T(8,128)S(1)}, f32[2,64,1024]{2,1,0:T(8,128)S(1)}, u32[]{:S(2)}, u32[]{:S(2)}) collective-permute-start(f32[2,64,1024]{2,1,0:T(8,128)S(1)} %get-tuple-element.114), channel_id=1, source_target_pairs={{0,96},{4,28},{8,104},{12,4},{16,112},{20,12},{24,120},{28,20},{32... | collective-permute-start | bytes 1572872 | tf_op jit(solution)/shard_map/ppermute | solution.py:52
  60.7 15.2 %collective-permute-start.19 = (f32[2,64,1024]{2,1,0:T(8,128)S(1)}, f32[2,64,1024]{2,1,0:T(8,128)}, u32[]{:S(2)}, u32[]{:S(2)}) collective-permute-start(f32[2,64,1024]{2,1,0:T(8,128)S(1)} %get-tuple-element.115), channel_id=1, source_target_pairs={{0,32},{4,12},{8,40},{12,20},{16,48},{20,28},{24,56},{28,4},{32,64... | collective-permute-start | bytes 1572872 | tf_op jit(solution)/shard_map/ppermute | solution.py:52
  64.9 23.0 %collective-permute-start.7 = (f32[2,4,16,2048]{3,2,1,0:T(8,128)}, f32[2,4,16,2048]{3,2,1,0:T(8,128)}, u32[]{:S(2)}, u32[]{:S(2)}) collective-permute-start(f32[2,4,16,2048]{3,2,1,0:T(8,128)} %pad_maximum_fusion.4), channel_id=1, source_target_pairs={{0,96},{4,28},{8,104},{12,4},{16,112},{20,12},{24,120},{28,20},{32... | collective-permute-start | bytes 3145736 | tf_op jit(solution)/shard_map/ppermute | solution.py:52
  68.8 19.1 %collective-permute-start.8 = (f32[2,4,16,2048]{3,2,1,0:T(8,128)}, f32[2,4,16,2048]{3,2,1,0:T(8,128)}, u32[]{:S(2)}, u32[]{:S(2)}) collective-permute-start(f32[2,4,16,2048]{3,2,1,0:T(8,128)} %pad_maximum_fusion.5), channel_id=1, source_target_pairs={{0,32},{4,12},{8,40},{12,20},{16,48},{20,28},{24,56},{28,4},{32,64... | collective-permute-start | bytes 3145736 | tf_op jit(solution)/shard_map/ppermute | solution.py:52
  71.8 16.8 %collective-permute-start.33 = (f32[2,64,1024]{2,1,0:T(8,128)}, f32[2,64,1024]{2,1,0:T(8,128)S(1)}, u32[]{:S(2)}, u32[]{:S(2)}) collective-permute-start(f32[2,64,1024]{2,1,0:T(8,128)} %get-tuple-element.116), channel_id=1, source_target_pairs={{0,96},{4,28},{8,104},{12,4},{16,112},{20,12},{24,120},{28,20},{32... | collective-permute-start | bytes 1572872 | tf_op jit(solution)/shard_map/ppermute | solution.py:52
  75.0 15.7 %collective-permute-start.32 = (f32[2,64,1024]{2,1,0:T(8,128)}, f32[2,64,1024]{2,1,0:T(8,128)}, u32[]{:S(2)}, u32[]{:S(2)}) collective-permute-start(f32[2,64,1024]{2,1,0:T(8,128)} %get-tuple-element.117), channel_id=1, source_target_pairs={{0,32},{4,12},{8,40},{12,20},{16,48},{20,28},{24,56},{28,4},{32,64... | collective-permute-start | bytes 1572872 | tf_op jit(solution)/shard_map/ppermute | solution.py:52
  87.9 37.4 %collective-permute-start.21 = (f32[4,2,4,16,2048]{4,3,2,1,0:T(8,128)S(1)}, f32[4,2,4,16,2048]{4,3,2,1,0:T(8,128)S(1)}, u32[]{:S(2)}, u32[]{:S(2)}) collective-permute-start(f32[4,2,4,16,2048]{4,3,2,1,0:T(8,128)S(1)} %bitcast.409), channel_id=1, source_target_pairs={{0,4},{4,0},{8,12},{12,8},{16,20},{20,16},{24,28},{28,24},{32,36},... | collective-permute-start | bytes 12582920 | tf_op jit(solution)/shard_map/ppermute | solution.py:52
  92.9 23.7 %collective-permute-start.34 = (f32[2,64,1024]{2,1,0:T(8,128)S(1)}, f32[2,64,1024]{2,1,0:T(8,128)S(1)}, u32[]{:S(2)}, u32[]{:S(2)}) collective-permute-start(f32[2,64,1024]{2,1,0:T(8,128)S(1)} %pad_maximum_fusion.8), channel_id=1, source_target_pairs={{0,8},{4,36},{8,16},{12,44},{16,24},{20,52},{24,0},{28,60},{32,40}... | collective-permute-start | bytes 1572872 | tf_op jit(solution)/shard_map/ppermute | solution.py:52
  96.4 11.6 %collective-permute-start.10 = (f32[4,16,2048]{2,1,0:T(8,128)S(1)}, f32[4,16,2048]{2,1,0:T(8,128)S(1)}, u32[]{:S(2)}, u32[]{:S(2)}) collective-permute-start(f32[4,16,2048]{2,1,0:T(8,128)S(1)} %get-tuple-element.86), channel_id=1, source_target_pairs={{0,96},{4,28},{8,104},{12,4},{16,112},{20,12},{24,120},{28,20},{32... | collective-permute-start | bytes 1572872 | tf_op jit(solution)/shard_map/ppermute | solution.py:52
  96.5 12.9 %collective-permute-start.9 = (f32[4,16,2048]{2,1,0:T(8,128)S(1)}, f32[4,16,2048]{2,1,0:T(8,128)S(1)}, u32[]{:S(2)}, u32[]{:S(2)}) collective-permute-start(f32[4,16,2048]{2,1,0:T(8,128)S(1)} %get-tuple-element.87), channel_id=1, source_target_pairs={{0,32},{4,12},{8,40},{12,20},{16,48},{20,28},{24,56},{28,4},{32,64... | collective-permute-start | bytes 1572872 | tf_op jit(solution)/shard_map/ppermute | solution.py:52
  101.0 15.7 %collective-permute-start.35 = (f32[2,64,1024]{2,1,0:T(8,128)S(1)}, f32[2,64,1024]{2,1,0:T(8,128)S(1)}, u32[]{:S(2)}, u32[]{:S(2)}) collective-permute-start(f32[2,64,1024]{2,1,0:T(8,128)S(1)} %pad_maximum_fusion.9), channel_id=1, source_target_pairs={{0,16},{4,68},{8,24},{12,76},{16,0},{20,84},{24,8},{28,92},{32,48}... | collective-permute-start | bytes 1572872 | tf_op jit(solution)/shard_map/ppermute | solution.py:52
  126.1 14.9 %collective-permute-start.22 = (f32[2,4,16,2048]{3,2,1,0:T(8,128)S(1)}, f32[2,4,16,2048]{3,2,1,0:T(8,128)S(1)}, u32[]{:S(2)}, u32[]{:S(2)}) collective-permute-start(f32[2,4,16,2048]{3,2,1,0:T(8,128)S(1)} %pad_maximum_fusion.6), channel_id=1, source_target_pairs={{0,96},{4,28},{8,104},{12,4},{16,112},{20,12},{24,120},{28,20},{32... | collective-permute-start | bytes 3145736 | tf_op jit(solution)/shard_map/ppermute | solution.py:52
  127.5 16.1 %collective-permute-start.23 = (f32[2,4,16,2048]{3,2,1,0:T(8,128)S(1)}, f32[2,4,16,2048]{3,2,1,0:T(8,128)S(1)}, u32[]{:S(2)}, u32[]{:S(2)}) collective-permute-start(f32[2,4,16,2048]{3,2,1,0:T(8,128)S(1)} %pad_maximum_fusion.7), channel_id=1, source_target_pairs={{0,32},{4,12},{8,40},{12,20},{16,48},{20,28},{24,56},{28,4},{32,64... | collective-permute-start | bytes 3145736 | tf_op jit(solution)/shard_map/ppermute | solution.py:52
  131.6 28.7 %collective-permute-start.39 = (f32[128,1024]{1,0:T(8,128)S(1)}, f32[128,1024]{1,0:T(8,128)S(1)}, u32[]{:S(2)}, u32[]{:S(2)}) collective-permute-start(f32[128,1024]{1,0:T(8,128)S(1)} %pad_maximum_fusion.11.refs_0_.refs_8_), channel_id=1, source_target_pairs={{0,1},{1,2},{2,3},{3,0},{4,5},{5,6},{6,7},{7,4},{8,9},{9,10},{10,1... | collective-permute-start | bytes 1572872 | tf_op jit(solution)/shard_map/ppermute | solution.py:297
  133.2 27.5 %collective-permute-start.38 = (f32[128,1024]{1,0:T(8,128)S(1)}, f32[128,1024]{1,0:T(8,128)S(1)}, u32[]{:S(2)}, u32[]{:S(2)}) collective-permute-start(f32[128,1024]{1,0:T(8,128)S(1)} %pad_maximum_fusion.11.refs_0_.refs_8_), channel_id=1, source_target_pairs={{0,2},{1,3},{2,0},{3,1},{4,6},{5,7},{6,4},{7,5},{8,10},{9,11},{10,... | collective-permute-start | bytes 1572872 | tf_op jit(solution)/shard_map/ppermute | solution.py:297
  137.0 27.7 %collective-permute-start.37 = (f32[128,1024]{1,0:T(8,128)S(1)}, f32[128,1024]{1,0:T(8,128)S(1)}, u32[]{:S(2)}, u32[]{:S(2)}) collective-permute-start(f32[128,1024]{1,0:T(8,128)S(1)} %pad_maximum_fusion.11.refs_0_.refs_8_), channel_id=1, source_target_pairs={{0,3},{1,0},{2,1},{3,2},{4,7},{5,4},{6,5},{7,6},{8,11},{9,8},{10,9... | collective-permute-start | bytes 1572872 | tf_op jit(solution)/shard_map/ppermute | solution.py:297
  153.0 13.2 %collective-permute-start.16 = (f32[32,2048]{1,0:T(8,128)S(1)}, f32[32,2048]{1,0:T(8,128)S(1)}, u32[]{:S(2)}, u32[]{:S(2)}) collective-permute-start(f32[32,2048]{1,0:T(8,128)S(1)} %pad_maximum_fusion.14.refs_0_), channel_id=1, source_target_pairs={{0,1},{1,2},{2,3},{3,0},{4,5},{5,6},{6,7},{7,4},{8,9},{9,10},{10,1... | collective-permute-start | bytes 786440 | tf_op jit(solution)/shard_map/ppermute | solution.py:280
  173.6 14.0 %collective-permute-start.31 = (f32[32,2048]{1,0:T(8,128)S(1)}, f32[32,2048]{1,0:T(8,128)S(1)}, u32[]{:S(2)}, u32[]{:S(2)}) collective-permute-start(f32[32,2048]{1,0:T(8,128)S(1)} %pad_maximum_fusion.18.refs_0_.refs_4_), channel_id=1, source_target_pairs={{0,1},{1,2},{2,3},{3,0},{4,5},{5,6},{6,7},{7,4},{8,9},{9,10},{10,1... | collective-permute-start | bytes 786440 | tf_op jit(solution)/shard_map/ppermute | solution.py:297
  173.7 13.9 %collective-permute-start.30 = (f32[32,2048]{1,0:T(8,128)S(1)}, f32[32,2048]{1,0:T(8,128)S(1)}, u32[]{:S(2)}, u32[]{:S(2)}) collective-permute-start(f32[32,2048]{1,0:T(8,128)S(1)} %pad_maximum_fusion.18.refs_0_.refs_4_), channel_id=1, source_target_pairs={{0,2},{1,3},{2,0},{3,1},{4,6},{5,7},{6,4},{7,5},{8,10},{9,11},{10,... | collective-permute-start | bytes 786440 | tf_op jit(solution)/shard_map/ppermute | solution.py:297
  176.0 12.3 %collective-permute-start.29 = (f32[32,2048]{1,0:T(8,128)S(1)}, f32[32,2048]{1,0:T(8,128)S(1)}, u32[]{:S(2)}, u32[]{:S(2)}) collective-permute-start(f32[32,2048]{1,0:T(8,128)S(1)} %pad_maximum_fusion.18.refs_0_.refs_4_), channel_id=1, source_target_pairs={{0,3},{1,0},{2,1},{3,2},{4,7},{5,4},{6,5},{7,6},{8,11},{9,8},{10,9... | collective-permute-start | bytes 786440 | tf_op jit(solution)/shard_map/ppermute | solution.py:297
  (39 other events, 377.2 us)

commit v4 on v3

--- a/solution.py
+++ b/solution.py
@@ -126,15 +126,6 @@
         valid = lax.broadcasted_iota(jnp.int32, (SEQ, columns), 0) < lengths_ref[seq]
         values = cotangent_ref[rows, :].astype(jnp.float32)
         masked_ref[rows, :] = jnp.where(valid, values, 0.0).astype(masked_ref.dtype)
-
-
-def prepare(rows_ref, lengths_ref, x_ref, cotangent_ref, ordered_ref, masked_ref, turned_ref):
-    strip = x_ref.shape[1] // (CHIPS * CORES * HALVES)
-    write_masked(lengths_ref, cotangent_ref, masked_ref)
-    turned_ref[...] = x_ref[...].T
-    for index in range(x_ref.shape[1] // strip):
-        start = pl.multiple_of(rows_ref[index], strip)
-        ordered_ref[index * strip:(index + 1) * strip, :] = turned_ref[pl.ds(start, strip), :]
 
 
 def down_blocks(pre_refs, masked_ref, keep_ref, send_ref):
@@ -156,12 +147,12 @@
             out_ref[0, :, place, :, :] = part.reshape(HALVES, rows // HALVES, part.shape[1])
 
 
-def first_down_kernel(blocks_ref, rows_ref, lengths_ref, x_ref, cotangent_ref, *refs):
-    pre_refs, (keep_ref, send_ref, ordered_ref, masked_ref, turned_ref) = refs[:-5], refs[-5:]
+def first_down_kernel(blocks_ref, lengths_ref, cotangent_ref, *refs):
+    pre_refs, (keep_ref, send_ref, masked_ref) = refs[:-3], refs[-3:]
 
     @pl.when(pl.program_id(0) == 0)
     def _():
-        prepare(rows_ref, lengths_ref, x_ref, cotangent_ref, ordered_ref, masked_ref, turned_ref)
+        write_masked(lengths_ref, cotangent_ref, masked_ref)
 
     down_blocks(pre_refs, masked_ref, keep_ref, send_ref)
 
@@ -170,11 +161,10 @@
     down_blocks(refs[:-2], masked_ref, *refs[-2:])
 
 
-def down_call(table, pre_act, places, lengths=None, x=None, cotangent=None, masked=None):
+def down_call(table, pre_act, places, lengths=None, cotangent=None, masked=None):
     is_first = masked is None
     tokens, width = (cotangent if is_first else masked).shape
     rows = pre_act.shape[1] // (CHIPS * CORES)
-    strip = width // (CHIPS * CORES * HALVES)
 
     def pre_spec(which, place):
         return pl.BlockSpec(
@@ -182,23 +172,16 @@
         )
 
     whole = pl.BlockSpec((tokens, width), lambda k, *_: (0, 0))
-    turned = pl.BlockSpec((width, tokens), lambda k, *_: (0, 0))
     out_block = pl.BlockSpec(
         (1, HALVES, len(places), rows // HALVES, width), lambda k, *_: (k, 0, 0, 0, 0)
     )
     out_shape = [
         jax.ShapeDtypeStruct((RING, HALVES, len(places), rows // HALVES, width), jnp.float32)
     ] * 2
-    prefetch, wholes, scratch, extra = [table.reshape(-1)], [masked], [], []
+    prefetch, wholes, extra = [table.reshape(-1)], [masked], []
     if is_first:
-        half = lax.iota(jnp.int32, HALVES)[None, None, :, None]
-        strips = (table[:, :, None, :] * HALVES + half).reshape(-1) * strip
-        prefetch, wholes = prefetch + [strips, lengths], [x, cotangent]
-        scratch, extra = [pltpu.VMEM((width, tokens), jnp.bfloat16)], [turned, whole]
-        out_shape = out_shape + [
-            jax.ShapeDtypeStruct((width, tokens), jnp.bfloat16),
-            jax.ShapeDtypeStruct((tokens, width), jnp.bfloat16),
-        ]
+        prefetch, wholes, extra = prefetch + [lengths], [cotangent], [whole]
+        out_shape = out_shape + [jax.ShapeDtypeStruct((tokens, width), jnp.bfloat16)]
     count = 2 * len(places)
     return pl.pallas_call(
         first_down_kernel if is_first else down_kernel,
@@ -208,7 +191,6 @@
             in_specs=[whole] * len(wholes)
             + [pre_spec(which, place) for which in range(2) for place in places],
             out_specs=[out_block, out_block] + extra,
-            scratch_shapes=scratch,
         ),
         out_shape=out_shape,
         compiler_params=pltpu.CompilerParams(vmem_limit_bytes=60 * MIB),
@@ -221,8 +203,7 @@
     )(*prefetch, *wholes, *[pre_act] * count)
 
 
-def up_kernel(ordered_ref, masked_ref, pre_ref, weight_ref, *refs):
-    keep_ref, send_ref = refs[-2:]
+def up_columns(ordered_ref, masked_ref, pre_ref, weight_ref, keep_ref, send_ref):
     tokens, width = masked_ref.shape
     grads = []
     part = tokens // 4
@@ -243,22 +224,51 @@
     send_ref[...] = jnp.dot(ordered_ref[half:, :], grad, preferred_element_type=jnp.float32)
 
 
-def up_call(ordered, masked, pre_act, weight, start, count):
-    width, tokens = ordered.shape
+def first_up_kernel(rows_ref, x_ref, masked_ref, pre_ref, weight_ref,
+                    keep_ref, send_ref, ordered_ref, turned_ref):
+    @pl.when(pl.program_id(0) == 0)
+    def _():
+        strip = x_ref.shape[1] // (CHIPS * CORES * HALVES)
+        turned_ref[...] = x_ref[...].T
+        for index in range(x_ref.shape[1] // strip):
+            start = pl.multiple_of(rows_ref[index], strip)
+            ordered_ref[index * strip:(index + 1) * strip, :] = turned_ref[pl.ds(start, strip), :]
+
+    up_columns(ordered_ref, masked_ref, pre_ref, weight_ref, keep_ref, send_ref)
+
+
+def up_kernel(rows_ref, ordered_ref, masked_ref, pre_ref, weight_ref, keep_ref, send_ref):
+    up_columns(ordered_ref, masked_ref, pre_ref, weight_ref, keep_ref, send_ref)
+
+
+def up_call(table, x, ordered, masked, pre_act, weight, start, count):
+    is_first = ordered is None
+    tokens, width = masked.shape
+    strip = width // (CHIPS * CORES * HALVES)
+    half = lax.iota(jnp.int32, HALVES)[None, None, :, None]
+    strips = (table[:, :, None, :] * HALVES + half).reshape(-1) * strip
     at = start // FF_BLOCK
-    out_block = pl.BlockSpec((width // CORES, FF_BLOCK), lambda j: (0, j))
-    out_shape = jax.ShapeDtypeStruct((width // CORES, count), jnp.float32)
-    keep, send = pl.pallas_call(
-        up_kernel,
-        grid=(count // FF_BLOCK,),
-        in_specs=[
-            pl.BlockSpec((width, tokens), lambda j: (0, 0)),
-            pl.BlockSpec((tokens, width), lambda j: (0, 0)),
-            pl.BlockSpec((tokens, FF_BLOCK), lambda j: (0, at + j)),
-            pl.BlockSpec((FF_BLOCK, width), lambda j: (at + j, 0)),
-        ],
-        out_specs=[out_block, out_block],
-        out_shape=[out_shape, out_shape],
+    turned = pl.BlockSpec((width, tokens), lambda j, *_: (0, 0))
+    whole = pl.BlockSpec((tokens, width), lambda j, *_: (0, 0))
+    out_block = pl.BlockSpec((width // CORES, FF_BLOCK), lambda j, *_: (0, j))
+    out_shape = [jax.ShapeDtypeStruct((width // CORES, count), jnp.float32)] * 2
+    if is_first:
+        out_shape = out_shape + [jax.ShapeDtypeStruct((width, tokens), jnp.bfloat16)]
+    keep, send, *ordered_out = pl.pallas_call(
+        first_up_kernel if is_first else up_kernel,
+        grid_spec=pltpu.PrefetchScalarGridSpec(
+            num_scalar_prefetch=1,
+            grid=(count // FF_BLOCK,),
+            in_specs=[
+                whole if is_first else turned,
+                whole,
+                pl.BlockSpec((tokens, FF_BLOCK), lambda j, *_: (0, at + j)),
+                pl.BlockSpec((FF_BLOCK, width), lambda j, *_: (at + j, 0)),
+            ],
+            out_specs=[out_block, out_block] + [turned] * is_first,
+            scratch_shapes=[pltpu.VMEM((width, tokens), jnp.bfloat16)] * is_first,
+        ),
+        out_shape=out_shape,
         compiler_params=pltpu.CompilerParams(vmem_limit_bytes=40 * MIB),
         cost_estimate=pl.CostEstimate(
             flops=4 * tokens * width * count,
@@ -266,9 +276,9 @@
             transcendentals=2 * tokens * count,
         ),
         name="up_partial",
-    )(ordered, masked, pre_act, weight)
-    shape = (RING, HALVES, RING, width // (CHIPS * CORES * HALVES), count)
-    return keep.reshape(shape), send.reshape(shape)
+    )(strips, x if is_first else ordered, masked, pre_act, weight)
+    shape = (RING, HALVES, RING, strip, count)
+    return keep.reshape(shape), send.reshape(shape), *ordered_out
 
 
 def replica_route(step):
@@ -423,7 +433,7 @@
 ORDER = ['d0', 'd1', 'e0', 'e1', 'a0', 'd2', 'e2', 'a1', 'b0', 'a2', 'b1', 'a3', 'd3', 'd5', 'b2', 'a4', 'b3', 'a5', 'a6', 'b5']
 GATES = {'b0': ('a1',), 'a0': ('d1', 'e1'), 'kb': ('e2',)}
 RINGS = {'a': True, 'b': False, 'd': False}
-SPLIT = 2
+SPLIT = 4
 FAR = {'a': True, 'b': False, 'd': False}
 JOINT = False
 
@@ -438,20 +448,19 @@
 
     places = [tuple(range(RING // 2)), tuple(range(RING // 2, RING))]
     kept, sent, sums, firsts, ends, blocks = {}, {}, {}, {}, {}, {}
-    kept["d"], sent["d"], ordered, masked = down_call(
-        table, pre_act, places[0], lengths, layer_input, cotangent
-    )
+    kept["d"], sent["d"], masked = down_call(table, pre_act, places[0], lengths, cotangent)
     kept["e"], sent["e"] = down_call(table, pre_act, places[1], masked=masked)
-    split = pre_act.shape[1] // 4 * SPLIT
+    split = pre_act.shape[1] // 8 * SPLIT
 
     def core(name):
         if name == "a":
-            kept[name], sent[name] = up_call(
-                wait("ka", ordered), masked, pre_act, down_weight, 0, split
+            kept[name], sent[name], sent["x"] = up_call(
+                table, layer_input, None, wait("ka", masked), pre_act, down_weight, 0, split
             )
         if name == "b":
             kept[name], sent[name] = up_call(
-                wait("kb", ordered), masked, pre_act, down_weight, split, pre_act.shape[1] - split
+                table, layer_input, wait("kb", sent["x"]), masked, pre_act, down_weight,
+                split, pre_act.shape[1] - split,
             )
         return inner_permute(wait(name + "0", sent[name]), core_route())
 

time: 209 us -> 208 us (level)
  waiting for transfers between devices: 56.3 us -> 49.4 us
  other arithmetic: 31.1 us -> 33.8 us
    ppermute x37, waiting for transfers between devices: 45.6 us -> 41.8 us  [inner_permute(): return lax.ppermute(block, 'inner', route)]
    ppermute x6, waiting for transfers between devices: 10.7 us -> 7.59 us  [across_replicas(): lax.ppermute(block, 'rep', replica_route(-step))]
    pallas_call x2, Pallas kernels: 24.1 us -> 26.8 us  [up_call(): pl.pallas_call(first_up_kernel if is_first else up_kernel, grid_spec=pltp...]
  transfers between devices with their start and end apart: 47 -> 47, of which waited for: 22 -> 24; matrix products, arithmetic and copies ran while one was open for 15% -> 16% of each run, Pallas kernels for 17% -> 18%
where the time goes in v4:
time: 208 us; the launch traced here: 207 us
  starting transfers between devices  68.6 us (33%)
  Pallas kernels  50.3 us (24%)
  waiting for transfers between devices  49.4 us (24%)
  other arithmetic  33.8 us (16%)
  local copies, waits for them, and re-layouts  3.98 us (2%)
    ppermute x37, starting transfers between devices, inner_permute(): return lax.ppermute(block, 'inner', route)  51.7 us
    ppermute x37, waiting for transfers between devices, inner_permute(): return lax.ppermute(block, 'inner', route)  41.8 us
    pallas_call x2, Pallas kernels, up_call(): pl.pallas_call(first_up_kernel if is_first else up_kernel, grid_spec=pltp...  26.8 us
    pallas_call x2, Pallas kernels, down_call(): pl.pallas_call(first_down_kernel if is_first else down_kernel, grid_spec=...  19.8 us
    ppermute x6, starting transfers between devices, across_replicas(): lax.ppermute(block, 'rep', replica_route(-step))  10.5 us
    ppermute x6, waiting for transfers between devices, across_replicas(): lax.ppermute(block, 'rep', replica_route(-step))  7.59 us
    add x4, other arithmetic, core_sum(): return lambda k, h: keep[k, h] + other[k, h]  7.32 us
    add x5, other arithmetic, ring_pass(): piece(3, 1) + from_ahead[0]  6.79 us
  transfers between devices with their start and end apart: 47, of which 24 were waited for; matrix products, arithmetic and copies ran while one was open for 16% of the time, Pallas kernels for 18%

profile of v4, /device:TPU:0, one launch (start us, length us, event | category | flops | bytes accessed | tf_op | source)
XLA Modules:
  0.0 207.3 jit_solution(15905003352181376106)
XLA Ops:
  1.4 10.3 %down_partial.2 = (f32[4,2,2,64,1024]{4,3,2,1,0:T(8,128)}, f32[4,2,2,64,1024]{4,3,2,1,0:T(8,128)}, bf16[1024,1024]{1,0:T(8,128)(2,1)}) custom-call(s32[32]{0:T(128)} %reshape.827.blocks_ref, s32[8]{0:T(128)} %lengths_ref.1, bf16[1024,1024]{1,0:T(8,128)(2,1)} %cotangent_ref.1, bf16[1024,4096]{1,0:T(8,128)(2,1)} %pre_ref.3, bf16[1024,4096]{1,0:T(8,128)(2,1)} %pre_ref.3, ...), custom_call_target="tpu_custom_call" | custom-call | flops 4294967296 | bytes 16777216 | tf_op jit(solution)/shard_map/down_partial/pallas_call | solution.py:186
  11.7 9.5 %down_partial.3 = (f32[4,2,2,64,1024]{4,3,2,1,0:T(8,128)}, f32[4,2,2,64,1024]{4,3,2,1,0:T(8,128)}) custom-call(s32[32]{0:T(128)} %reshape.827.blocks_ref, bf16[1024,1024]{1,0:T(8,128)(2,1)} %get-tuple-element.44.masked_ref, bf16[1024,4096]{1,0:T(8,128)(2,1)} %pre_ref.3, bf16[1024,4096]{1,0:T(8,128)(2,1)} %pre_ref.3, bf16[1024,4096]{1,0:T(8,128)(2,1)} %pre_ref.3, ...), custom_call_target="tpu_custom_call" | custom-call | flops 4294967296 | bytes 16777216 | tf_op jit(solution)/shard_map/down_partial/pallas_call | solution.py:186
  21.7 3.6 %slice_add_fusion.25 = (f32[1,1,2,64,1024]{4,3,2,1,0:T(8,128)S(1)}, f32[1,1,2,64,1024]{4,3,2,1,0:T(8,128)S(1)}, f32[1,2,64,1024]{3,2,1,0:T(8,128)S(1)}, f32[1,2,...) fusion(f32[4,2,2,64,1024]{4,3,2,1,0:T(8,128)} %collective-permute-done, ...), kind=kLoop, calls=%fused_computation.63 | loop fusion | flops 786432 | bytes 9437184 | tf_op jit(solution)/shard_map/add | solution.py:101
  35.8 2.8 %collective-permute-start.5 = (f32[2,2,64,1024]{3,2,1,0:T(8,128)}, f32[2,2,64,1024]{3,2,1,0:T(8,128)}, u32[]{:S(2)}, u32[]{:S(2)}) collective-permute-start(f32[2,2,64,1024]{3,2,1,0:T(8,128)} %pad_maximum_fusion.3), channel_id=1, source_target_pairs={{0,96},{4,28},{8,104},{12,4},{16,112},{20,12},{24,120},{28,20},{32... | collective-permute-start | bytes 3145736 | tf_op jit(solution)/shard_map/ppermute | solution.py:52
  40.3 14.1 %up_partial.2 = (f32[512,2048]{1,0:T(8,128)S(1)}, f32[512,2048]{1,0:T(8,128)}, bf16[1024,1024]{1,0:T(8,128)(2,1)S(1)}) custom-call(s32[64]{0:T(128)S(1)} %mul.69.rows_ref, bf16[1024,1024]{1,0:T(8,128)(2,1)S(1)} %copy-done.1, bf16[1024,1024]{1,0:T(8,128)(2,1)S(1)} %copy-done, bf16[1024,4096]{1,0:T(8,128)(2,1)} %pre_ref.3, bf16[4096,1024]{1,0:T(8,128)(2,1)} %weight_ref.3), custom_call_target="tpu_custom_call" | custom-call | flops 8589934592 | bytes 20971520 | tf_op jit(solution)/shard_map/up_partial/pallas_call | solution.py:257
  57.8 2.9 %collective-permute-start.20 = (f32[2,64,1024]{2,1,0:T(8,128)S(1)}, f32[2,64,1024]{2,1,0:T(8,128)S(1)}, u32[]{:S(2)}, u32[]{:S(2)}) collective-permute-start(f32[2,64,1024]{2,1,0:T(8,128)S(1)} %get-tuple-element.114), channel_id=1, source_target_pairs={{0,96},{4,28},{8,104},{12,4},{16,112},{20,12},{24,120},{28,20},{32... | collective-permute-start | bytes 1572872 | tf_op jit(solution)/shard_map/ppermute | solution.py:52
  64.7 2.8 %collective-permute-start.7 = (f32[2,4,16,2048]{3,2,1,0:T(8,128)}, f32[2,4,16,2048]{3,2,1,0:T(8,128)}, u32[]{:S(2)}, u32[]{:S(2)}) collective-permute-start(f32[2,4,16,2048]{3,2,1,0:T(8,128)} %pad_maximum_fusion.4), channel_id=1, source_target_pairs={{0,96},{4,28},{8,104},{12,4},{16,112},{20,12},{24,120},{28,20},{32... | collective-permute-start | bytes 3145736 | tf_op jit(solution)/shard_map/ppermute | solution.py:52
  68.7 3.2 %bitcast_add_fusion = (f32[2,64,1024]{2,1,0:T(8,128)}, f32[2,64,1024]{2,1,0:T(8,128)}) fusion(f32[2,2,64,1024]{3,2,1,0:T(8,128)} %collective-permute-done.2, f32[4,2,2,64,1024]{4,3,2,1,0:T(8,128)} %collective-permute-done, f32[4,2,2,64,1024]{4,3,2,1,0:T(8,128)} %get-tuple-element.47, f32[2,2,64,1024]{3,2,1,0:T(8,128)} %collective-permute-done.1), kind=kLoop, calls=%fused_computation.60 | loop fusion | flops 524288 | bytes 4194304 | tf_op jit(solution)/shard_map/add | solution.py:66
  71.9 3.2 %collective-permute-start.33 = (f32[2,64,1024]{2,1,0:T(8,128)}, f32[2,64,1024]{2,1,0:T(8,128)S(1)}, u32[]{:S(2)}, u32[]{:S(2)}) collective-permute-start(f32[2,64,1024]{2,1,0:T(8,128)} %get-tuple-element.116), channel_id=1, source_target_pairs={{0,96},{4,28},{8,104},{12,4},{16,112},{20,12},{24,120},{28,20},{32... | collective-permute-start | bytes 1572872 | tf_op jit(solution)/shard_map/ppermute | solution.py:52
  76.7 12.6 %up_partial.3 = (f32[512,2048]{1,0:T(8,128)S(1)}, f32[512,2048]{1,0:T(8,128)S(1)}) custom-call(s32[64]{0:T(128)S(1)} %mul.69.rows_ref, bf16[1024,1024]{1,0:T(8,128)(2,1)S(1)} %get-tuple-element.66.ordered_ref, bf16[1024,1024]{1,0:T(8,128)(2,1)S(1)} %copy-done, bf16[1024,4096]{1,0:T(8,128)(2,1)} %pre_ref.3, bf16[4096,1024]{1,0:T(8,128)(2,1)} %weight_ref.3), custom_call_target="tpu_custom_call" | custom-call | flops 8589934592 | bytes 20971520 | tf_op jit(solution)/shard_map/up_partial/pallas_call | solution.py:257
  100.5 3.7 %collective-permute-start.35 = (f32[2,64,1024]{2,1,0:T(8,128)S(1)}, f32[2,64,1024]{2,1,0:T(8,128)S(1)}, u32[]{:S(2)}, u32[]{:S(2)}) collective-permute-start(f32[2,64,1024]{2,1,0:T(8,128)S(1)} %pad_maximum_fusion.9), channel_id=1, source_target_pairs={{0,16},{4,68},{8,24},{12,76},{16,0},{20,84},{24,8},{28,92},{32,48}... | collective-permute-start | bytes 1572872 | tf_op jit(solution)/shard_map/ppermute | solution.py:52
  107.6 2.9 %collective-permute-done.9 = f32[4,16,2048]{2,1,0:T(8,128)S(1)} collective-permute-done((f32[4,16,2048]{2,1,0:T(8,128)S(1)}, f32[4,16,2048]{2,1,0:T(8,128)S(1)}, u32[]{:S(2)}, u32[]{:S(2)}) %collective-permute-start.9) | collective-permute-done | bytes 524320 | tf_op jit(solution)/shard_map/ppermute | solution.py:52
  111.6 3.6 %collective-permute-start.12 = (f32[2,16,2048]{2,1,0:T(8,128)S(1)}, f32[2,16,2048]{2,1,0:T(8,128)S(1)}, u32[]{:S(2)}, u32[]{:S(2)}) collective-permute-start(f32[2,16,2048]{2,1,0:T(8,128)S(1)} %pad_maximum_fusion.13), channel_id=1, source_target_pairs={{0,8},{4,36},{8,16},{12,44},{16,24},{20,52},{24,0},{28,60},{32,40}... | collective-permute-start | bytes 786440 | tf_op jit(solution)/shard_map/ppermute | solution.py:52
  116.9 3.2 %collective-permute-done.36 = f32[2,64,1024]{2,1,0:T(8,128)S(1)} collective-permute-done((f32[2,64,1024]{2,1,0:T(8,128)S(1)}, f32[2,64,1024]{2,1,0:T(8,128)S(1)}, u32[]{:S(2)}, u32[]{:S(2)}) %collective-permute-start.36) | collective-permute-done | bytes 524320 | tf_op jit(solution)/shard_map/ppermute | solution.py:52
  125.5 4.6 %collective-permute-start.22 = (f32[2,4,16,2048]{3,2,1,0:T(8,128)S(1)}, f32[2,4,16,2048]{3,2,1,0:T(8,128)S(1)}, u32[]{:S(2)}, u32[]{:S(2)}) collective-permute-start(f32[2,4,16,2048]{3,2,1,0:T(8,128)S(1)} %pad_maximum_fusion.6), channel_id=1, source_target_pairs={{0,96},{4,28},{8,104},{12,4},{16,112},{20,12},{24,120},{28,20},{32... | collective-permute-start | bytes 3145736 | tf_op jit(solution)/shard_map/ppermute | solution.py:52
  139.0 2.8 %collective-permute-start.37 = (f32[128,1024]{1,0:T(8,128)S(1)}, f32[128,1024]{1,0:T(8,128)S(1)}, u32[]{:S(2)}, u32[]{:S(2)}) collective-permute-start(f32[128,1024]{1,0:T(8,128)S(1)} %pad_maximum_fusion.11.refs_0_.refs_8_), channel_id=1, source_target_pairs={{0,3},{1,0},{2,1},{3,2},{4,7},{5,4},{6,5},{7,6},{8,11},{9,8},{10,9... | collective-permute-start | bytes 1572872 | tf_op jit(solution)/shard_map/ppermute | solution.py:307
  142.5 3.9 %collective-permute-done.23 = f32[2,4,16,2048]{3,2,1,0:T(8,128)S(1)} collective-permute-done((f32[2,4,16,2048]{3,2,1,0:T(8,128)S(1)}, f32[2,4,16,2048]{3,2,1,0:T(8,128)S(1)}, u32[]{:S(2)}, u32[]{:S(2)}) %collective-permute-start.23) | collective-permute-done | bytes 1048608 | tf_op jit(solution)/shard_map/ppermute | solution.py:52
  149.6 6.2 %collective-permute-done.25 = f32[4,16,2048]{2,1,0:T(8,128)S(1)} collective-permute-done((f32[4,16,2048]{2,1,0:T(8,128)S(1)}, f32[4,16,2048]{2,1,0:T(8,128)S(1)}, u32[]{:S(2)}, u32[]{:S(2)}) %collective-permute-start.25) | collective-permute-done | bytes 524320 | tf_op jit(solution)/shard_map/ppermute | solution.py:52
  157.3 2.8 %collective-permute-start.15 = (f32[32,2048]{1,0:T(8,128)S(1)}, f32[32,2048]{1,0:T(8,128)S(1)}, u32[]{:S(2)}, u32[]{:S(2)}) collective-permute-start(f32[32,2048]{1,0:T(8,128)S(1)} %pad_maximum_fusion.14.refs_0_), channel_id=1, source_target_pairs={{0,3},{1,0},{2,1},{3,2},{4,7},{5,4},{6,5},{7,6},{8,11},{9,8},{10,9... | collective-permute-start | bytes 786440 | tf_op jit(solution)/shard_map/ppermute | solution.py:290
  162.4 3.3 %collective-permute-start.27 = (f32[2,16,2048]{2,1,0:T(8,128)}, f32[2,16,2048]{2,1,0:T(8,128)}, u32[]{:S(2)}, u32[]{:S(2)}) collective-permute-start(f32[2,16,2048]{2,1,0:T(8,128)} %pad_maximum_fusion.16), channel_id=1, source_target_pairs={{0,16},{4,68},{8,24},{12,76},{16,0},{20,84},{24,8},{28,92},{32,48}... | collective-permute-start | bytes 786440 | tf_op jit(solution)/shard_map/ppermute | solution.py:52
  170.3 2.9 %collective-permute-done.27 = f32[2,16,2048]{2,1,0:T(8,128)} collective-permute-done((f32[2,16,2048]{2,1,0:T(8,128)}, f32[2,16,2048]{2,1,0:T(8,128)}, u32[]{:S(2)}, u32[]{:S(2)}) %collective-permute-start.27) | collective-permute-done | bytes 262176 | tf_op jit(solution)/shard_map/ppermute | solution.py:52
  179.5 6.9 %collective-permute-done.31.refs_3_.refs_7_ = f32[32,2048]{1,0:T(8,128)S(1)} collective-permute-done((f32[32,2048]{1,0:T(8,128)S(1)}, f32[32,2048]{1,0:T(8,128)S(1)}, u32[]{:S(2)}, u32[]{:S(2)}) %collective-permute-start.31) | collective-permute-done | bytes 262176 | tf_op jit(solution)/shard_map/ppermute | solution.py:307
  194.2 3.2 %collective-permute-done.41 = f32[3,16,128]{2,1,0:T(8,128)S(1)} collective-permute-done((f32[3,16,128]{2,1,0:T(8,128)S(1)}, f32[3,16,128]{2,1,0:T(8,128)S(1)}, u32[]{:S(2)}, u32[]{:S(2)}) %collective-permute-start.41) | collective-permute-done | bytes 24608 | tf_op jit(solution)/shard_map/ppermute | solution.py:52
  201.4 3.5 %collective-permute-done.45 = f32[3,16,128]{2,1,0:T(8,128)S(1)} collective-permute-done((f32[3,16,128]{2,1,0:T(8,128)S(1)}, f32[3,16,128]{2,1,0:T(8,128)S(1)}, u32[]{:S(2)}, u32[]{:S(2)}) %collective-permute-start.45) | collective-permute-done | bytes 24608 | tf_op jit(solution)/shard_map/ppermute | solution.py:52
  (167 shorter events, 87.5 us)
Async XLA Ops:
  26.5 28.0 %collective-permute-start.1 = (f32[2,2,64,1024]{3,2,1,0:T(8,128)}, f32[2,2,64,1024]{3,2,1,0:T(8,128)}, u32[]{:S(2)}, u32[]{:S(2)}) collective-permute-start(f32[2,2,64,1024]{3,2,1,0:T(8,128)} %pad_maximum_fusion), channel_id=1, source_target_pairs={{0,32},{4,12},{8,40},{12,20},{16,48},{20,28},{24,56},{28,4},{32,64... | collective-permute-start | bytes 3145736 | tf_op jit(solution)/shard_map/ppermute | solution.py:52
  29.3 25.2 %collective-permute-start.2 = (f32[2,2,64,1024]{3,2,1,0:T(8,128)}, f32[2,2,64,1024]{3,2,1,0:T(8,128)}, u32[]{:S(2)}, u32[]{:S(2)}) collective-permute-start(f32[2,2,64,1024]{3,2,1,0:T(8,128)} %pad_maximum_fusion.1), channel_id=1, source_target_pairs={{0,96},{4,28},{8,104},{12,4},{16,112},{20,12},{24,120},{28,20},{32... | collective-permute-start | bytes 3145736 | tf_op jit(solution)/shard_map/ppermute | solution.py:52
  34.3 20.2 %collective-permute-start.4 = (f32[2,2,64,1024]{3,2,1,0:T(8,128)}, f32[2,2,64,1024]{3,2,1,0:T(8,128)}, u32[]{:S(2)}, u32[]{:S(2)}) collective-permute-start(f32[2,2,64,1024]{3,2,1,0:T(8,128)} %pad_maximum_fusion.2), channel_id=1, source_target_pairs={{0,32},{4,12},{8,40},{12,20},{16,48},{20,28},{24,56},{28,4},{32,64... | collective-permute-start | bytes 3145736 | tf_op jit(solution)/shard_map/ppermute | solution.py:52
  35.8 19.8 %collective-permute-start.5 = (f32[2,2,64,1024]{3,2,1,0:T(8,128)}, f32[2,2,64,1024]{3,2,1,0:T(8,128)}, u32[]{:S(2)}, u32[]{:S(2)}) collective-permute-start(f32[2,2,64,1024]{3,2,1,0:T(8,128)} %pad_maximum_fusion.3), channel_id=1, source_target_pairs={{0,96},{4,28},{8,104},{12,4},{16,112},{20,12},{24,120},{28,20},{32... | collective-permute-start | bytes 3145736 | tf_op jit(solution)/shard_map/ppermute | solution.py:52
  57.8 17.3 %collective-permute-start.20 = (f32[2,64,1024]{2,1,0:T(8,128)S(1)}, f32[2,64,1024]{2,1,0:T(8,128)S(1)}, u32[]{:S(2)}, u32[]{:S(2)}) collective-permute-start(f32[2,64,1024]{2,1,0:T(8,128)S(1)} %get-tuple-element.114), channel_id=1, source_target_pairs={{0,96},{4,28},{8,104},{12,4},{16,112},{20,12},{24,120},{28,20},{32... | collective-permute-start | bytes 1572872 | tf_op jit(solution)/shard_map/ppermute | solution.py:52
  60.7 14.4 %collective-permute-start.19 = (f32[2,64,1024]{2,1,0:T(8,128)S(1)}, f32[2,64,1024]{2,1,0:T(8,128)S(1)}, u32[]{:S(2)}, u32[]{:S(2)}) collective-permute-start(f32[2,64,1024]{2,1,0:T(8,128)S(1)} %get-tuple-element.115), channel_id=1, source_target_pairs={{0,32},{4,12},{8,40},{12,20},{16,48},{20,28},{24,56},{28,4},{32,64... | collective-permute-start | bytes 1572872 | tf_op jit(solution)/shard_map/ppermute | solution.py:52
  64.7 24.6 %collective-permute-start.7 = (f32[2,4,16,2048]{3,2,1,0:T(8,128)}, f32[2,4,16,2048]{3,2,1,0:T(8,128)}, u32[]{:S(2)}, u32[]{:S(2)}) collective-permute-start(f32[2,4,16,2048]{3,2,1,0:T(8,128)} %pad_maximum_fusion.4), channel_id=1, source_target_pairs={{0,96},{4,28},{8,104},{12,4},{16,112},{20,12},{24,120},{28,20},{32... | collective-permute-start | bytes 3145736 | tf_op jit(solution)/shard_map/ppermute | solution.py:52
  68.7 20.7 %collective-permute-start.8 = (f32[2,4,16,2048]{3,2,1,0:T(8,128)}, f32[2,4,16,2048]{3,2,1,0:T(8,128)S(1)}, u32[]{:S(2)}, u32[]{:S(2)}) collective-permute-start(f32[2,4,16,2048]{3,2,1,0:T(8,128)} %pad_maximum_fusion.5), channel_id=1, source_target_pairs={{0,32},{4,12},{8,40},{12,20},{16,48},{20,28},{24,56},{28,4},{32,64... | collective-permute-start | bytes 3145736 | tf_op jit(solution)/shard_map/ppermute | solution.py:52
  71.9 18.1 %collective-permute-start.33 = (f32[2,64,1024]{2,1,0:T(8,128)}, f32[2,64,1024]{2,1,0:T(8,128)S(1)}, u32[]{:S(2)}, u32[]{:S(2)}) collective-permute-start(f32[2,64,1024]{2,1,0:T(8,128)} %get-tuple-element.116), channel_id=1, source_target_pairs={{0,96},{4,28},{8,104},{12,4},{16,112},{20,12},{24,120},{28,20},{32... | collective-permute-start | bytes 1572872 | tf_op jit(solution)/shard_map/ppermute | solution.py:52
  75.1 15.5 %collective-permute-start.32 = (f32[2,64,1024]{2,1,0:T(8,128)}, f32[2,64,1024]{2,1,0:T(8,128)}, u32[]{:S(2)}, u32[]{:S(2)}) collective-permute-start(f32[2,64,1024]{2,1,0:T(8,128)} %get-tuple-element.117), channel_id=1, source_target_pairs={{0,32},{4,12},{8,40},{12,20},{16,48},{20,28},{24,56},{28,4},{32,64... | collective-permute-start | bytes 1572872 | tf_op jit(solution)/shard_map/ppermute | solution.py:52
  89.4 35.3 %collective-permute-start.21 = (f32[4,2,4,16,2048]{4,3,2,1,0:T(8,128)S(1)}, f32[4,2,4,16,2048]{4,3,2,1,0:T(8,128)S(1)}, u32[]{:S(2)}, u32[]{:S(2)}) collective-permute-start(f32[4,2,4,16,2048]{4,3,2,1,0:T(8,128)S(1)} %bitcast.409), channel_id=1, source_target_pairs={{0,4},{4,0},{8,12},{12,8},{16,20},{20,16},{24,28},{28,24},{32,36},... | collective-permute-start | bytes 12582920 | tf_op jit(solution)/shard_map/ppermute | solution.py:52
  92.8 22.4 %collective-permute-start.34 = (f32[2,64,1024]{2,1,0:T(8,128)S(1)}, f32[2,64,1024]{2,1,0:T(8,128)S(1)}, u32[]{:S(2)}, u32[]{:S(2)}) collective-permute-start(f32[2,64,1024]{2,1,0:T(8,128)S(1)} %pad_maximum_fusion.8), channel_id=1, source_target_pairs={{0,8},{4,36},{8,16},{12,44},{16,24},{20,52},{24,0},{28,60},{32,40}... | collective-permute-start | bytes 1572872 | tf_op jit(solution)/shard_map/ppermute | solution.py:52
  97.8 12.7 %collective-permute-start.9 = (f32[4,16,2048]{2,1,0:T(8,128)S(1)}, f32[4,16,2048]{2,1,0:T(8,128)S(1)}, u32[]{:S(2)}, u32[]{:S(2)}) collective-permute-start(f32[4,16,2048]{2,1,0:T(8,128)S(1)} %get-tuple-element.87), channel_id=1, source_target_pairs={{0,32},{4,12},{8,40},{12,20},{16,48},{20,28},{24,56},{28,4},{32,64... | collective-permute-start | bytes 1572872 | tf_op jit(solution)/shard_map/ppermute | solution.py:52
  100.5 16.4 %collective-permute-start.35 = (f32[2,64,1024]{2,1,0:T(8,128)S(1)}, f32[2,64,1024]{2,1,0:T(8,128)S(1)}, u32[]{:S(2)}, u32[]{:S(2)}) collective-permute-start(f32[2,64,1024]{2,1,0:T(8,128)S(1)} %pad_maximum_fusion.9), channel_id=1, source_target_pairs={{0,16},{4,68},{8,24},{12,76},{16,0},{20,84},{24,8},{28,92},{32,48}... | collective-permute-start | bytes 1572872 | tf_op jit(solution)/shard_map/ppermute | solution.py:52
  106.2 13.9 %collective-permute-start.36 = (f32[2,64,1024]{2,1,0:T(8,128)S(1)}, f32[2,64,1024]{2,1,0:T(8,128)S(1)}, u32[]{:S(2)}, u32[]{:S(2)}) collective-permute-start(f32[2,64,1024]{2,1,0:T(8,128)S(1)} %pad_maximum_fusion.10), channel_id=1, source_target_pairs={{0,24},{4,100},{8,0},{12,108},{16,8},{20,116},{24,16},{28,124},{32... | collective-permute-start | bytes 1572872 | tf_op jit(solution)/shard_map/ppermute | solution.py:52
  122.9 11.4 %collective-permute-start.14 = (f32[16,2048]{1,0:T(8,128)S(1)}, f32[16,2048]{1,0:T(8,128)S(1)}, u32[]{:S(2)}, u32[]{:S(2)}) collective-permute-start(f32[16,2048]{1,0:T(8,128)S(1)} %fusion.70), channel_id=1, source_target_pairs={{0,24},{4,100},{8,0},{12,108},{16,8},{20,116},{24,16},{28,124},{32... | collective-permute-start | bytes 393224 | tf_op jit(solution)/shard_map/ppermute | solution.py:52
  125.5 17.0 %collective-permute-start.22 = (f32[2,4,16,2048]{3,2,1,0:T(8,128)S(1)}, f32[2,4,16,2048]{3,2,1,0:T(8,128)S(1)}, u32[]{:S(2)}, u32[]{:S(2)}) collective-permute-start(f32[2,4,16,2048]{3,2,1,0:T(8,128)S(1)} %pad_maximum_fusion.6), channel_id=1, source_target_pairs={{0,96},{4,28},{8,104},{12,4},{16,112},{20,12},{24,120},{28,20},{32... | collective-permute-start | bytes 3145736 | tf_op jit(solution)/shard_map/ppermute | solution.py:52
  130.2 16.1 %collective-permute-start.23 = (f32[2,4,16,2048]{3,2,1,0:T(8,128)S(1)}, f32[2,4,16,2048]{3,2,1,0:T(8,128)S(1)}, u32[]{:S(2)}, u32[]{:S(2)}) collective-permute-start(f32[2,4,16,2048]{3,2,1,0:T(8,128)S(1)} %pad_maximum_fusion.7), channel_id=1, source_target_pairs={{0,32},{4,12},{8,40},{12,20},{16,48},{20,28},{24,56},{28,4},{32,64... | collective-permute-start | bytes 3145736 | tf_op jit(solution)/shard_map/ppermute | solution.py:52
  132.8 29.6 %collective-permute-start.39 = (f32[128,1024]{1,0:T(8,128)S(1)}, f32[128,1024]{1,0:T(8,128)S(1)}, u32[]{:S(2)}, u32[]{:S(2)}) collective-permute-start(f32[128,1024]{1,0:T(8,128)S(1)} %pad_maximum_fusion.11.refs_0_.refs_8_), channel_id=1, source_target_pairs={{0,1},{1,2},{2,3},{3,0},{4,5},{5,6},{6,7},{7,4},{8,9},{9,10},{10,1... | collective-permute-start | bytes 1572872 | tf_op jit(solution)/shard_map/ppermute | solution.py:307
  134.3 28.1 %collective-permute-start.38 = (f32[128,1024]{1,0:T(8,128)S(1)}, f32[128,1024]{1,0:T(8,128)S(1)}, u32[]{:S(2)}, u32[]{:S(2)}) collective-permute-start(f32[128,1024]{1,0:T(8,128)S(1)} %pad_maximum_fusion.11.refs_0_.refs_8_), channel_id=1, source_target_pairs={{0,2},{1,3},{2,0},{3,1},{4,6},{5,7},{6,4},{7,5},{8,10},{9,11},{10,... | collective-permute-start | bytes 1572872 | tf_op jit(solution)/shard_map/ppermute | solution.py:307
  139.0 26.8 %collective-permute-start.37 = (f32[128,1024]{1,0:T(8,128)S(1)}, f32[128,1024]{1,0:T(8,128)S(1)}, u32[]{:S(2)}, u32[]{:S(2)}) collective-permute-start(f32[128,1024]{1,0:T(8,128)S(1)} %pad_maximum_fusion.11.refs_0_.refs_8_), channel_id=1, source_target_pairs={{0,3},{1,0},{2,1},{3,2},{4,7},{5,4},{6,5},{7,6},{8,11},{9,8},{10,9... | collective-permute-start | bytes 1572872 | tf_op jit(solution)/shard_map/ppermute | solution.py:307
  155.7 11.8 %collective-permute-start.16 = (f32[32,2048]{1,0:T(8,128)S(1)}, f32[32,2048]{1,0:T(8,128)S(1)}, u32[]{:S(2)}, u32[]{:S(2)}) collective-permute-start(f32[32,2048]{1,0:T(8,128)S(1)} %pad_maximum_fusion.14.refs_0_), channel_id=1, source_target_pairs={{0,1},{1,2},{2,3},{3,0},{4,5},{5,6},{6,7},{7,4},{8,9},{9,10},{10,1... | collective-permute-start | bytes 786440 | tf_op jit(solution)/shard_map/ppermute | solution.py:290
  167.6 11.4 %collective-permute-start.18 = (f32[16,2048]{1,0:T(8,128)S(1)}, f32[16,2048]{1,0:T(8,128)S(1)}, u32[]{:S(2)}, u32[]{:S(2)}) collective-permute-start(f32[16,2048]{1,0:T(8,128)S(1)} %slice.713), channel_id=1, source_target_pairs={{0,3},{1,0},{2,1},{3,2},{4,7},{5,4},{6,5},{7,6},{8,11},{9,8},{10,9... | collective-permute-start | bytes 393224 | tf_op jit(solution)/shard_map/ppermute | solution.py:298
  175.5 10.9 %collective-permute-start.31 = (f32[32,2048]{1,0:T(8,128)S(1)}, f32[32,2048]{1,0:T(8,128)S(1)}, u32[]{:S(2)}, u32[]{:S(2)}) collective-permute-start(f32[32,2048]{1,0:T(8,128)S(1)} %pad_maximum_fusion.18.refs_0_.refs_4_), channel_id=1, source_target_pairs={{0,1},{1,2},{2,3},{3,0},{4,5},{5,6},{6,7},{7,4},{8,9},{9,10},{10,1... | collective-permute-start | bytes 786440 | tf_op jit(solution)/shard_map/ppermute | solution.py:307
  (40 other events, 352.2 us)

commit v5 on v4

--- a/solution.py
+++ b/solution.py
@@ -193,7 +193,7 @@
             out_specs=[out_block, out_block] + extra,
         ),
         out_shape=out_shape,
-        compiler_params=pltpu.CompilerParams(vmem_limit_bytes=60 * MIB),
+        compiler_params=pltpu.CompilerParams(vmem_limit_bytes=24 * MIB),
         cost_estimate=pl.CostEstimate(
             flops=2 * tokens * width * rows * RING * count,
             bytes_accessed=4 * tokens * width + (2 * tokens + 4 * width) * rows * RING * count,
@@ -269,9 +269,9 @@
             scratch_shapes=[pltpu.VMEM((width, tokens), jnp.bfloat16)] * is_first,
         ),
         out_shape=out_shape,
-        compiler_params=pltpu.CompilerParams(vmem_limit_bytes=40 * MIB),
+        compiler_params=pltpu.CompilerParams(vmem_limit_bytes=34 * MIB),
         cost_estimate=pl.CostEstimate(
-            flops=4 * tokens * width * count,
+            flops=12 * tokens * width * count,
             bytes_accessed=4 * tokens * width + 2 * tokens * count + 6 * width * count,
             transcendentals=2 * tokens * count,
         ),
@@ -431,7 +431,7 @@
 
 
 ORDER = ['d0', 'd1', 'e0', 'e1', 'a0', 'd2', 'e2', 'a1', 'b0', 'a2', 'b1', 'a3', 'd3', 'd5', 'b2', 'a4', 'b3', 'a5', 'a6', 'b5']
-GATES = {'b0': ('a1',), 'a0': ('d1', 'e1'), 'kb': ('e2',)}
+GATES = {'a0': ('d1', 'e1'), 'kb': ('a0',), 'b5': ('a5', 'a3'), 'd2': ('e1',)}
 RINGS = {'a': True, 'b': False, 'd': False}
 SPLIT = 4
 FAR = {'a': True, 'b': False, 'd': False}

time: 208 us -> 205 us (0.986)
  other arithmetic: 33.8 us -> 26.3 us
  local copies, waits for them, and re-layouts: 3.98 us -> 8.74 us
  Pallas kernels: 50.3 us -> 46.5 us
  starting transfers between devices: 68.6 us -> 70.8 us
    unnamed x35 -> x41, local copies, waits for them, and re-layouts: 3.25 us -> 8.53 us
    another operation x5, other arithmetic: 3.43 us -> 0.4 us  [ring_start(): jnp.stack([piece(2, 1), piece(3, 0)])]
    another operation x5, other arithmetic: 3.4 us -> 0.39 us  [ring_start(): jnp.stack([piece(2, 0), piece(1, 1)])]
    pallas_call x2, Pallas kernels: 19.8 us -> 16.8 us  [down_call(): pl.pallas_call(first_down_kernel if is_first else down_kernel, grid_spec=...]
    ppermute x37, starting transfers between devices: 51.7 us -> 54 us  [inner_permute(): return lax.ppermute(block, 'inner', route)]
  transfers between devices with their start and end apart: 47 -> 47, of which waited for: 24 -> 20; matrix products, arithmetic and copies ran while one was open for 16% -> 13% of each run, Pallas kernels for 18% -> 17%
where the time goes in v5:
time: 205 us; the launch traced here: 204 us
  starting transfers between devices  70.8 us (35%)
  waiting for transfers between devices  50.8 us (25%)
  Pallas kernels  46.5 us (23%)
  other arithmetic  26.3 us (13%)
  local copies, waits for them, and re-layouts  8.74 us (4%)
    ppermute x37, starting transfers between devices, inner_permute(): return lax.ppermute(block, 'inner', route)  54 us
    ppermute x37, waiting for transfers between devices, inner_permute(): return lax.ppermute(block, 'inner', route)  42.6 us
    pallas_call x2, Pallas kernels, up_call(): pl.pallas_call(first_up_kernel if is_first else up_kernel, grid_spec=pltp...  26 us
    pallas_call x2, Pallas kernels, down_call(): pl.pallas_call(first_down_kernel if is_first else down_kernel, grid_spec=...  16.8 us
    ppermute x6, starting transfers between devices, across_replicas(): lax.ppermute(block, 'rep', replica_route(-step))  10.6 us
    unnamed x41, local copies, waits for them, and re-layouts  8.53 us
    ppermute x6, waiting for transfers between devices, across_replicas(): lax.ppermute(block, 'rep', replica_route(-step))  8.13 us
    add x4, other arithmetic, core_sum(): return lambda k, h: keep[k, h] + other[k, h]  7.86 us
  transfers between devices with their start and end apart: 47, of which 20 were waited for; matrix products, arithmetic and copies ran while one was open for 13% of the time, Pallas kernels for 17%

profile of v5, /device:TPU:0, one launch (start us, length us, event | category | flops | bytes accessed | tf_op | source)
XLA Modules:
  0.0 204.4 jit_solution(2174689653302668798)
XLA Ops:
  0.9 3.4 %copy-done = bf16[1024,4096]{1,0:T(8,128)(2,1)S(1)} copy-done((bf16[1024,4096]{1,0:T(8,128)(2,1)S(1)}, bf16[1024,4096]{1,0:T(8,128)(2,1)}, u32[]{:S(2)}) %copy-start) | copy-done | bytes 8388632
  6.5 8.6 %down_partial.2 = (f32[4,2,2,64,1024]{4,3,2,1,0:T(8,128)S(1)}, f32[4,2,2,64,1024]{4,3,2,1,0:T(8,128)}, bf16[1024,1024]{1,0:T(8,128)(2,1)S(1)}) custom-call(s32[32]{0:T(128)S(1)} %reshape.827.blocks_ref, s32[8]{0:T(128)S(1)} %copy-done.6, bf16[1024,1024]{1,0:T(8,128)(2,1)S(1)} %copy-done.5, bf16[1024,4096]{1,0:T(8,128)(2,1)S(1)} %copy-done, ...), custom_call_target="tpu_custom_call" | custom-call | flops 4294967296 | bytes 16777216 | tf_op jit(solution)/shard_map/down_partial/pallas_call | solution.py:186
  15.1 8.2 %down_partial.3 = (f32[4,2,2,64,1024]{4,3,2,1,0:T(8,128)S(1)}, f32[4,2,2,64,1024]{4,3,2,1,0:T(8,128)}) custom-call(s32[32]{0:T(128)S(1)} %reshape.827.blocks_ref, bf16[1024,1024]{1,0:T(8,128)(2,1)S(1)} %get-tuple-element.43.masked_ref, bf16[1024,4096]{1,0:T(8,128)(2,1)S(1)} %copy-done.1, bf16[1024,4096]{1,0:T(8,128)(2,1)S(1)} %copy-done.1, ...), custom_call_target="tpu_custom_call" | custom-call | flops 4294967296 | bytes 16777216 | tf_op jit(solution)/shard_map/down_partial/pallas_call | solution.py:186
  26.0 3.7 %slice_add_fusion.25 = (f32[1,1,2,64,1024]{4,3,2,1,0:T(8,128)S(1)}, f32[1,1,2,64,1024]{4,3,2,1,0:T(8,128)S(1)}, f32[1,2,64,1024]{3,2,1,0:T(8,128)S(1)}, f32[1,2,...) fusion(f32[4,2,2,64,1024]{4,3,2,1,0:T(8,128)} %collective-permute-done, ...), kind=kLoop, calls=%fused_computation.63 | loop fusion | flops 786432 | bytes 9437184 | tf_op jit(solution)/shard_map/add | solution.py:101
  33.3 2.8 %slice_add_fusion.1 = (f32[1,1,2,64,1024]{4,3,2,1,0:T(8,128)S(1)}, f32[1,1,2,64,1024]{4,3,2,1,0:T(8,128)S(1)}, f32[1,2,64,1024]{3,2,1,0:T(8,128)S(1)}, f32[1,2,6...) fusion(f32[4,2,2,64,1024]{4,3,2,1,0:T(8,128)} %collective-permute-done.3, ...), kind=kLoop, calls=%fused_computation.9 | loop fusion | flops 786432 | bytes 9437184 | tf_op jit(solution)/shard_map/add | solution.py:101
  39.8 13.4 %up_partial.2 = (f32[512,2048]{1,0:T(8,128)S(1)}, f32[512,2048]{1,0:T(8,128)S(1)}, bf16[1024,1024]{1,0:T(8,128)(2,1)S(1)}) custom-call(s32[64]{0:T(128)S(1)} %mul.69.rows_ref, bf16[1024,1024]{1,0:T(8,128)(2,1)S(1)} %copy-done.7, bf16[1024,1024]{1,0:T(8,128)(2,1)S(1)} %get-tuple-element.43.masked_ref, bf16[1024,4096]{1,0:T(8,128)(2,1)} %pre_ref.3, ...), custom_call_target="tpu_custom_call" | custom-call | flops 25769803776 | bytes 20971520 | tf_op jit(solution)/shard_map/up_partial/pallas_call | solution.py:257
  53.2 4.0 %collective-permute-done.4 = f32[2,2,64,1024]{3,2,1,0:T(8,128)S(1)} collective-permute-done((f32[2,2,64,1024]{3,2,1,0:T(8,128)S(1)}, f32[2,2,64,1024]{3,2,1,0:T(8,128)S(1)}, u32[]{:S(2)}, u32[]{:S(2)}) %collective-permute-start.4) | collective-permute-done | bytes 1048608 | tf_op jit(solution)/shard_map/ppermute | solution.py:52
  57.8 3.0 %bitcast_add_fusion = (f32[2,64,1024]{2,1,0:T(8,128)S(1)}, f32[2,64,1024]{2,1,0:T(8,128)}) fusion(f32[2,2,64,1024]{3,2,1,0:T(8,128)S(1)} %collective-permute-done.2, f32[4,2,2,64,1024]{4,3,2,1,0:T(8,128)} %collective-permute-done, f32[4,2,2,64,1024]{4,3,2,1,0:T(8,128)} %copy-done.4, f32[2,2,64,1024]{3,2,1,0:T(8,128)S(1)} %collective-permute-done.1), kind=kLoop, calls=%fused_computation.60 | loop fusion | flops 524288 | bytes 4194304 | tf_op jit(solution)/shard_map/add | solution.py:66
  60.8 2.8 %collective-permute-start.31 = (f32[2,64,1024]{2,1,0:T(8,128)S(1)}, f32[2,64,1024]{2,1,0:T(8,128)S(1)}, u32[]{:S(2)}, u32[]{:S(2)}) collective-permute-start(f32[2,64,1024]{2,1,0:T(8,128)S(1)} %get-tuple-element.114), channel_id=1, source_target_pairs={{0,96},{4,28},{8,104},{12,4},{16,112},{20,12},{24,120},{28,20},{32... | collective-permute-start | bytes 1572872 | tf_op jit(solution)/shard_map/ppermute | solution.py:52
  66.1 3.4 %collective-permute-start.33 = (f32[2,64,1024]{2,1,0:T(8,128)}, f32[2,64,1024]{2,1,0:T(8,128)}, u32[]{:S(2)}, u32[]{:S(2)}) collective-permute-start(f32[2,64,1024]{2,1,0:T(8,128)} %get-tuple-element.112), channel_id=1, source_target_pairs={{0,96},{4,28},{8,104},{12,4},{16,112},{20,12},{24,120},{28,20},{32... | collective-permute-start | bytes 1572872 | tf_op jit(solution)/shard_map/ppermute | solution.py:52
  70.3 3.3 %collective-permute-start.7 = (f32[2,4,16,2048]{3,2,1,0:T(8,128)S(1)}, f32[2,4,16,2048]{3,2,1,0:T(8,128)S(1)}, u32[]{:S(2)}, u32[]{:S(2)}) collective-permute-start(f32[2,4,16,2048]{3,2,1,0:T(8,128)S(1)} %pad_maximum_fusion.4), channel_id=1, source_target_pairs={{0,96},{4,28},{8,104},{12,4},{16,112},{20,12},{24,120},{28,20},{32... | collective-permute-start | bytes 3145736 | tf_op jit(solution)/shard_map/ppermute | solution.py:52
  74.5 12.6 %up_partial.3 = (f32[512,2048]{1,0:T(8,128)S(1)}, f32[512,2048]{1,0:T(8,128)S(1)}) custom-call(s32[64]{0:T(128)S(1)} %mul.69.rows_ref, bf16[1024,1024]{1,0:T(8,128)(2,1)S(1)} %get-tuple-element.63.ordered_ref, bf16[1024,1024]{1,0:T(8,128)(2,1)S(1)} %get-tuple-element.43.masked_ref, bf16[1024,4096]{1,0:T(8,128)(2,1)} %pre_ref.3, bf16[4096,1024]{1,0:T(8,128)(2,1)} %weight_ref.3), custom_call_target="tpu_custom_call" | custom-call | flops 25769803776 | bytes 20971520 | tf_op jit(solution)/shard_map/up_partial/pallas_call | solution.py:257
  91.7 3.3 %collective-permute-start.10 = (f32[4,16,2048]{2,1,0:T(8,128)S(1)}, f32[4,16,2048]{2,1,0:T(8,128)S(1)}, u32[]{:S(2)}, u32[]{:S(2)}) collective-permute-start(f32[4,16,2048]{2,1,0:T(8,128)S(1)} %get-tuple-element.84), channel_id=1, source_target_pairs={{0,96},{4,28},{8,104},{12,4},{16,112},{20,12},{24,120},{28,20},{32... | collective-permute-start | bytes 1572872 | tf_op jit(solution)/shard_map/ppermute | solution.py:52
  97.4 3.6 %collective-permute-start.35 = (f32[2,64,1024]{2,1,0:T(8,128)S(1)}, f32[2,64,1024]{2,1,0:T(8,128)S(1)}, u32[]{:S(2)}, u32[]{:S(2)}) collective-permute-start(f32[2,64,1024]{2,1,0:T(8,128)S(1)} %pad_maximum_fusion.9), channel_id=1, source_target_pairs={{0,16},{4,68},{8,24},{12,76},{16,0},{20,84},{24,8},{28,92},{32,48}... | collective-permute-start | bytes 1572872 | tf_op jit(solution)/shard_map/ppermute | solution.py:52
  101.1 7.7 %collective-permute-done.10 = f32[4,16,2048]{2,1,0:T(8,128)S(1)} collective-permute-done((f32[4,16,2048]{2,1,0:T(8,128)S(1)}, f32[4,16,2048]{2,1,0:T(8,128)S(1)}, u32[]{:S(2)}, u32[]{:S(2)}) %collective-permute-start.10) | collective-permute-done | bytes 524320 | tf_op jit(solution)/shard_map/ppermute | solution.py:52
  113.4 4.7 %collective-permute-done.36 = f32[2,64,1024]{2,1,0:T(8,128)S(1)} collective-permute-done((f32[2,64,1024]{2,1,0:T(8,128)S(1)}, f32[2,64,1024]{2,1,0:T(8,128)S(1)}, u32[]{:S(2)}, u32[]{:S(2)}) %collective-permute-start.36) | collective-permute-done | bytes 524320 | tf_op jit(solution)/shard_map/ppermute | solution.py:52
  118.0 2.8 %collective-permute-done.11 = f32[2,16,2048]{2,1,0:T(8,128)S(1)} collective-permute-done((f32[2,16,2048]{2,1,0:T(8,128)S(1)}, f32[2,16,2048]{2,1,0:T(8,128)S(1)}, u32[]{:S(2)}, u32[]{:S(2)}) %collective-permute-start.11) | collective-permute-done | bytes 262176 | tf_op jit(solution)/shard_map/ppermute | solution.py:52
  123.3 3.8 %collective-permute-start.20 = (f32[2,4,16,2048]{3,2,1,0:T(8,128)S(1)}, f32[2,4,16,2048]{3,2,1,0:T(8,128)S(1)}, u32[]{:S(2)}, u32[]{:S(2)}) collective-permute-start(f32[2,4,16,2048]{3,2,1,0:T(8,128)S(1)} %pad_maximum_fusion.6), channel_id=1, source_target_pairs={{0,96},{4,28},{8,104},{12,4},{16,112},{20,12},{24,120},{28,20},{32... | collective-permute-start | bytes 3145736 | tf_op jit(solution)/shard_map/ppermute | solution.py:52
  135.9 2.7 %collective-permute-start.37 = (f32[128,1024]{1,0:T(8,128)S(1)}, f32[128,1024]{1,0:T(8,128)S(1)}, u32[]{:S(2)}, u32[]{:S(2)}) collective-permute-start(f32[128,1024]{1,0:T(8,128)S(1)} %pad_maximum_fusion.11.refs_0_.refs_8_), channel_id=1, source_target_pairs={{0,3},{1,0},{2,1},{3,2},{4,7},{5,4},{6,5},{7,6},{8,11},{9,8},{10,9... | collective-permute-start | bytes 1572872 | tf_op jit(solution)/shard_map/ppermute | solution.py:307
  139.4 3.8 %collective-permute-done.21 = f32[2,4,16,2048]{3,2,1,0:T(8,128)S(1)} collective-permute-done((f32[2,4,16,2048]{3,2,1,0:T(8,128)S(1)}, f32[2,4,16,2048]{3,2,1,0:T(8,128)S(1)}, u32[]{:S(2)}, u32[]{:S(2)}) %collective-permute-start.21) | collective-permute-done | bytes 1048608 | tf_op jit(solution)/shard_map/ppermute | solution.py:52
  146.7 6.2 %collective-permute-done.23 = f32[4,16,2048]{2,1,0:T(8,128)S(1)} collective-permute-done((f32[4,16,2048]{2,1,0:T(8,128)S(1)}, f32[4,16,2048]{2,1,0:T(8,128)S(1)}, u32[]{:S(2)}, u32[]{:S(2)}) %collective-permute-start.23) | collective-permute-done | bytes 524320 | tf_op jit(solution)/shard_map/ppermute | solution.py:52
  160.6 2.8 %collective-permute-start.25 = (f32[2,16,2048]{2,1,0:T(8,128)}, f32[2,16,2048]{2,1,0:T(8,128)}, u32[]{:S(2)}, u32[]{:S(2)}) collective-permute-start(f32[2,16,2048]{2,1,0:T(8,128)} %pad_maximum_fusion.16), channel_id=1, source_target_pairs={{0,16},{4,68},{8,24},{12,76},{16,0},{20,84},{24,8},{28,92},{32,48}... | collective-permute-start | bytes 786440 | tf_op jit(solution)/shard_map/ppermute | solution.py:52
  176.5 8.1 %collective-permute-done.29.refs_3_.refs_7_ = f32[32,2048]{1,0:T(8,128)S(1)} collective-permute-done((f32[32,2048]{1,0:T(8,128)S(1)}, f32[32,2048]{1,0:T(8,128)S(1)}, u32[]{:S(2)}, u32[]{:S(2)}) %collective-permute-start.29) | collective-permute-done | bytes 262176 | tf_op jit(solution)/shard_map/ppermute | solution.py:307
  191.7 3.2 %collective-permute-done.41 = f32[3,16,128]{2,1,0:T(8,128)S(1)} collective-permute-done((f32[3,16,128]{2,1,0:T(8,128)S(1)}, f32[3,16,128]{2,1,0:T(8,128)S(1)}, u32[]{:S(2)}, u32[]{:S(2)}) %collective-permute-start.41) | collective-permute-done | bytes 24608 | tf_op jit(solution)/shard_map/ppermute | solution.py:52
  (173 shorter events, 81.2 us)
Async XLA Ops:
  29.9 23.3 %collective-permute-start.1 = (f32[2,2,64,1024]{3,2,1,0:T(8,128)S(1)}, f32[2,2,64,1024]{3,2,1,0:T(8,128)S(1)}, u32[]{:S(2)}, u32[]{:S(2)}) collective-permute-start(f32[2,2,64,1024]{3,2,1,0:T(8,128)S(1)} %pad_maximum_fusion), channel_id=1, source_target_pairs={{0,32},{4,12},{8,40},{12,20},{16,48},{20,28},{24,56},{28,4},{32,64... | collective-permute-start | bytes 3145736 | tf_op jit(solution)/shard_map/ppermute | solution.py:52
  31.7 21.5 %collective-permute-start.2 = (f32[2,2,64,1024]{3,2,1,0:T(8,128)S(1)}, f32[2,2,64,1024]{3,2,1,0:T(8,128)S(1)}, u32[]{:S(2)}, u32[]{:S(2)}) collective-permute-start(f32[2,2,64,1024]{3,2,1,0:T(8,128)S(1)} %pad_maximum_fusion.1), channel_id=1, source_target_pairs={{0,96},{4,28},{8,104},{12,4},{16,112},{20,12},{24,120},{28,20},{32... | collective-permute-start | bytes 3145736 | tf_op jit(solution)/shard_map/ppermute | solution.py:52
  36.3 20.9 %collective-permute-start.4 = (f32[2,2,64,1024]{3,2,1,0:T(8,128)S(1)}, f32[2,2,64,1024]{3,2,1,0:T(8,128)S(1)}, u32[]{:S(2)}, u32[]{:S(2)}) collective-permute-start(f32[2,2,64,1024]{3,2,1,0:T(8,128)S(1)} %pad_maximum_fusion.2), channel_id=1, source_target_pairs={{0,32},{4,12},{8,40},{12,20},{16,48},{20,28},{24,56},{28,4},{32,64... | collective-permute-start | bytes 3145736 | tf_op jit(solution)/shard_map/ppermute | solution.py:52
  37.8 20.0 %collective-permute-start.5 = (f32[2,2,64,1024]{3,2,1,0:T(8,128)S(1)}, f32[2,2,64,1024]{3,2,1,0:T(8,128)S(1)}, u32[]{:S(2)}, u32[]{:S(2)}) collective-permute-start(f32[2,2,64,1024]{3,2,1,0:T(8,128)S(1)} %pad_maximum_fusion.3), channel_id=1, source_target_pairs={{0,96},{4,28},{8,104},{12,4},{16,112},{20,12},{24,120},{28,20},{32... | collective-permute-start | bytes 3145736 | tf_op jit(solution)/shard_map/ppermute | solution.py:52
  60.8 12.9 %collective-permute-start.31 = (f32[2,64,1024]{2,1,0:T(8,128)S(1)}, f32[2,64,1024]{2,1,0:T(8,128)S(1)}, u32[]{:S(2)}, u32[]{:S(2)}) collective-permute-start(f32[2,64,1024]{2,1,0:T(8,128)S(1)} %get-tuple-element.114), channel_id=1, source_target_pairs={{0,96},{4,28},{8,104},{12,4},{16,112},{20,12},{24,120},{28,20},{32... | collective-permute-start | bytes 1572872 | tf_op jit(solution)/shard_map/ppermute | solution.py:52
  63.6 23.5 %collective-permute-start.30 = (f32[2,64,1024]{2,1,0:T(8,128)}, f32[2,64,1024]{2,1,0:T(8,128)}, u32[]{:S(2)}, u32[]{:S(2)}) collective-permute-start(f32[2,64,1024]{2,1,0:T(8,128)} %get-tuple-element.115), channel_id=1, source_target_pairs={{0,32},{4,12},{8,40},{12,20},{16,48},{20,28},{24,56},{28,4},{32,64... | collective-permute-start | bytes 1572872 | tf_op jit(solution)/shard_map/ppermute | solution.py:52
  66.1 21.1 %collective-permute-start.33 = (f32[2,64,1024]{2,1,0:T(8,128)}, f32[2,64,1024]{2,1,0:T(8,128)}, u32[]{:S(2)}, u32[]{:S(2)}) collective-permute-start(f32[2,64,1024]{2,1,0:T(8,128)} %get-tuple-element.112), channel_id=1, source_target_pairs={{0,96},{4,28},{8,104},{12,4},{16,112},{20,12},{24,120},{28,20},{32... | collective-permute-start | bytes 1572872 | tf_op jit(solution)/shard_map/ppermute | solution.py:52
  69.5 17.7 %collective-permute-start.32 = (f32[2,64,1024]{2,1,0:T(8,128)}, f32[2,64,1024]{2,1,0:T(8,128)}, u32[]{:S(2)}, u32[]{:S(2)}) collective-permute-start(f32[2,64,1024]{2,1,0:T(8,128)} %get-tuple-element.113), channel_id=1, source_target_pairs={{0,32},{4,12},{8,40},{12,20},{16,48},{20,28},{24,56},{28,4},{32,64... | collective-permute-start | bytes 1572872 | tf_op jit(solution)/shard_map/ppermute | solution.py:52
  70.3 21.2 %collective-permute-start.7 = (f32[2,4,16,2048]{3,2,1,0:T(8,128)S(1)}, f32[2,4,16,2048]{3,2,1,0:T(8,128)S(1)}, u32[]{:S(2)}, u32[]{:S(2)}) collective-permute-start(f32[2,4,16,2048]{3,2,1,0:T(8,128)S(1)} %pad_maximum_fusion.4), channel_id=1, source_target_pairs={{0,96},{4,28},{8,104},{12,4},{16,112},{20,12},{24,120},{28,20},{32... | collective-permute-start | bytes 3145736 | tf_op jit(solution)/shard_map/ppermute | solution.py:52
  74.5 17.0 %collective-permute-start.8 = (f32[2,4,16,2048]{3,2,1,0:T(8,128)S(1)}, f32[2,4,16,2048]{3,2,1,0:T(8,128)S(1)}, u32[]{:S(2)}, u32[]{:S(2)}) collective-permute-start(f32[2,4,16,2048]{3,2,1,0:T(8,128)S(1)} %pad_maximum_fusion.5), channel_id=1, source_target_pairs={{0,32},{4,12},{8,40},{12,20},{16,48},{20,28},{24,56},{28,4},{32,64... | collective-permute-start | bytes 3145736 | tf_op jit(solution)/shard_map/ppermute | solution.py:52
  87.1 35.4 %collective-permute-start.19 = (f32[4,2,4,16,2048]{4,3,2,1,0:T(8,128)S(1)}, f32[4,2,4,16,2048]{4,3,2,1,0:T(8,128)S(1)}, u32[]{:S(2)}, u32[]{:S(2)}) collective-permute-start(f32[4,2,4,16,2048]{4,3,2,1,0:T(8,128)S(1)} %bitcast.409), channel_id=1, source_target_pairs={{0,4},{4,0},{8,12},{12,8},{16,20},{20,16},{24,28},{28,24},{32,36},... | collective-permute-start | bytes 12582920 | tf_op jit(solution)/shard_map/ppermute | solution.py:52
  89.5 21.6 %collective-permute-start.34 = (f32[2,64,1024]{2,1,0:T(8,128)S(1)}, f32[2,64,1024]{2,1,0:T(8,128)S(1)}, u32[]{:S(2)}, u32[]{:S(2)}) collective-permute-start(f32[2,64,1024]{2,1,0:T(8,128)S(1)} %pad_maximum_fusion.8), channel_id=1, source_target_pairs={{0,8},{4,36},{8,16},{12,44},{16,24},{20,52},{24,0},{28,60},{32,40}... | collective-permute-start | bytes 1572872 | tf_op jit(solution)/shard_map/ppermute | solution.py:52
  91.7 17.1 %collective-permute-start.10 = (f32[4,16,2048]{2,1,0:T(8,128)S(1)}, f32[4,16,2048]{2,1,0:T(8,128)S(1)}, u32[]{:S(2)}, u32[]{:S(2)}) collective-permute-start(f32[4,16,2048]{2,1,0:T(8,128)S(1)} %get-tuple-element.84), channel_id=1, source_target_pairs={{0,96},{4,28},{8,104},{12,4},{16,112},{20,12},{24,120},{28,20},{32... | collective-permute-start | bytes 1572872 | tf_op jit(solution)/shard_map/ppermute | solution.py:52
  95.0 13.8 %collective-permute-start.9 = (f32[4,16,2048]{2,1,0:T(8,128)S(1)}, f32[4,16,2048]{2,1,0:T(8,128)S(1)}, u32[]{:S(2)}, u32[]{:S(2)}) collective-permute-start(f32[4,16,2048]{2,1,0:T(8,128)S(1)} %get-tuple-element.85), channel_id=1, source_target_pairs={{0,32},{4,12},{8,40},{12,20},{16,48},{20,28},{24,56},{28,4},{32,64... | collective-permute-start | bytes 1572872 | tf_op jit(solution)/shard_map/ppermute | solution.py:52
  97.4 16.0 %collective-permute-start.35 = (f32[2,64,1024]{2,1,0:T(8,128)S(1)}, f32[2,64,1024]{2,1,0:T(8,128)S(1)}, u32[]{:S(2)}, u32[]{:S(2)}) collective-permute-start(f32[2,64,1024]{2,1,0:T(8,128)S(1)} %pad_maximum_fusion.9), channel_id=1, source_target_pairs={{0,16},{4,68},{8,24},{12,76},{16,0},{20,84},{24,8},{28,92},{32,48}... | collective-permute-start | bytes 1572872 | tf_op jit(solution)/shard_map/ppermute | solution.py:52
  123.3 16.1 %collective-permute-start.20 = (f32[2,4,16,2048]{3,2,1,0:T(8,128)S(1)}, f32[2,4,16,2048]{3,2,1,0:T(8,128)S(1)}, u32[]{:S(2)}, u32[]{:S(2)}) collective-permute-start(f32[2,4,16,2048]{3,2,1,0:T(8,128)S(1)} %pad_maximum_fusion.6), channel_id=1, source_target_pairs={{0,96},{4,28},{8,104},{12,4},{16,112},{20,12},{24,120},{28,20},{32... | collective-permute-start | bytes 3145736 | tf_op jit(solution)/shard_map/ppermute | solution.py:52
  127.2 16.1 %collective-permute-start.21 = (f32[2,4,16,2048]{3,2,1,0:T(8,128)S(1)}, f32[2,4,16,2048]{3,2,1,0:T(8,128)S(1)}, u32[]{:S(2)}, u32[]{:S(2)}) collective-permute-start(f32[2,4,16,2048]{3,2,1,0:T(8,128)S(1)} %pad_maximum_fusion.7), channel_id=1, source_target_pairs={{0,32},{4,12},{8,40},{12,20},{16,48},{20,28},{24,56},{28,4},{32,64... | collective-permute-start | bytes 3145736 | tf_op jit(solution)/shard_map/ppermute | solution.py:52
  130.8 28.6 %collective-permute-start.39 = (f32[128,1024]{1,0:T(8,128)S(1)}, f32[128,1024]{1,0:T(8,128)S(1)}, u32[]{:S(2)}, u32[]{:S(2)}) collective-permute-start(f32[128,1024]{1,0:T(8,128)S(1)} %pad_maximum_fusion.11.refs_0_.refs_8_), channel_id=1, source_target_pairs={{0,1},{1,2},{2,3},{3,0},{4,5},{5,6},{6,7},{7,4},{8,9},{9,10},{10,1... | collective-permute-start | bytes 1572872 | tf_op jit(solution)/shard_map/ppermute | solution.py:307
  132.4 28.2 %collective-permute-start.38 = (f32[128,1024]{1,0:T(8,128)S(1)}, f32[128,1024]{1,0:T(8,128)S(1)}, u32[]{:S(2)}, u32[]{:S(2)}) collective-permute-start(f32[128,1024]{1,0:T(8,128)S(1)} %pad_maximum_fusion.11.refs_0_.refs_8_), channel_id=1, source_target_pairs={{0,2},{1,3},{2,0},{3,1},{4,6},{5,7},{6,4},{7,5},{8,10},{9,11},{10,... | collective-permute-start | bytes 1572872 | tf_op jit(solution)/shard_map/ppermute | solution.py:307
  135.9 27.5 %collective-permute-start.37 = (f32[128,1024]{1,0:T(8,128)S(1)}, f32[128,1024]{1,0:T(8,128)S(1)}, u32[]{:S(2)}, u32[]{:S(2)}) collective-permute-start(f32[128,1024]{1,0:T(8,128)S(1)} %pad_maximum_fusion.11.refs_0_.refs_8_), channel_id=1, source_target_pairs={{0,3},{1,0},{2,1},{3,2},{4,7},{5,4},{6,5},{7,6},{8,11},{9,8},{10,9... | collective-permute-start | bytes 1572872 | tf_op jit(solution)/shard_map/ppermute | solution.py:307
  152.9 13.3 %collective-permute-start.16 = (f32[32,2048]{1,0:T(8,128)S(1)}, f32[32,2048]{1,0:T(8,128)S(1)}, u32[]{:S(2)}, u32[]{:S(2)}) collective-permute-start(f32[32,2048]{1,0:T(8,128)S(1)} %pad_maximum_fusion.14.refs_0_), channel_id=1, source_target_pairs={{0,1},{1,2},{2,3},{3,0},{4,5},{5,6},{6,7},{7,4},{8,9},{9,10},{10,1... | collective-permute-start | bytes 786440 | tf_op jit(solution)/shard_map/ppermute | solution.py:290
  154.4 11.8 %collective-permute-start.15 = (f32[32,2048]{1,0:T(8,128)S(1)}, f32[32,2048]{1,0:T(8,128)S(1)}, u32[]{:S(2)}, u32[]{:S(2)}) collective-permute-start(f32[32,2048]{1,0:T(8,128)S(1)} %pad_maximum_fusion.14.refs_0_), channel_id=1, source_target_pairs={{0,3},{1,0},{2,1},{3,2},{4,7},{5,4},{6,5},{7,6},{8,11},{9,8},{10,9... | collective-permute-start | bytes 786440 | tf_op jit(solution)/shard_map/ppermute | solution.py:290
  172.5 12.1 %collective-permute-start.29 = (f32[32,2048]{1,0:T(8,128)S(1)}, f32[32,2048]{1,0:T(8,128)S(1)}, u32[]{:S(2)}, u32[]{:S(2)}) collective-permute-start(f32[32,2048]{1,0:T(8,128)S(1)} %pad_maximum_fusion.18.refs_0_.refs_4_), channel_id=1, source_target_pairs={{0,1},{1,2},{2,3},{3,0},{4,5},{5,6},{6,7},{7,4},{8,9},{9,10},{10,1... | collective-permute-start | bytes 786440 | tf_op jit(solution)/shard_map/ppermute | solution.py:307
  172.6 12.0 %collective-permute-start.28 = (f32[32,2048]{1,0:T(8,128)S(1)}, f32[32,2048]{1,0:T(8,128)S(1)}, u32[]{:S(2)}, u32[]{:S(2)}) collective-permute-start(f32[32,2048]{1,0:T(8,128)S(1)} %pad_maximum_fusion.18.refs_0_.refs_4_), channel_id=1, source_target_pairs={{0,2},{1,3},{2,0},{3,1},{4,6},{5,7},{6,4},{7,5},{8,10},{9,11},{10,... | collective-permute-start | bytes 786440 | tf_op jit(solution)/shard_map/ppermute | solution.py:307
  (43 other events, 357.8 us)

commit v6 on v5

--- a/solution.py
+++ b/solution.py
@@ -193,7 +193,7 @@
             out_specs=[out_block, out_block] + extra,
         ),
         out_shape=out_shape,
-        compiler_params=pltpu.CompilerParams(vmem_limit_bytes=24 * MIB),
+        compiler_params=pltpu.CompilerParams(vmem_limit_bytes=60 * MIB),
         cost_estimate=pl.CostEstimate(
             flops=2 * tokens * width * rows * RING * count,
             bytes_accessed=4 * tokens * width + (2 * tokens + 4 * width) * rows * RING * count,

time: 205 us -> 200 us (0.976)
  local copies, waits for them, and re-layouts: 8.74 us -> 2.09 us
  other arithmetic: 26.3 us -> 22.3 us
  Pallas kernels: 46.5 us -> 49.6 us
  waiting for transfers between devices: 50.8 us -> 53.9 us
    unnamed x41 -> x27, local copies, waits for them, and re-layouts: 8.53 us -> 1.37 us
    ppermute x37, waiting for transfers between devices: 42.6 us -> 45.7 us  [inner_permute(): return lax.ppermute(block, 'inner', route)]
    pallas_call x2, Pallas kernels: 16.8 us -> 19.8 us  [down_call(): pl.pallas_call(first_down_kernel if is_first else down_kernel, grid_spec=...]
  transfers between devices with their start and end apart: 47 -> 47, of which waited for: 20 -> 19; matrix products, arithmetic and copies ran while one was open for 13% -> 11% of each run, Pallas kernels for 17% -> 18%
where the time goes in v6:
time: 200 us; the launch traced here: 199 us
  starting transfers between devices  70.1 us (35%)
  waiting for transfers between devices  53.9 us (27%)
  Pallas kernels  49.6 us (25%)
  other arithmetic  22.3 us (11%)
  local copies, waits for them, and re-layouts  2.09 us (1%)
    ppermute x37, starting transfers between devices, inner_permute(): return lax.ppermute(block, 'inner', route)  53.3 us
    ppermute x37, waiting for transfers between devices, inner_permute(): return lax.ppermute(block, 'inner', route)  45.7 us
    pallas_call x2, Pallas kernels, up_call(): pl.pallas_call(first_up_kernel if is_first else up_kernel, grid_spec=pltp...  26 us
    pallas_call x2, Pallas kernels, down_call(): pl.pallas_call(first_down_kernel if is_first else down_kernel, grid_spec=...  19.8 us
    ppermute x6, starting transfers between devices, across_replicas(): lax.ppermute(block, 'rep', replica_route(-step))  10.6 us
    ppermute x6, waiting for transfers between devices, across_replicas(): lax.ppermute(block, 'rep', replica_route(-step))  8.12 us
    add x4, other arithmetic, core_sum(): return lambda k, h: keep[k, h] + other[k, h]  7.86 us
    add x5, other arithmetic, ring_pass(): piece(3, 1) + from_ahead[0]  6.74 us
  transfers between devices with their start and end apart: 47, of which 19 were waited for; matrix products, arithmetic and copies ran while one was open for 11% of the time, Pallas kernels for 18%

profile of v6, /device:TPU:0, one launch (start us, length us, event | category | flops | bytes accessed | tf_op | source)
XLA Modules:
  0.0 199.2 jit_solution(15433008790851978361)
XLA Ops:
  1.4 10.3 %down_partial.2 = (f32[4,2,2,64,1024]{4,3,2,1,0:T(8,128)}, f32[4,2,2,64,1024]{4,3,2,1,0:T(8,128)}, bf16[1024,1024]{1,0:T(8,128)(2,1)}) custom-call(s32[32]{0:T(128)} %reshape.827.blocks_ref, s32[8]{0:T(128)} %lengths_ref.1, bf16[1024,1024]{1,0:T(8,128)(2,1)} %cotangent_ref.1, bf16[1024,4096]{1,0:T(8,128)(2,1)} %pre_ref.3, bf16[1024,4096]{1,0:T(8,128)(2,1)} %pre_ref.3, ...), custom_call_target="tpu_custom_call" | custom-call | flops 4294967296 | bytes 16777216 | tf_op jit(solution)/shard_map/down_partial/pallas_call | solution.py:186
  11.7 9.5 %down_partial.3 = (f32[4,2,2,64,1024]{4,3,2,1,0:T(8,128)}, f32[4,2,2,64,1024]{4,3,2,1,0:T(8,128)}) custom-call(s32[32]{0:T(128)} %reshape.827.blocks_ref, bf16[1024,1024]{1,0:T(8,128)(2,1)} %get-tuple-element.43.masked_ref, bf16[1024,4096]{1,0:T(8,128)(2,1)} %pre_ref.3, bf16[1024,4096]{1,0:T(8,128)(2,1)} %pre_ref.3, bf16[1024,4096]{1,0:T(8,128)(2,1)} %pre_ref.3, ...), custom_call_target="tpu_custom_call" | custom-call | flops 4294967296 | bytes 16777216 | tf_op jit(solution)/shard_map/down_partial/pallas_call | solution.py:186
  21.9 3.7 %slice_add_fusion.25 = (f32[1,1,2,64,1024]{4,3,2,1,0:T(8,128)S(1)}, f32[1,1,2,64,1024]{4,3,2,1,0:T(8,128)S(1)}, f32[1,2,64,1024]{3,2,1,0:T(8,128)S(1)}, f32[1,2,...) fusion(f32[4,2,2,64,1024]{4,3,2,1,0:T(8,128)} %collective-permute-done, ...), kind=kLoop, calls=%fused_computation.63 | loop fusion | flops 786432 | bytes 9437184 | tf_op jit(solution)/shard_map/add | solution.py:101
  29.2 2.8 %slice_add_fusion.1 = (f32[1,1,2,64,1024]{4,3,2,1,0:T(8,128)S(1)}, f32[1,1,2,64,1024]{4,3,2,1,0:T(8,128)S(1)}, f32[1,2,64,1024]{3,2,1,0:T(8,128)S(1)}, f32[1,2,6...) fusion(f32[4,2,2,64,1024]{4,3,2,1,0:T(8,128)} %collective-permute-done.3, ...), kind=kLoop, calls=%fused_computation.9 | loop fusion | flops 786432 | bytes 9437184 | tf_op jit(solution)/shard_map/add | solution.py:101
  35.6 13.4 %up_partial.2 = (f32[512,2048]{1,0:T(8,128)S(1)}, f32[512,2048]{1,0:T(8,128)S(1)}, bf16[1024,1024]{1,0:T(8,128)(2,1)S(1)}) custom-call(s32[64]{0:T(128)S(1)} %mul.69.rows_ref, bf16[1024,1024]{1,0:T(8,128)(2,1)S(1)} %copy-done.1, bf16[1024,1024]{1,0:T(8,128)(2,1)S(1)} %copy-done, bf16[1024,4096]{1,0:T(8,128)(2,1)} %pre_ref.3, bf16[4096,1024]{1,0:T(8,128)(2,1)} %weight_ref.3), custom_call_target="tpu_custom_call" | custom-call | flops 25769803776 | bytes 20971520 | tf_op jit(solution)/shard_map/up_partial/pallas_call | solution.py:257
  49.0 4.0 %collective-permute-done.4 = f32[2,2,64,1024]{3,2,1,0:T(8,128)S(1)} collective-permute-done((f32[2,2,64,1024]{3,2,1,0:T(8,128)S(1)}, f32[2,2,64,1024]{3,2,1,0:T(8,128)S(1)}, u32[]{:S(2)}, u32[]{:S(2)}) %collective-permute-start.4) | collective-permute-done | bytes 1048608 | tf_op jit(solution)/shard_map/ppermute | solution.py:52
  53.7 2.7 %bitcast_add_fusion = (f32[2,64,1024]{2,1,0:T(8,128)S(1)}, f32[2,64,1024]{2,1,0:T(8,128)}) fusion(f32[2,2,64,1024]{3,2,1,0:T(8,128)S(1)} %collective-permute-done.2, f32[4,2,2,64,1024]{4,3,2,1,0:T(8,128)} %collective-permute-done, f32[4,2,2,64,1024]{4,3,2,1,0:T(8,128)} %get-tuple-element.46, f32[2,2,64,1024]{3,2,1,0:T(8,128)S(1)} %collective-permute-done.1), kind=kLoop, calls=%fused_computation.60 | loop fusion | flops 524288 | bytes 4194304 | tf_op jit(solution)/shard_map/add | solution.py:66
  56.3 2.8 %collective-permute-start.31 = (f32[2,64,1024]{2,1,0:T(8,128)S(1)}, f32[2,64,1024]{2,1,0:T(8,128)S(1)}, u32[]{:S(2)}, u32[]{:S(2)}) collective-permute-start(f32[2,64,1024]{2,1,0:T(8,128)S(1)} %get-tuple-element.114), channel_id=1, source_target_pairs={{0,96},{4,28},{8,104},{12,4},{16,112},{20,12},{24,120},{28,20},{32... | collective-permute-start | bytes 1572872 | tf_op jit(solution)/shard_map/ppermute | solution.py:52
  61.6 3.2 %collective-permute-start.33 = (f32[2,64,1024]{2,1,0:T(8,128)}, f32[2,64,1024]{2,1,0:T(8,128)}, u32[]{:S(2)}, u32[]{:S(2)}) collective-permute-start(f32[2,64,1024]{2,1,0:T(8,128)} %get-tuple-element.112), channel_id=1, source_target_pairs={{0,96},{4,28},{8,104},{12,4},{16,112},{20,12},{24,120},{28,20},{32... | collective-permute-start | bytes 1572872 | tf_op jit(solution)/shard_map/ppermute | solution.py:52
  66.9 3.3 %collective-permute-start.7 = (f32[2,4,16,2048]{3,2,1,0:T(8,128)S(1)}, f32[2,4,16,2048]{3,2,1,0:T(8,128)S(1)}, u32[]{:S(2)}, u32[]{:S(2)}) collective-permute-start(f32[2,4,16,2048]{3,2,1,0:T(8,128)S(1)} %pad_maximum_fusion.4), channel_id=1, source_target_pairs={{0,96},{4,28},{8,104},{12,4},{16,112},{20,12},{24,120},{28,20},{32... | collective-permute-start | bytes 3145736 | tf_op jit(solution)/shard_map/ppermute | solution.py:52
  70.4 12.6 %up_partial.3 = (f32[512,2048]{1,0:T(8,128)S(1)}, f32[512,2048]{1,0:T(8,128)S(1)}) custom-call(s32[64]{0:T(128)S(1)} %mul.69.rows_ref, bf16[1024,1024]{1,0:T(8,128)(2,1)S(1)} %get-tuple-element.63.ordered_ref, bf16[1024,1024]{1,0:T(8,128)(2,1)S(1)} %copy-done, bf16[1024,4096]{1,0:T(8,128)(2,1)} %pre_ref.3, bf16[4096,1024]{1,0:T(8,128)(2,1)} %weight_ref.3), custom_call_target="tpu_custom_call" | custom-call | flops 25769803776 | bytes 20971520 | tf_op jit(solution)/shard_map/up_partial/pallas_call | solution.py:257
  92.5 4.0 %collective-permute-start.35 = (f32[2,64,1024]{2,1,0:T(8,128)S(1)}, f32[2,64,1024]{2,1,0:T(8,128)S(1)}, u32[]{:S(2)}, u32[]{:S(2)}) collective-permute-start(f32[2,64,1024]{2,1,0:T(8,128)S(1)} %pad_maximum_fusion.9), channel_id=1, source_target_pairs={{0,16},{4,68},{8,24},{12,76},{16,0},{20,84},{24,8},{28,92},{32,48}... | collective-permute-start | bytes 1572872 | tf_op jit(solution)/shard_map/ppermute | solution.py:52
  96.6 6.0 %collective-permute-done.10 = f32[4,16,2048]{2,1,0:T(8,128)S(1)} collective-permute-done((f32[4,16,2048]{2,1,0:T(8,128)S(1)}, f32[4,16,2048]{2,1,0:T(8,128)S(1)}, u32[]{:S(2)}, u32[]{:S(2)}) %collective-permute-start.10) | collective-permute-done | bytes 524320 | tf_op jit(solution)/shard_map/ppermute | solution.py:52
  104.0 2.6 %collective-permute-start.12 = (f32[2,16,2048]{2,1,0:T(8,128)S(1)}, f32[2,16,2048]{2,1,0:T(8,128)S(1)}, u32[]{:S(2)}, u32[]{:S(2)}) collective-permute-start(f32[2,16,2048]{2,1,0:T(8,128)S(1)} %pad_maximum_fusion.13), channel_id=1, source_target_pairs={{0,8},{4,36},{8,16},{12,44},{16,24},{20,52},{24,0},{28,60},{32,40}... | collective-permute-start | bytes 786440 | tf_op jit(solution)/shard_map/ppermute | solution.py:52
  108.3 4.3 %collective-permute-done.36 = f32[2,64,1024]{2,1,0:T(8,128)S(1)} collective-permute-done((f32[2,64,1024]{2,1,0:T(8,128)S(1)}, f32[2,64,1024]{2,1,0:T(8,128)S(1)}, u32[]{:S(2)}, u32[]{:S(2)}) %collective-permute-start.36) | collective-permute-done | bytes 524320 | tf_op jit(solution)/shard_map/ppermute | solution.py:52
  112.6 2.8 %collective-permute-done.11 = f32[2,16,2048]{2,1,0:T(8,128)S(1)} collective-permute-done((f32[2,16,2048]{2,1,0:T(8,128)S(1)}, f32[2,16,2048]{2,1,0:T(8,128)S(1)}, u32[]{:S(2)}, u32[]{:S(2)}) %collective-permute-start.11) | collective-permute-done | bytes 262176 | tf_op jit(solution)/shard_map/ppermute | solution.py:52
  118.4 3.8 %collective-permute-start.20 = (f32[2,4,16,2048]{3,2,1,0:T(8,128)S(1)}, f32[2,4,16,2048]{3,2,1,0:T(8,128)S(1)}, u32[]{:S(2)}, u32[]{:S(2)}) collective-permute-start(f32[2,4,16,2048]{3,2,1,0:T(8,128)S(1)} %pad_maximum_fusion.6), channel_id=1, source_target_pairs={{0,96},{4,28},{8,104},{12,4},{16,112},{20,12},{24,120},{28,20},{32... | collective-permute-start | bytes 3145736 | tf_op jit(solution)/shard_map/ppermute | solution.py:52
  125.5 2.7 %collective-permute-start.38 = (f32[128,1024]{1,0:T(8,128)S(1)}, f32[128,1024]{1,0:T(8,128)S(1)}, u32[]{:S(2)}, u32[]{:S(2)}) collective-permute-start(f32[128,1024]{1,0:T(8,128)S(1)} %pad_maximum_fusion.11.refs_0_.refs_8_), channel_id=1, source_target_pairs={{0,2},{1,3},{2,0},{3,1},{4,6},{5,7},{6,4},{7,5},{8,10},{9,11},{10,... | collective-permute-start | bytes 1572872 | tf_op jit(solution)/shard_map/ppermute | solution.py:307
  130.0 2.8 %collective-permute-start.37 = (f32[128,1024]{1,0:T(8,128)S(1)}, f32[128,1024]{1,0:T(8,128)S(1)}, u32[]{:S(2)}, u32[]{:S(2)}) collective-permute-start(f32[128,1024]{1,0:T(8,128)S(1)} %pad_maximum_fusion.11.refs_0_.refs_8_), channel_id=1, source_target_pairs={{0,3},{1,0},{2,1},{3,2},{4,7},{5,4},{6,5},{7,6},{8,11},{9,8},{10,9... | collective-permute-start | bytes 1572872 | tf_op jit(solution)/shard_map/ppermute | solution.py:307
  134.4 3.8 %collective-permute-done.21 = f32[2,4,16,2048]{3,2,1,0:T(8,128)S(1)} collective-permute-done((f32[2,4,16,2048]{3,2,1,0:T(8,128)S(1)}, f32[2,4,16,2048]{3,2,1,0:T(8,128)S(1)}, u32[]{:S(2)}, u32[]{:S(2)}) %collective-permute-start.21) | collective-permute-done | bytes 1048608 | tf_op jit(solution)/shard_map/ppermute | solution.py:52
  140.6 7.1 %collective-permute-done.23 = f32[4,16,2048]{2,1,0:T(8,128)S(1)} collective-permute-done((f32[4,16,2048]{2,1,0:T(8,128)S(1)}, f32[4,16,2048]{2,1,0:T(8,128)S(1)}, u32[]{:S(2)}, u32[]{:S(2)}) %collective-permute-start.23) | collective-permute-done | bytes 524320 | tf_op jit(solution)/shard_map/ppermute | solution.py:52
  155.2 2.8 %collective-permute-start.25 = (f32[2,16,2048]{2,1,0:T(8,128)}, f32[2,16,2048]{2,1,0:T(8,128)}, u32[]{:S(2)}, u32[]{:S(2)}) collective-permute-start(f32[2,16,2048]{2,1,0:T(8,128)} %pad_maximum_fusion.16), channel_id=1, source_target_pairs={{0,16},{4,68},{8,24},{12,76},{16,0},{20,84},{24,8},{28,92},{32,48}... | collective-permute-start | bytes 786440 | tf_op jit(solution)/shard_map/ppermute | solution.py:52
  171.3 8.1 %collective-permute-done.29.refs_3_.refs_7_ = f32[32,2048]{1,0:T(8,128)S(1)} collective-permute-done((f32[32,2048]{1,0:T(8,128)S(1)}, f32[32,2048]{1,0:T(8,128)S(1)}, u32[]{:S(2)}, u32[]{:S(2)}) %collective-permute-start.29) | collective-permute-done | bytes 262176 | tf_op jit(solution)/shard_map/ppermute | solution.py:307
  186.1 3.5 %collective-permute-done.41 = f32[3,16,128]{2,1,0:T(8,128)S(1)} collective-permute-done((f32[3,16,128]{2,1,0:T(8,128)S(1)}, f32[3,16,128]{2,1,0:T(8,128)S(1)}, u32[]{:S(2)}, u32[]{:S(2)}) %collective-permute-start.41) | collective-permute-done | bytes 24608 | tf_op jit(solution)/shard_map/ppermute | solution.py:52
  (159 shorter events, 75.2 us)
Async XLA Ops:
  25.7 23.3 %collective-permute-start.1 = (f32[2,2,64,1024]{3,2,1,0:T(8,128)S(1)}, f32[2,2,64,1024]{3,2,1,0:T(8,128)S(1)}, u32[]{:S(2)}, u32[]{:S(2)}) collective-permute-start(f32[2,2,64,1024]{3,2,1,0:T(8,128)S(1)} %pad_maximum_fusion), channel_id=1, source_target_pairs={{0,32},{4,12},{8,40},{12,20},{16,48},{20,28},{24,56},{28,4},{32,64... | collective-permute-start | bytes 3145736 | tf_op jit(solution)/shard_map/ppermute | solution.py:52
  27.5 21.5 %collective-permute-start.2 = (f32[2,2,64,1024]{3,2,1,0:T(8,128)S(1)}, f32[2,2,64,1024]{3,2,1,0:T(8,128)S(1)}, u32[]{:S(2)}, u32[]{:S(2)}) collective-permute-start(f32[2,2,64,1024]{3,2,1,0:T(8,128)S(1)} %pad_maximum_fusion.1), channel_id=1, source_target_pairs={{0,96},{4,28},{8,104},{12,4},{16,112},{20,12},{24,120},{28,20},{32... | collective-permute-start | bytes 3145736 | tf_op jit(solution)/shard_map/ppermute | solution.py:52
  32.1 20.9 %collective-permute-start.4 = (f32[2,2,64,1024]{3,2,1,0:T(8,128)S(1)}, f32[2,2,64,1024]{3,2,1,0:T(8,128)S(1)}, u32[]{:S(2)}, u32[]{:S(2)}) collective-permute-start(f32[2,2,64,1024]{3,2,1,0:T(8,128)S(1)} %pad_maximum_fusion.2), channel_id=1, source_target_pairs={{0,32},{4,12},{8,40},{12,20},{16,48},{20,28},{24,56},{28,4},{32,64... | collective-permute-start | bytes 3145736 | tf_op jit(solution)/shard_map/ppermute | solution.py:52
  33.6 20.1 %collective-permute-start.5 = (f32[2,2,64,1024]{3,2,1,0:T(8,128)S(1)}, f32[2,2,64,1024]{3,2,1,0:T(8,128)S(1)}, u32[]{:S(2)}, u32[]{:S(2)}) collective-permute-start(f32[2,2,64,1024]{3,2,1,0:T(8,128)S(1)} %pad_maximum_fusion.3), channel_id=1, source_target_pairs={{0,96},{4,28},{8,104},{12,4},{16,112},{20,12},{24,120},{28,20},{32... | collective-permute-start | bytes 3145736 | tf_op jit(solution)/shard_map/ppermute | solution.py:52
  56.3 14.0 %collective-permute-start.31 = (f32[2,64,1024]{2,1,0:T(8,128)S(1)}, f32[2,64,1024]{2,1,0:T(8,128)S(1)}, u32[]{:S(2)}, u32[]{:S(2)}) collective-permute-start(f32[2,64,1024]{2,1,0:T(8,128)S(1)} %get-tuple-element.114), channel_id=1, source_target_pairs={{0,96},{4,28},{8,104},{12,4},{16,112},{20,12},{24,120},{28,20},{32... | collective-permute-start | bytes 1572872 | tf_op jit(solution)/shard_map/ppermute | solution.py:52
  59.1 23.9 %collective-permute-start.30 = (f32[2,64,1024]{2,1,0:T(8,128)}, f32[2,64,1024]{2,1,0:T(8,128)S(1)}, u32[]{:S(2)}, u32[]{:S(2)}) collective-permute-start(f32[2,64,1024]{2,1,0:T(8,128)} %get-tuple-element.115), channel_id=1, source_target_pairs={{0,32},{4,12},{8,40},{12,20},{16,48},{20,28},{24,56},{28,4},{32,64... | collective-permute-start | bytes 1572872 | tf_op jit(solution)/shard_map/ppermute | solution.py:52
  61.6 21.9 %collective-permute-start.33 = (f32[2,64,1024]{2,1,0:T(8,128)}, f32[2,64,1024]{2,1,0:T(8,128)}, u32[]{:S(2)}, u32[]{:S(2)}) collective-permute-start(f32[2,64,1024]{2,1,0:T(8,128)} %get-tuple-element.112), channel_id=1, source_target_pairs={{0,96},{4,28},{8,104},{12,4},{16,112},{20,12},{24,120},{28,20},{32... | collective-permute-start | bytes 1572872 | tf_op jit(solution)/shard_map/ppermute | solution.py:52
  64.8 18.7 %collective-permute-start.32 = (f32[2,64,1024]{2,1,0:T(8,128)}, f32[2,64,1024]{2,1,0:T(8,128)}, u32[]{:S(2)}, u32[]{:S(2)}) collective-permute-start(f32[2,64,1024]{2,1,0:T(8,128)} %get-tuple-element.113), channel_id=1, source_target_pairs={{0,32},{4,12},{8,40},{12,20},{16,48},{20,28},{24,56},{28,4},{32,64... | collective-permute-start | bytes 1572872 | tf_op jit(solution)/shard_map/ppermute | solution.py:52
  66.9 18.5 %collective-permute-start.7 = (f32[2,4,16,2048]{3,2,1,0:T(8,128)S(1)}, f32[2,4,16,2048]{3,2,1,0:T(8,128)S(1)}, u32[]{:S(2)}, u32[]{:S(2)}) collective-permute-start(f32[2,4,16,2048]{3,2,1,0:T(8,128)S(1)} %pad_maximum_fusion.4), channel_id=1, source_target_pairs={{0,96},{4,28},{8,104},{12,4},{16,112},{20,12},{24,120},{28,20},{32... | collective-permute-start | bytes 3145736 | tf_op jit(solution)/shard_map/ppermute | solution.py:52
  70.4 16.3 %collective-permute-start.8 = (f32[2,4,16,2048]{3,2,1,0:T(8,128)S(1)}, f32[2,4,16,2048]{3,2,1,0:T(8,128)S(1)}, u32[]{:S(2)}, u32[]{:S(2)}) collective-permute-start(f32[2,4,16,2048]{3,2,1,0:T(8,128)S(1)} %pad_maximum_fusion.5), channel_id=1, source_target_pairs={{0,32},{4,12},{8,40},{12,20},{16,48},{20,28},{24,56},{28,4},{32,64... | collective-permute-start | bytes 3145736 | tf_op jit(solution)/shard_map/ppermute | solution.py:52
  83.1 34.5 %collective-permute-start.19 = (f32[4,2,4,16,2048]{4,3,2,1,0:T(8,128)S(1)}, f32[4,2,4,16,2048]{4,3,2,1,0:T(8,128)S(1)}, u32[]{:S(2)}, u32[]{:S(2)}) collective-permute-start(f32[4,2,4,16,2048]{4,3,2,1,0:T(8,128)S(1)} %bitcast.409), channel_id=1, source_target_pairs={{0,4},{4,0},{8,12},{12,8},{16,20},{20,16},{24,28},{28,24},{32,36},... | collective-permute-start | bytes 12582920 | tf_op jit(solution)/shard_map/ppermute | solution.py:52
  83.7 22.9 %collective-permute-start.34 = (f32[2,64,1024]{2,1,0:T(8,128)S(1)}, f32[2,64,1024]{2,1,0:T(8,128)S(1)}, u32[]{:S(2)}, u32[]{:S(2)}) collective-permute-start(f32[2,64,1024]{2,1,0:T(8,128)S(1)} %pad_maximum_fusion.8), channel_id=1, source_target_pairs={{0,8},{4,36},{8,16},{12,44},{16,24},{20,52},{24,0},{28,60},{32,40}... | collective-permute-start | bytes 1572872 | tf_op jit(solution)/shard_map/ppermute | solution.py:52
  88.1 14.5 %collective-permute-start.10 = (f32[4,16,2048]{2,1,0:T(8,128)S(1)}, f32[4,16,2048]{2,1,0:T(8,128)S(1)}, u32[]{:S(2)}, u32[]{:S(2)}) collective-permute-start(f32[4,16,2048]{2,1,0:T(8,128)S(1)} %get-tuple-element.84), channel_id=1, source_target_pairs={{0,96},{4,28},{8,104},{12,4},{16,112},{20,12},{24,120},{28,20},{32... | collective-permute-start | bytes 1572872 | tf_op jit(solution)/shard_map/ppermute | solution.py:52
  90.1 13.8 %collective-permute-start.9 = (f32[4,16,2048]{2,1,0:T(8,128)S(1)}, f32[4,16,2048]{2,1,0:T(8,128)S(1)}, u32[]{:S(2)}, u32[]{:S(2)}) collective-permute-start(f32[4,16,2048]{2,1,0:T(8,128)S(1)} %get-tuple-element.85), channel_id=1, source_target_pairs={{0,32},{4,12},{8,40},{12,20},{16,48},{20,28},{24,56},{28,4},{32,64... | collective-permute-start | bytes 1572872 | tf_op jit(solution)/shard_map/ppermute | solution.py:52
  92.5 15.8 %collective-permute-start.35 = (f32[2,64,1024]{2,1,0:T(8,128)S(1)}, f32[2,64,1024]{2,1,0:T(8,128)S(1)}, u32[]{:S(2)}, u32[]{:S(2)}) collective-permute-start(f32[2,64,1024]{2,1,0:T(8,128)S(1)} %pad_maximum_fusion.9), channel_id=1, source_target_pairs={{0,16},{4,68},{8,24},{12,76},{16,0},{20,84},{24,8},{28,92},{32,48}... | collective-permute-start | bytes 1572872 | tf_op jit(solution)/shard_map/ppermute | solution.py:52
  118.4 16.1 %collective-permute-start.20 = (f32[2,4,16,2048]{3,2,1,0:T(8,128)S(1)}, f32[2,4,16,2048]{3,2,1,0:T(8,128)S(1)}, u32[]{:S(2)}, u32[]{:S(2)}) collective-permute-start(f32[2,4,16,2048]{3,2,1,0:T(8,128)S(1)} %pad_maximum_fusion.6), channel_id=1, source_target_pairs={{0,96},{4,28},{8,104},{12,4},{16,112},{20,12},{24,120},{28,20},{32... | collective-permute-start | bytes 3145736 | tf_op jit(solution)/shard_map/ppermute | solution.py:52
  122.2 16.1 %collective-permute-start.21 = (f32[2,4,16,2048]{3,2,1,0:T(8,128)S(1)}, f32[2,4,16,2048]{3,2,1,0:T(8,128)S(1)}, u32[]{:S(2)}, u32[]{:S(2)}) collective-permute-start(f32[2,4,16,2048]{3,2,1,0:T(8,128)S(1)} %pad_maximum_fusion.7), channel_id=1, source_target_pairs={{0,32},{4,12},{8,40},{12,20},{16,48},{20,28},{24,56},{28,4},{32,64... | collective-permute-start | bytes 3145736 | tf_op jit(solution)/shard_map/ppermute | solution.py:52
  123.9 30.2 %collective-permute-start.39 = (f32[128,1024]{1,0:T(8,128)S(1)}, f32[128,1024]{1,0:T(8,128)S(1)}, u32[]{:S(2)}, u32[]{:S(2)}) collective-permute-start(f32[128,1024]{1,0:T(8,128)S(1)} %pad_maximum_fusion.11.refs_0_.refs_8_), channel_id=1, source_target_pairs={{0,1},{1,2},{2,3},{3,0},{4,5},{5,6},{6,7},{7,4},{8,9},{9,10},{10,1... | collective-permute-start | bytes 1572872 | tf_op jit(solution)/shard_map/ppermute | solution.py:307
  125.5 29.8 %collective-permute-start.38 = (f32[128,1024]{1,0:T(8,128)S(1)}, f32[128,1024]{1,0:T(8,128)S(1)}, u32[]{:S(2)}, u32[]{:S(2)}) collective-permute-start(f32[128,1024]{1,0:T(8,128)S(1)} %pad_maximum_fusion.11.refs_0_.refs_8_), channel_id=1, source_target_pairs={{0,2},{1,3},{2,0},{3,1},{4,6},{5,7},{6,4},{7,5},{8,10},{9,11},{10,... | collective-permute-start | bytes 1572872 | tf_op jit(solution)/shard_map/ppermute | solution.py:307
  130.0 28.0 %collective-permute-start.37 = (f32[128,1024]{1,0:T(8,128)S(1)}, f32[128,1024]{1,0:T(8,128)S(1)}, u32[]{:S(2)}, u32[]{:S(2)}) collective-permute-start(f32[128,1024]{1,0:T(8,128)S(1)} %pad_maximum_fusion.11.refs_0_.refs_8_), channel_id=1, source_target_pairs={{0,3},{1,0},{2,1},{3,2},{4,7},{5,4},{6,5},{7,6},{8,11},{9,8},{10,9... | collective-permute-start | bytes 1572872 | tf_op jit(solution)/shard_map/ppermute | solution.py:307
  147.7 13.1 %collective-permute-start.16 = (f32[32,2048]{1,0:T(8,128)S(1)}, f32[32,2048]{1,0:T(8,128)S(1)}, u32[]{:S(2)}, u32[]{:S(2)}) collective-permute-start(f32[32,2048]{1,0:T(8,128)S(1)} %pad_maximum_fusion.14.refs_0_), channel_id=1, source_target_pairs={{0,1},{1,2},{2,3},{3,0},{4,5},{5,6},{6,7},{7,4},{8,9},{9,10},{10,1... | collective-permute-start | bytes 786440 | tf_op jit(solution)/shard_map/ppermute | solution.py:290
  149.2 11.7 %collective-permute-start.15 = (f32[32,2048]{1,0:T(8,128)S(1)}, f32[32,2048]{1,0:T(8,128)S(1)}, u32[]{:S(2)}, u32[]{:S(2)}) collective-permute-start(f32[32,2048]{1,0:T(8,128)S(1)} %pad_maximum_fusion.14.refs_0_), channel_id=1, source_target_pairs={{0,3},{1,0},{2,1},{3,2},{4,7},{5,4},{6,5},{7,6},{8,11},{9,8},{10,9... | collective-permute-start | bytes 786440 | tf_op jit(solution)/shard_map/ppermute | solution.py:290
  167.2 12.2 %collective-permute-start.29 = (f32[32,2048]{1,0:T(8,128)S(1)}, f32[32,2048]{1,0:T(8,128)S(1)}, u32[]{:S(2)}, u32[]{:S(2)}) collective-permute-start(f32[32,2048]{1,0:T(8,128)S(1)} %pad_maximum_fusion.18.refs_0_.refs_4_), channel_id=1, source_target_pairs={{0,1},{1,2},{2,3},{3,0},{4,5},{5,6},{6,7},{7,4},{8,9},{9,10},{10,1... | collective-permute-start | bytes 786440 | tf_op jit(solution)/shard_map/ppermute | solution.py:307
  167.3 12.1 %collective-permute-start.28 = (f32[32,2048]{1,0:T(8,128)S(1)}, f32[32,2048]{1,0:T(8,128)S(1)}, u32[]{:S(2)}, u32[]{:S(2)}) collective-permute-start(f32[32,2048]{1,0:T(8,128)S(1)} %pad_maximum_fusion.18.refs_0_.refs_4_), channel_id=1, source_target_pairs={{0,2},{1,3},{2,0},{3,1},{4,6},{5,7},{6,4},{7,5},{8,10},{9,11},{10,... | collective-permute-start | bytes 786440 | tf_op jit(solution)/shard_map/ppermute | solution.py:307
  (36 other events, 309.0 us)
